TPU v7x, 32 devices: a whole 2x2x4 slice. The times are simulated.
32 devices in a mesh: ctx: 8 (over z, core), tp: 4 (over y, x).
Axes of the slice: x: 2, y: 2, z: 4, core: 2. Of those that a mesh axis runs over, the one named last changes fastest.
Arguments:
- inner_x: bfloat16 [2, 1024, 16384], P(None, 'ctx', 'tp'), may hold values from -6 to 6
- gate_z: bfloat16 [2, 1024, 16384], P(None, 'ctx', 'tp'), may hold values from -6 to 6
- proj_bc: bfloat16 [2, 1024, 8, 512], P(None, 'ctx', 'tp'), may hold values from -6 to 6
- dt_raw: float32 [2, 256, 1024], P(None, 'tp', 'ctx'), may hold values from -6 to 41
- a_log: float32 [256], P('tp'), may hold values from -10 to 1
- dt_bias: float32 [256], P('tp'), may hold values from -0.5 to 0.5
- d_skip: float32 [256], P('tp'), may hold values from 0.5 to 1.5
- conv_x: float32 [4, 16384], P(None, 'tp'), may hold values from -3 to 3
- conv_bc: float32 [4, 8, 512], P(None, 'tp'), may hold values from -3 to 3
- bias_x: float32 [16384], P('tp'), may hold values from -0.5 to 0.5
- bias_bc: float32 [8, 512], P('tp'), may hold values from -0.5 to 0.5
- norm_gain: float32 [16384], P('tp'), may hold values from 0.25 to 1.75
- init_state: float32 [2, 256, 64, 256], P(None, 'tp'), may hold values from -6 to 6
- init_conv_x: bfloat16 [2, 3, 16384], P(None, None, 'tp'), may hold values from -6 to 6
- init_conv_bc: bfloat16 [2, 3, 8, 512], P(None, None, 'tp'), may hold values from -6 to 6
- lengths: int32 [2], replicated, may hold values from 512 to 1024, as said below
- dec_x: bfloat16 [4, 64, 16384], P(None, 'ctx', 'tp'), may hold values from -6 to 6
- dec_z: bfloat16 [4, 64, 16384], P(None, 'ctx', 'tp'), may hold values from -6 to 6
- dec_bc: bfloat16 [4, 64, 8, 512], P(None, 'ctx', 'tp'), may hold values from -6 to 6
- dec_dt: float32 [4, 256, 64], P(None, 'tp', 'ctx'), may hold values from -2.5 to 1
- row_prompt: int32 [64], P('ctx'), may hold values from 0 to 1
- w_out: bfloat16 [16384, 8192], P('tp', 'ctx'), may hold values from -0.046875 to 0.046875
Outputs:
- prefill_out: bfloat16 [2, 1024, 16384], P(None, 'ctx', 'tp')
- layer_out: bfloat16 [4, 64, 8192], P(None, 'tp', 'ctx')
Inputs may be any that keep to these rules, and one draw needn't show every extreme that they name: Positions from lengths[s] on are padding of prompt s. At least one prompt has all 1024 positions live.
All inputs are finite; a program needn't handle non-finite values.
Results may differ from a plain program's by a relative error of at most 0.005.
Values may be sent and summed in bfloat16 or wider, within the bound.
No kernel may reach another device: no remote copies, remote signals or barrier semaphores. Data moves between devices by JAX's collectives and lax.ppermute only.
A program may use at most 256 MiB of HBM per device.

v0:
```python
import functools

import jax
import jax.numpy as jnp
from jax import lax
from jax.experimental import pallas as pl
from jax.experimental.pallas import tpu as pltpu
from jax.sharding import PartitionSpec as P

epsilon = 1e-05
highest = lax.Precision.HIGHEST
f32, bf16 = jnp.float32, jnp.bfloat16
lanes = 128
vmem = 40 * 1024 * 1024


def silu(v):
    return v * (1.0 / (1.0 + jnp.exp(-v)))


def softplus(v):
    return jnp.maximum(v, 0.0) + jnp.log1p(jnp.exp(-jnp.abs(v)))


def exact(a, b):
    return jnp.dot(a, b, precision=highest, preferred_element_type=f32)


def exact_t(a, b):
    return lax.dot_general(
        a, b, (((1,), (1,)), ((), ())), precision=highest, preferred_element_type=f32
    )


def one_pass(a, b):
    return jnp.dot(a, b, preferred_element_type=f32)


def halves(a):
    high = a.astype(bf16)
    return high, (a - high.astype(f32)).astype(bf16)


def to_channels(columns, hd, first):
    row = lax.broadcasted_iota(jnp.int32, (lanes, columns), 0)
    col = lax.broadcasted_iota(jnp.int32, (lanes, columns), 1)
    return (row == col // hd + first).astype(f32)


def joined(refs, c):
    if len(refs) == 1:
        return refs[0][0]
    a, b = refs[0][0], refs[1][0]
    return jnp.concatenate([jnp.where(c == 0, a, b), jnp.where(c == 0, b, a)], axis=0)


def convolved(scratch, rim, body, taps_ref, bias_ref):
    rows = body.shape[0]
    taps = taps_ref.shape[0]
    scratch[0:8] = rim
    scratch[8 : 8 + rows] = body
    total = bias_ref[...]
    for k in range(taps):
        start = 8 - (taps - 1) + k
        total = total + taps_ref[k : k + 1] * scratch[start : start + rows]
    return silu(total)


def front_kernel(per, hd, sc, *refs):
    x_refs, refs = refs[:per], refs[per:]
    bc_refs, refs = refs[:per], refs[per:]
    (rim_x, rim_bc, dt, col, cx, cbc, bx, bbc, start) = refs[:9]
    (act_o, bc_o, run_o, step_o, pack_o, own_o, dec_o, start_o) = refs[9:17]
    xs, bs, bt = refs[17:]
    s, half = pl.program_id(0), pl.program_id(1)
    c, u = sc[0], sc[1]
    heads, rows = dt.shape[1:]
    n = bt.shape[0]
    bw = act_o.shape[2]

    @pl.when(half == 0)
    def _():
        at = u * rows + lax.broadcasted_iota(jnp.int32, (heads, rows), 1)
        live = jnp.where(at < sc[2 + s], 1.0, 0.0)
        step = softplus(dt[0] + col[:, 1:2]) * live
        i = lax.broadcasted_iota(jnp.int32, (rows, rows), 0)
        j = lax.broadcasted_iota(jnp.int32, (rows, rows), 1)
        run = exact(-col[:, 0:1] * step, (i <= j).astype(f32))
        to_end = jnp.exp(run[:, rows - 1 :] - run) * step
        run_o[0] = run
        step_o[0] = step
        pack_o[0] = jnp.transpose(jnp.concatenate([to_end, jnp.exp(run), run, step], axis=0))
        bc = convolved(bs, rim_bc[0], joined(bc_refs, c).astype(f32), cbc, bbc)
        bc_o[0] = bc
        bt[...] = jnp.transpose(bc[:, :n])

    act = convolved(xs, rim_x[0], joined(x_refs, c).astype(f32), cx, bx)
    act_o[0] = act
    first = half * (bw // hd)
    weighted = act * exact(pack_o[0], to_channels(bw, hd, first))
    own = exact(bt[...], weighted)
    decay = exact(pack_o[0, rows - 8 :, :], to_channels(bw, hd, first + heads))[7:8]
    dec_o[0] = jnp.broadcast_to(decay, (8, bw))

    @pl.when(u == 0)
    def _():
        begin = jnp.transpose(start[0])
        own_o[0] = own + decay * begin
        start_o[0] = begin.astype(bf16)

    @pl.when(u != 0)
    def _():
        own_o[0] = own
        start_o[0] = jnp.zeros(start_o.shape[1:], bf16)


def local_kernel(hd, act, bc, run, step, pack, skip, y_o, scores):
    half = pl.program_id(1)
    heads, rows = run.shape[1:]
    bw = act.shape[2]
    n = bc.shape[2] // 2

    @pl.when(half == 0)
    def _():
        scores[...] = exact_t(bc[0, :, n:], bc[0, :, :n])

    i = lax.broadcasted_iota(jnp.int32, (rows, rows), 0)
    j = lax.broadcasted_iota(jnp.int32, (rows, rows), 1)
    lower = i >= j
    lane = lax.broadcasted_iota(jnp.int32, (rows, lanes), 1)
    each = lanes // hd
    first = half * (bw // hd)

    def block(q, carry):
        at = pl.ds(pl.multiple_of(q * lanes, lanes), lanes)
        x = act[0, :, at]
        x_hi, x_lo = halves(x)
        y = skip[:, at] * x
        for e in range(each):
            h = first + q * each + e
            column = jnp.sum(jnp.where(lane == h + 2 * heads, pack[0], 0.0), axis=1, keepdims=True)
            gap = column - run[0, pl.ds(h, 1), :]
            mixing = jnp.exp(jnp.where(lower, gap, -1e30)) * (scores[...] * step[0, pl.ds(h, 1), :])
            m_hi, m_lo = halves(mixing)
            got = one_pass(m_hi, x_hi) + (one_pass(m_lo, x_hi) + one_pass(m_hi, x_lo))
            y = y + jnp.where(lane // hd == e, got, 0.0)
        y_o[0, :, at] = y
        return carry

    lax.fori_loop(0, bw // lanes, block, 0)


def back_kernel(per, hd, heads, sc, *refs):
    g_refs, refs = refs[:per], refs[per:]
    entry, bc, pack, local, gain, out_o, mixed = refs
    token_block = pl.program_id(0)
    c = sc[0]
    parts, n, bw = entry.shape
    gate = g_refs[0][0]
    if per == 2:
        gate = jnp.where(token_block == c, gate, g_refs[1][0])
    c_hi, c_lo = halves(bc[0, :, n:])
    total = None
    for k in range(parts):
        at = slice(k * bw, (k + 1) * bw)
        seen = one_pass(c_hi, entry[k]) + one_pass(c_lo, entry[k])
        grow = exact(pack[0], to_channels(bw, hd, heads + k * (bw // hd)))
        y = local[0, :, at] + grow * seen
        v = y * silu(gate[:, at].astype(f32))
        mixed[:, at] = v
        square = jnp.sum(v * v, axis=1, keepdims=True)
        total = square if total is None else total + square
    scale = lax.rsqrt(total / (parts * bw) + epsilon)
    out_o[0] = (mixed[...] * scale * gain[...]).astype(bf16)


def window_kernel(hd, full, factor, taps_ref, bias_ref, skip, local_o, c_o):
    taps = taps_ref.shape[0]
    steps, rows, gwidth = local_o.shape
    n = c_o.shape[2]
    acts = []
    for i in range(steps):
        total = bias_ref[...]
        for k in range(taps):
            total = total + taps_ref[k : k + 1] * full[i + k]
        acts.append(silu(total))
    coef = []
    for i in range(steps):
        read = acts[i][:, gwidth + n :]
        c_o[i] = read
        for j in range(i + 1):
            both = jnp.sum(read * acts[j][:, gwidth : gwidth + n], axis=1, keepdims=True)
            coef.append(both * factor[len(coef)])
    wide = exact(jnp.concatenate(coef, axis=0), to_channels(gwidth, hd, 0))
    at = 0
    for i in range(steps):
        y = skip[...] * acts[i][:, :gwidth]
        for j in range(i + 1):
            y = y + wide[at * rows : (at + 1) * rows] * acts[j][:, :gwidth]
            at += 1
        local_o[i] = y


def read_kernel(hd, asked, own, after, out_o):
    half = pl.program_id(0)
    prompts, _, n, bw = own.shape
    spread = exact(jnp.exp(after[...]), to_channels(bw, hd, half * (bw // hd)))
    rows = asked[:, :n]
    prompt = asked[:, n : n + 1]
    total = None
    for s in range(prompts):
        c_hi, c_lo = halves(jnp.where(prompt == s, rows, 0.0))
        s_hi, s_lo = halves(own[s, 0] * spread[s : s + 1])
        got = one_pass(c_hi, s_hi) + (one_pass(c_lo, s_hi) + one_pass(c_hi, s_lo))
        total = got if total is None else total + got
    out_o[...] = total.astype(bf16)


def finish_kernel(hd, *refs):
    *sums, local, grow, gate, gain, out_o = refs
    total = sums[0][...].astype(f32)
    for r in sums[1:]:
        total = total + r[...].astype(f32)
    gwidth = out_o.shape[1]
    y = exact(grow[...], to_channels(gwidth, hd, 0)) * total + local[...]
    v = y * silu(gate[...])
    scale = lax.rsqrt(jnp.mean(v * v, axis=1, keepdims=True) + epsilon)
    out_o[...] = (v * scale * gain[...]).astype(bf16)


def params():
    return pltpu.CompilerParams(vmem_limit_bytes=vmem)


def shards(
    inner_x,
    gate_z,
    proj_bc,
    dt_raw,
    a_log,
    dt_bias,
    d_skip,
    conv_x,
    conv_bc,
    bias_x,
    bias_bc,
    norm_gain,
    init_state,
    init_conv_x,
    init_conv_bc,
    lengths,
    dec_x,
    dec_z,
    dec_bc,
    dec_dt,
    row_prompt,
    w_out,
):
    prompts, tokens, width = inner_x.shape
    groups, pair = proj_bc.shape[2:]
    ns = pair // 2
    heads = dt_raw.shape[1] // groups
    gwidth = width // groups
    hd = gwidth // heads
    taps = conv_x.shape[0]
    steps, batch = dec_x.shape[:2]
    cols = w_out.shape[1]
    n = lax.axis_size("ctx")
    tp = lax.axis_size("tp")
    assert groups in (1, 2) and n % groups == 0 and 4 * heads == lanes
    per = groups
    m = n // per
    device = lax.axis_index("ctx")
    u, c = device // per, device % per
    unit_tokens = per * tokens
    rows_u = per * batch
    per_prompt = 2
    bw = gwidth // per_prompt
    parts = prompts * per_prompt

    def mine(arr, axis):
        return lax.dynamic_index_in_dim(arr, c, axis, keepdims=False)

    def swap(arr):
        return lax.ppermute(arr, "ctx", [(i, i ^ 1) for i in range(n)])

    def in_order(own, other, axis):
        first = jnp.where(c == 0, own, other)
        second = jnp.where(c == 0, other, own)
        return jnp.concatenate([first, second], axis=axis)

    def other_group(arr, size):
        if per == 1:
            return None
        at = [0] * (arr.ndim - 1) + [(1 - c) * size]
        return swap(lax.dynamic_slice(arr, at, arr.shape[:-1] + (size,)))

    def pair_up(arr, gaxis, taxis):
        if per == 1:
            return jnp.squeeze(arr, gaxis)
        other = swap(lax.dynamic_index_in_dim(arr, 1 - c, gaxis, keepdims=False))
        return in_order(mine(arr, gaxis), other, taxis)

    def shift(arr, k):
        return lax.ppermute(arr, "ctx", [(i, (i + k * per) % n) for i in range(n)])

    bc_flat = proj_bc.reshape(prompts, tokens, groups * pair)
    x_other = other_group(inner_x, gwidth)
    bc_other = other_group(bc_flat, pair)
    last_x = inner_x[:, tokens - taps + 1 :]
    last_bc = bc_flat[:, tokens - taps + 1 :]
    wide = gwidth + pair
    rim = jnp.zeros((prompts, taps - 1, wide), bf16)
    for g in range(per):
        pairs = [(v * per + per - 1, (v + 1) * per + g) for v in range(m - 1)]
        send = jnp.concatenate(
            [last_x[..., g * gwidth : (g + 1) * gwidth], last_bc[..., g * pair : (g + 1) * pair]],
            axis=-1,
        )
        got = lax.ppermute(send, "ctx", pairs)
        rim = jnp.where(c == g, got, rim)
    places = device * tokens + jnp.arange(tokens, dtype=jnp.int32)
    target = lengths[:, None] - (taps - 1) + jnp.arange(taps - 1, dtype=jnp.int32)[None, :]
    picker = (places[None, None, :] == target[:, :, None]).astype(bf16)
    tails = jnp.concatenate(
        [
            jnp.einsum("sjt,stc->sjc", picker, inner_x, preferred_element_type=f32),
            jnp.einsum("sjt,stc->sjc", picker, bc_flat, preferred_element_type=f32),
        ],
        axis=-1,
    )
    tails = lax.psum(tails, "ctx")
    dt = pair_up(dt_raw.reshape(prompts, groups, heads, tokens), 1, 2)
    z_other = other_group(gate_z, gwidth)
    dec_bc_flat = dec_bc.reshape(steps, batch, groups * pair)
    dec_flat = jnp.concatenate(
        [
            jnp.concatenate(
                [dec_x[..., g * gwidth : (g + 1) * gwidth], dec_bc_flat[..., g * pair : (g + 1) * pair],
                 dec_z[..., g * gwidth : (g + 1) * gwidth]],
                axis=-1,
            )[:, :, None]
            for g in range(groups)
        ],
        axis=2,
    )
    dec_all = pair_up(dec_flat, 2, 1).astype(f32)
    dec_raw, dec_gate = dec_all[..., :wide], dec_all[..., wide:]
    dec_step = pair_up(dec_dt.reshape(steps, groups, heads, batch), 1, 2)
    prompt_of = row_prompt if per == 1 else in_order(row_prompt, swap(row_prompt), 0)

    rate = jnp.exp(mine(a_log.reshape(groups, heads), 0))
    dtb = mine(dt_bias.reshape(groups, heads), 0)
    skip = jnp.repeat(mine(d_skip.reshape(groups, heads), 0), hd)[None]
    gain = mine(norm_gain.reshape(groups, 1, gwidth), 0)
    col = jnp.pad(jnp.stack([rate, dtb], axis=1), ((0, 0), (0, lanes - 2)))
    cbc = conv_bc.reshape(taps, groups * pair)
    bbc = bias_bc.reshape(1, groups * pair)
    bx = bias_x.reshape(1, width)
    start_rim = jnp.concatenate(
        [
            mine(init_conv_x.reshape(prompts, taps - 1, groups, gwidth), 2),
            mine(init_conv_bc, 2),
        ],
        axis=-1,
    )
    rim = jnp.where(u == 0, start_rim, rim).astype(f32)
    rim = jnp.pad(rim, ((0, 0), (8 - (taps - 1), 0), (0, 0)))
    start = init_state.reshape(prompts, groups * gwidth, ns)
    sc = jnp.concatenate([jnp.stack([c, u]).astype(jnp.int32), lengths])

    x_in = [inner_x] + ([x_other] if per == 2 else [])
    bc_in = [bc_flat] + ([bc_other] if per == 2 else [])
    T = unit_tokens
    spec = pl.BlockSpec
    in_specs = [spec((1, tokens, bw), lambda s, k, sc: (s, 0, sc[0] * per_prompt + k))]
    in_specs += [spec((1, tokens, bw), lambda s, k, sc: (s, 0, k))] * (per - 1)
    in_specs += [spec((1, tokens, pair), lambda s, k, sc: (s, 0, sc[0]))]
    in_specs += [spec((1, tokens, pair), lambda s, k, sc: (s, 0, 0))] * (per - 1)
    in_specs += [
        spec((1, 8, bw), lambda s, k, sc: (s, 0, k)),
        spec((1, 8, pair), lambda s, k, sc: (s, 0, 0)),
        spec((1, heads, T), lambda s, k, sc: (s, 0, 0)),
        spec((heads, lanes), lambda s, k, sc: (0, 0)),
        spec((taps, bw), lambda s, k, sc: (0, sc[0] * per_prompt + k)),
        spec((taps, pair), lambda s, k, sc: (0, sc[0])),
        spec((1, bw), lambda s, k, sc: (0, sc[0] * per_prompt + k)),
        spec((1, pair), lambda s, k, sc: (0, sc[0])),
        spec((1, bw, ns), lambda s, k, sc: (s, sc[0] * per_prompt + k, 0)),
    ]
    chunk = lambda s, k, sc: (s * per_prompt + k, 0, 0)
    whole = lambda s, k, sc: (s, 0, 0)
    act, bc, run, step, pack, own, decay, begin = pl.pallas_call(
        functools.partial(front_kernel, per, hd),
        grid_spec=pltpu.PrefetchScalarGridSpec(
            num_scalar_prefetch=1,
            grid=(prompts, per_prompt),
            in_specs=in_specs,
            out_specs=[
                spec((1, T, bw), lambda s, k, sc: (s, 0, k)),
                spec((1, T, pair), whole),
                spec((1, heads, T), whole),
                spec((1, heads, T), whole),
                spec((1, T, lanes), whole),
                spec((1, ns, bw), chunk),
                spec((1, 8, bw), chunk),
                spec((1, ns, bw), chunk),
            ],
            scratch_shapes=[
                pltpu.VMEM((T + 8, bw), f32),
                pltpu.VMEM((T + 8, pair), f32),
                pltpu.VMEM((ns, T), f32),
            ],
        ),
        out_shape=[
            jax.ShapeDtypeStruct((prompts, T, gwidth), f32),
            jax.ShapeDtypeStruct((prompts, T, pair), f32),
            jax.ShapeDtypeStruct((prompts, heads, T), f32),
            jax.ShapeDtypeStruct((prompts, heads, T), f32),
            jax.ShapeDtypeStruct((prompts, T, lanes), f32),
            jax.ShapeDtypeStruct((parts, ns, bw), f32),
            jax.ShapeDtypeStruct((parts, 8, bw), f32),
            jax.ShapeDtypeStruct((parts, ns, bw), bf16),
        ],
        compiler_params=params(),
        name="front",
    )(sc, *x_in, *bc_in, rim[..., :gwidth], rim[..., gwidth:], dt, col, conv_x, cbc, bx, bbc, start)

    arrived = []
    carry = jnp.zeros(own.shape[1:], bf16)
    along = [(i, i + per) for i in range(n - per)]
    for t in range(parts + m - 2):
        at_k = jnp.clip(t - u, 0, parts - 1)
        own_t = lax.dynamic_index_in_dim(own, at_k, 0, keepdims=False)
        decay_t = lax.dynamic_index_in_dim(decay, at_k, 0, keepdims=False)[:1]
        leave = (decay_t * carry.astype(f32) + own_t).astype(bf16)
        carry = lax.ppermute(leave, "ctx", along)
        arrived.append(carry)

    y_local = pl.pallas_call(
        functools.partial(local_kernel, hd),
        grid=(prompts, per_prompt),
        in_specs=[
            spec((1, T, bw), lambda s, k: (s, 0, k)),
            spec((1, T, pair), lambda s, k: (s, 0, 0)),
            spec((1, heads, T), lambda s, k: (s, 0, 0)),
            spec((1, heads, T), lambda s, k: (s, 0, 0)),
            spec((1, T, lanes), lambda s, k: (s, 0, 0)),
            spec((1, bw), lambda s, k: (0, k)),
        ],
        out_specs=spec((1, T, bw), lambda s, k: (s, 0, k)),
        out_shape=jax.ShapeDtypeStruct((prompts, T, gwidth), f32),
        scratch_shapes=[pltpu.VMEM((T, T), f32)],
        compiler_params=params(),
        cost_estimate=pl.CostEstimate(
            flops=60_000 * T * T, bytes_accessed=16 * T * gwidth, transcendentals=0
        ),
        name="local",
    )(act, bc, run, step, pack, skip)

    tails_g = jnp.concatenate(
        [
            lax.dynamic_slice_in_dim(tails, c * gwidth, gwidth, 2),
            lax.dynamic_slice_in_dim(tails, width + c * pair, pair, 2),
        ],
        axis=-1,
    )
    window = tails_g[0][:, None]
    for s in range(1, prompts):
        window = jnp.where(prompt_of[None, :, None] == s, tails_g[s][:, None], window)
    window = jnp.broadcast_to(window, (taps - 1, rows_u, wide))
    full = jnp.concatenate([window, dec_raw], axis=0)
    tap_w = jnp.concatenate(
        [mine(conv_x.reshape(taps, groups, gwidth), 1), mine(conv_bc, 1)], axis=-1
    )
    tap_b = jnp.concatenate([mine(bias_x.reshape(groups, gwidth), 0), mine(bias_bc, 0)])[None]
    stepd = jax.nn.softplus(jnp.transpose(dec_step, (0, 2, 1)) + dtb)
    logd = -rate * stepd
    upto = [logd[0]]
    for i in range(1, steps):
        upto.append(upto[-1] + logd[i])
    factor = jnp.stack(
        [jnp.exp(upto[i] - upto[j]) * stepd[j] for i in range(steps) for j in range(i + 1)]
    )
    factor = jnp.pad(factor, ((0, 0), (0, 0), (0, lanes - heads)))
    grow = jnp.pad(
        jnp.exp(jnp.stack(upto)).reshape(steps * rows_u, heads), ((0, 0), (0, lanes - heads))
    )
    local, cd = pl.pallas_call(
        functools.partial(window_kernel, hd),
        out_shape=[
            jax.ShapeDtypeStruct((steps, rows_u, gwidth), f32),
            jax.ShapeDtypeStruct((steps, rows_u, ns), f32),
        ],
        compiler_params=params(),
        name="window",
    )(full, factor, tap_w, tap_b, skip)

    span = run[:, :, T - 1]
    asked_rows = steps * rows_u
    payload = jnp.concatenate(
        [
            jnp.concatenate(
                [
                    cd.reshape(asked_rows, ns),
                    jnp.broadcast_to(
                        jnp.tile(prompt_of.astype(f32), steps)[:, None], (asked_rows, lanes)
                    ),
                ],
                axis=1,
            ),
            jnp.pad(span, ((0, 8 - prompts), (0, ns + lanes - heads))),
        ],
        axis=0,
    )
    blocks = [payload] + [shift(payload, k) for k in range(1, m)]
    after = jnp.zeros((8, lanes), f32)
    for k in range(1, m):
        span_k = blocks[k][asked_rows:, :lanes]
        after = after + jnp.where((u - k) % m > u, span_k, 0.0)
    asked = jnp.concatenate([b[:asked_rows] for b in blocks], axis=0)
    read = pl.pallas_call(
        functools.partial(read_kernel, hd),
        grid=(per_prompt,),
        in_specs=[
            spec((m * asked_rows, ns + lanes), lambda k: (0, 0)),
            spec((prompts, 1, ns, bw), lambda k: (0, k, 0, 0)),
            spec((8, lanes), lambda k: (0, 0)),
        ],
        out_specs=spec((m * asked_rows, bw), lambda k: (0, k)),
        out_shape=jax.ShapeDtypeStruct((m * asked_rows, gwidth), bf16),
        compiler_params=params(),
        name="read",
    )(asked, own.reshape(prompts, per_prompt, ns, bw), after)
    sums = [read[:asked_rows]]
    for k in range(1, m):
        sums.append(shift(read[k * asked_rows : (k + 1) * asked_rows], -k))
    hidden = pl.pallas_call(
        functools.partial(finish_kernel, hd),
        out_shape=jax.ShapeDtypeStruct((asked_rows, gwidth), bf16),
        compiler_params=params(),
        name="finish",
    )(*sums, local.reshape(asked_rows, gwidth), grow, dec_gate.reshape(asked_rows, gwidth), gain)
    hidden = hidden.reshape(steps, rows_u, gwidth)
    got = jnp.stack([hidden] + [shift(hidden, k) for k in range(1, m)])
    got = jnp.concatenate([got[::-1], got[::-1]])
    got = lax.dynamic_slice_in_dim(got, m - 1 - u, m, 0)
    if per == 2:
        got = in_order(got, swap(got), 3)
    product = jnp.dot(
        jnp.swapaxes(got, 0, 1).reshape(-1, width), w_out, preferred_element_type=f32
    )
    terms = lax.all_to_all(product.reshape(steps, tp, -1, cols), "tp", 1, 1)
    layer_out = jnp.sum(terms, axis=1).astype(bf16)

    outs = []
    for s in range(prompts):
        entry = []
        for k in range(s * per_prompt, (s + 1) * per_prompt):
            e = begin[k]
            for v in range(1, m):
                e = jnp.where(u == v, arrived[k + v - 1], e)
            entry.append(e)
        z_in = [gate_z] + ([z_other] if per == 2 else [])
        z_specs = [spec((1, tokens, gwidth), lambda j, sc, s=s: (s, 0, sc[0]))]
        z_specs += [spec((1, tokens, gwidth), lambda j, sc, s=s: (s, 0, 0))] * (per - 1)
        out = pl.pallas_call(
            functools.partial(back_kernel, per, hd, heads),
            grid_spec=pltpu.PrefetchScalarGridSpec(
                num_scalar_prefetch=1,
                grid=(per,),
                in_specs=z_specs
                + [
                    spec((per_prompt, ns, bw), lambda j, sc: (0, 0, 0)),
                    spec((1, tokens, pair), lambda j, sc, s=s: (s, j, 0)),
                    spec((1, tokens, lanes), lambda j, sc, s=s: (s, j, 0)),
                    spec((1, tokens, gwidth), lambda j, sc, s=s: (s, j, 0)),
                    spec((1, gwidth), lambda j, sc: (0, 0)),
                ],
                out_specs=spec(
                    (1, tokens, gwidth), lambda j, sc: (jnp.where(j == sc[0], 0, 1), 0, 0)
                ),
                scratch_shapes=[pltpu.VMEM((tokens, gwidth), f32)],
            ),
            out_shape=jax.ShapeDtypeStruct((per, tokens, gwidth), bf16),
            compiler_params=params(),
            name="back",
        )(sc, *z_in, jnp.stack(entry), bc, pack, y_local, gain)
        outs.append(out[0] if per == 1 else in_order(out[0], swap(out[1]), 1))
    return (jnp.stack(outs), layer_out)


def solution(mesh):
    in_specs = (
        P(None, "ctx", "tp"),
        P(None, "ctx", "tp"),
        P(None, "ctx", "tp", None),
        P(None, "tp", "ctx"),
        P("tp"),
        P("tp"),
        P("tp"),
        P(None, "tp"),
        P(None, "tp", None),
        P("tp"),
        P("tp", None),
        P("tp"),
        P(None, "tp", None, None),
        P(None, None, "tp"),
        P(None, None, "tp", None),
        P(),
        P(None, "ctx", "tp"),
        P(None, "ctx", "tp"),
        P(None, "ctx", "tp", None),
        P(None, "tp", "ctx"),
        P("ctx"),
        P("tp", "ctx"),
    )
    out_specs = (P(None, "ctx", "tp"), P(None, "tp", "ctx"))
    return jax.shard_map(shards, mesh=mesh, in_specs=in_specs, out_specs=out_specs, check_vma=False)
```

profile of v0, /device:TPU:0, one launch (start us, length us, event | category | flops | bytes accessed | tf_op | source)
XLA Modules:
  0.0 278.6 jit_solution(10481275608511540300)
XLA Ops:
  7.3 0.8 reshape.179
  9.2 1.0 fusion.51
  10.2 1.0 fusion.52
  11.2 1.0 reshape.178
  12.2 0.9 maximum_bitcast_fusion.3
  13.1 1.8 fusion.23
  16.2 0.7 pad_maximum_fusion.6
  17.4 1.0 constant_dynamic-slice_fusion.20
  20.8 0.7 constant_dynamic-slice_fusion.19
  26.2 4.6 %collective-permute-start.2 = (bf16[2,128,512]{2,1,0:T(8,128)(2,1)}, bf16[2,128,512]{2,1,0:T(8,128)(2,1)S(1)}, u32[]{:S(2)}, u32[]{:S(2)}) collective-permute-start(bf16[2,128,512]{2,1,0:T(8,128)(2,1)} %constant_dynamic-slice_fusion.19), channel_id=1, source_target_pairs={{0,4},{4,0},{8,12},{12,8},{16,20},{20,16},{24,28},{28,24},{1,5},{5... | collective-permute-start | bytes 786440 | tf_op jit(solution)/shard_map/ppermute | solution.py:285
  32.5 0.7 collective-permute-done.5
  33.2 0.8 bitcast_select_fusion.5
  34.0 37.9 %all-reduce.7.cloned.1.call-done = f32[2,3,5120]{2,1,0:T(4,128)} async-done(((f32[2,3,5120]{2,1,0:T(4,128)}), f32[2,3,5120]{2,1,0:T(4,128)}) %all-reduce.7.cloned.1.call-update) | async-done | bytes 122896 | tf_op jit(solution)/shard_map/psum | solution.py:332
  71.9 0.9 constant_dynamic-slice_fusion.6
  72.7 0.7 constant_dynamic-slice_fusion.5
  73.6 1.4 broadcast_select_fusion.7
  75.2 1.3 window.1
  76.5 0.7 copy-done.11
  77.2 0.9 copy-done.12
  78.2 18.1 %front.1 = (f32[2,256,2048]{2,1,0:T(8,128)S(1)}, f32[2,256,512]{2,1,0:T(8,128)S(1)}, f32[2,32,256]{2,1,0:T(8,128)S(1)}, f32[2,32,256]{2,1,0:T(8,128)S(1)}, f32[2...) custom-call(s32[4]{0:T(128)S(1)} %pad_add_fusion.sc, ...), custom_call_target="tpu_custom_call" | custom-call | tf_op jit(solution)/shard_map/front/pallas_call | solution.py:393
  96.3 2.0 copy-done.20
  98.6 2.4 collective-permute-start.17
  101.0 1.4 collective-permute-start.18
  102.4 2.3 collective-permute-start.19
  104.8 1.3 fusion.9
  106.1 1.6 collective-permute-start.6
  107.8 2.5 collective-permute-done.18
  110.3 2.2 copy-done.2
  112.5 3.2 %read.1 = bf16[256,2048]{1,0:T(8,128)(2,1)S(1)} custom-call(f32[256,384]{1,0:T(8,128)S(1)} %pad_maximum_fusion.5.asked, f32[2,2,256,1024]{3,2,1,0:T(8,128)S(1)} %bitcast.193, f32[8,128]{1,0:T(8,128)S(1)} %fusion.36.after), custom_call_target="tpu_custom_call" | custom-call | tf_op jit(solution)/shard_map/read/pallas_call | solution.py:522
  115.9 5.1 %collective-permute-start.20 = (bf16[64,2048]{1,0:T(8,128)(2,1)S(1)}, bf16[64,2048]{1,0:T(8,128)(2,1)S(1)}, u32[]{:S(2)}, u32[]{:S(2)}) collective-permute-start(bf16[64,2048]{1,0:T(8,128)(2,1)S(1)} %get-tuple-element.44), channel_id=1, source_target_pairs={{0,24},{4,28},{8,0},{12,4},{16,8},{20,12},{24,16},{28,20},{1,25},{... | collective-permute-start | bytes 786440 | tf_op jit(solution)/shard_map/ppermute | solution.py:305
  121.7 6.0 %collective-permute-done.20.refs_1_ = bf16[64,2048]{1,0:T(8,128)(2,1)S(1)} collective-permute-done((bf16[64,2048]{1,0:T(8,128)(2,1)S(1)}, bf16[64,2048]{1,0:T(8,128)(2,1)S(1)}, u32[]{:S(2)}, u32[]{:S(2)}) %collective-permute-start.20) | collective-permute-done | bytes 262176 | tf_op jit(solution)/shard_map/ppermute | solution.py:305
  127.7 15.0 %collective-permute-done.21.refs_2_ = bf16[64,2048]{1,0:T(8,128)(2,1)S(1)} collective-permute-done((bf16[64,2048]{1,0:T(8,128)(2,1)S(1)}, bf16[64,2048]{1,0:T(8,128)(2,1)S(1)}, u32[]{:S(2)}, u32[]{:S(2)}) %collective-permute-start.21) | collective-permute-done | bytes 262176 | tf_op jit(solution)/shard_map/ppermute | solution.py:305
  143.4 2.0 collective-permute-start.23
  145.5 2.0 collective-permute-start.24
  147.5 2.8 %collective-permute-start.25 = (bf16[4,16,2048]{2,1,0:T(8,128)(2,1)S(1)}, bf16[4,16,2048]{2,1,0:T(8,128)(2,1)S(1)}, u32[]{:S(2)}, u32[]{:S(2)}) collective-permute-start(bf16[4,16,2048]{2,1,0:T(8,128)(2,1)S(1)} %bitcast.197), channel_id=1, source_target_pairs={{0,24},{4,28},{8,0},{12,4},{16,8},{20,12},{24,16},{28,20},{1,25},{... | collective-permute-start | bytes 786440 | tf_op jit(solution)/shard_map/ppermute | solution.py:305
  150.3 1.6 fusion.8
  151.9 1.3 collective-permute-start.7
  153.2 1.4 collective-permute-done.23
  154.6 9.0 %collective-permute-done.24 = bf16[4,16,2048]{2,1,0:T(8,128)(2,1)S(1)} collective-permute-done((bf16[4,16,2048]{2,1,0:T(8,128)(2,1)S(1)}, bf16[4,16,2048]{2,1,0:T(8,128)(2,1)S(1)}, u32[]{:S(2)}, u32[]{:S(2)}) %collective-permute-start.24) | collective-permute-done | bytes 262176 | tf_op jit(solution)/shard_map/ppermute | solution.py:305
  164.4 1.2 pad_maximum_fusion.4
  166.2 6.4 %collective-permute-done.7 = bf16[256,1024]{1,0:T(8,128)(2,1)S(1)} collective-permute-done((bf16[256,1024]{1,0:T(8,128)(2,1)S(1)}, bf16[256,1024]{1,0:T(8,128)(2,1)S(1)}, u32[]{:S(2)}, u32[]{:S(2)}) %collective-permute-start.7) | collective-permute-done | bytes 524320 | tf_op jit(solution)/shard_map/ppermute | solution.py:437
  172.6 1.6 fusion.7
  174.2 10.0 %collective-permute-start.8 = (bf16[256,1024]{1,0:T(8,128)(2,1)S(1)}, bf16[256,1024]{1,0:T(8,128)(2,1)S(1)}, u32[]{:S(2)}, u32[]{:S(2)}) collective-permute-start(bf16[256,1024]{1,0:T(8,128)(2,1)S(1)} %fusion.7), channel_id=1, source_target_pairs={{0,8},{4,12},{8,16},{12,20},{16,24},{20,28},{1,9},{5,13},{9,17},{1... | collective-permute-start | bytes 1572872 | tf_op jit(solution)/shard_map/ppermute | solution.py:437
  184.2 9.2 %collective-permute-done.8 = bf16[256,1024]{1,0:T(8,128)(2,1)S(1)} collective-permute-done((bf16[256,1024]{1,0:T(8,128)(2,1)S(1)}, bf16[256,1024]{1,0:T(8,128)(2,1)S(1)}, u32[]{:S(2)}, u32[]{:S(2)}) %collective-permute-start.8) | collective-permute-done | bytes 524320 | tf_op jit(solution)/shard_map/ppermute | solution.py:437
  193.6 4.4 %collective-permute-start.9 = (bf16[256,1024]{1,0:T(8,128)(2,1)S(1)}, bf16[256,1024]{1,0:T(8,128)(2,1)S(1)}, u32[]{:S(2)}, u32[]{:S(2)}) collective-permute-start(bf16[256,1024]{1,0:T(8,128)(2,1)S(1)} %fusion.6), channel_id=1, source_target_pairs={{0,8},{4,12},{8,16},{12,20},{16,24},{20,28},{1,9},{5,13},{9,17},{1... | collective-permute-start | bytes 1572872 | tf_op jit(solution)/shard_map/ppermute | solution.py:437
  198.6 7.8 %collective-permute-done.9 = bf16[256,1024]{1,0:T(8,128)(2,1)S(1)} collective-permute-done((bf16[256,1024]{1,0:T(8,128)(2,1)S(1)}, bf16[256,1024]{1,0:T(8,128)(2,1)S(1)}, u32[]{:S(2)}, u32[]{:S(2)}) %collective-permute-start.9) | collective-permute-done | bytes 524320 | tf_op jit(solution)/shard_map/ppermute | solution.py:437
  206.6 4.4 %collective-permute-start.11 = (bf16[256,1024]{1,0:T(8,128)(2,1)S(1)}, bf16[256,1024]{1,0:T(8,128)(2,1)S(1)}, u32[]{:S(2)}, u32[]{:S(2)}) collective-permute-start(bf16[256,1024]{1,0:T(8,128)(2,1)S(1)} %fusion.5), channel_id=1, source_target_pairs={{0,8},{4,12},{8,16},{12,20},{16,24},{20,28},{1,9},{5,13},{9,17},{1... | collective-permute-start | bytes 1572872 | tf_op jit(solution)/shard_map/ppermute | solution.py:437
  211.0 6.8 %fusion = f32[4,4,16,1024]{3,2,0,1:T(8,128)} fusion(bf16[4096,1024]{1,0:T(8,128)(2,1)} %param.43, bf16[4,4,16,2048]{3,2,0,1:T(8,128)(2,1)S(1)} %get-tuple-element.35, bf16[4,4,16,2048]{3,2,0,1:T(8,128)(2,1)S(1)} %get-tuple-element.34), kind=kOutput, calls=%fused_computation | convolution fusion | flops 2151677952 | bytes 11534336 | tf_op jit(solution)/shard_map/dot_general | solution.py:550
  217.8 4.4 %all-to-all-start = ((f32[4,4,16,1024]{3,2,0,1:T(8,128)}), f32[4,4,16,1024]{3,2,0,1:T(8,128)}, u32[]{:S(2)}, u32[]{:S(2)}) async-start(f32[4,4,16,1024]{3,2,0,1:T(8,128)} %fusion), calls=%async_computation | async-start | bytes 2097152 | tf_op jit(solution)/shard_map/all_to_all | solution.py:553
  222.2 0.8 copy-done.28
  223.0 2.4 fusion.4
  225.4 5.2 %collective-permute-start.12 = (bf16[256,1024]{1,0:T(8,128)(2,1)}, bf16[256,1024]{1,0:T(8,128)(2,1)}, u32[]{:S(2)}, u32[]{:S(2)}) collective-permute-start(bf16[256,1024]{1,0:T(8,128)(2,1)} %fusion.4), channel_id=1, source_target_pairs={{0,8},{4,12},{8,16},{12,20},{16,24},{20,28},{1,9},{5,13},{9,17},{1... | collective-permute-start | bytes 1572872 | tf_op jit(solution)/shard_map/ppermute | solution.py:437
  230.6 1.0 constant_dynamic-slice_fusion.21
  231.6 2.2 copy-done.21
  233.8 0.8 copy-done.23
  234.7 15.9 %local.1.refs_5_ = f32[2,256,2048]{2,1,0:T(8,128)S(1)} custom-call(f32[2,256,2048]{2,1,0:T(8,128)S(1)} %copy-done.21, f32[2,256,512]{2,1,0:T(8,128)S(1)} %copy-done.9, f32[2,32,256]{2,1,0:T(8,128)S(1)} %copy-done.19, f32[2,32,256]{2,1,0:T(8,128)S(1)} %copy-done.23, f32[2,256,128]{2,1,0:T(8,128)S(1)} %get-tuple-element.16.pack.refs_4_, ...), custom_call_target="tpu_custom_call" | custom-call | flops 3932160000 | bytes 8388608 | tf_op jit(solution)/shard_map/local/pallas_call | solution.py:440
  250.6 2.0 copy-done.4
  252.6 2.0 reduce_sum.9
  254.6 2.6 fusion.21
  257.2 0.8 copy-done.5
  258.0 4.7 %back.2 = bf16[2,128,2048]{2,1,0:T(8,128)(2,1)S(1)} custom-call(s32[4]{0:T(128)S(1)} %pad_add_fusion.sc, bf16[2,128,4096]{2,1,0:T(8,128)(2,1)S(1)} %copy-done.7, bf16[2,128,2048]{2,1,0:T(8,128)(2,1)} %collective-permute-done.refs_1_, bf16[2,256,1024]{2,1,0:T(8,128)(2,1)S(1)} %pad_maximum_fusion.2.refs_2_, f32[2,256,512]{2,1,0:T(8,128)S(1)} %copy-done.9, ...), custom_call_target="tpu_custom_call" | custom-call | tf_op jit(solution)/shard_map/back/pallas_call | solution.py:567
  263.4 4.7 %back.3 = bf16[2,128,2048]{2,1,0:T(8,128)(2,1)S(1)} custom-call(s32[4]{0:T(128)S(1)} %pad_add_fusion.sc, bf16[2,128,4096]{2,1,0:T(8,128)(2,1)S(1)} %copy-done.7, bf16[2,128,2048]{2,1,0:T(8,128)(2,1)} %collective-permute-done.refs_1_, bf16[2,256,1024]{2,1,0:T(8,128)(2,1)S(1)} %pad_maximum_fusion.3.refs_2_, f32[2,256,512]{2,1,0:T(8,128)S(1)} %copy-done.9, ...), custom_call_target="tpu_custom_call" | custom-call | tf_op jit(solution)/shard_map/back/pallas_call | solution.py:567
  268.4 1.7 collective-permute-done.13
  270.3 1.5 pad_maximum_fusion
  (223 shorter events, 16.7 us)
Async XLA Ops:
  7.2 16.3 %copy-start = (f32[4096]{0:T(1024)S(1)}, f32[4096]{0:T(1024)}, u32[]{:S(2)}) copy-start(f32[4096]{0:T(1024)} %param.33) | copy-start | bytes 49156
  7.2 7.8 %copy-start.29 = (bf16[2,128,2,512]{3,2,1,0:T(2,128)(2,1)S(1)}, bf16[2,128,2,512]{3,2,1,0:T(2,128)(2,1)}, u32[]{:S(2)}) copy-start(bf16[2,128,2,512]{3,2,1,0:T(2,128)(2,1)} %param.24) | copy-start | bytes 1572868
  7.2 64.7 %all-reduce.7.cloned.1.call-start = ((), (), s32[]{:S(2)}) async-start(), calls=%async_computation.1 | async-start | bytes 327680 | tf_op jit(solution)/shard_map/psum | solution.py:332
  8.8 6.6 %copy-start.46 = (s32[2]{0:T(128)S(1)}, s32[2]{0:T(128)}, u32[]{:S(2)}) copy-start(s32[2]{0:T(128)} %param.37) | copy-start | bytes 28
  8.8 17.5 %collective-permute-start.16 = (f32[4,32,8]{1,2,0:T(8,128)}, f32[4,32,8]{1,2,0:T(8,128)S(1)}, u32[]{:S(2)}, u32[]{:S(2)}) collective-permute-start(f32[4,32,8]{1,2,0:T(8,128)} %bitcast.48), channel_id=1, source_target_pairs={{0,4},{4,0},{8,12},{12,8},{16,20},{20,16},{24,28},{28,24},{1,5},{5... | collective-permute-start | bytes 12296 | tf_op jit(solution)/shard_map/ppermute | solution.py:285
  11.2 4.5 %copy-start.6 = (bf16[2,128,4096]{2,1,0:T(8,128)(2,1)S(1)}, bf16[2,128,4096]{2,1,0:T(8,128)(2,1)}, u32[]{:S(2)}) copy-start(bf16[2,128,4096]{2,1,0:T(8,128)(2,1)} %refs_0_.3) | copy-start | bytes 6291460
  14.9 58.7 %collective-permute-start.15 = (bf16[4,8,4608]{2,1,0:T(8,128)(2,1)}, bf16[4,8,4608]{2,1,0:T(8,128)(2,1)}, u32[]{:S(2)}, u32[]{:S(2)}) collective-permute-start(bf16[4,8,4608]{2,1,0:T(8,128)(2,1)} %fusion.23), channel_id=1, source_target_pairs={{0,4},{4,0},{8,12},{12,8},{16,20},{20,16},{24,28},{28,24},{1,5},{5... | collective-permute-start | bytes 884744 | tf_op jit(solution)/shard_map/ppermute | solution.py:285
  15.7 4.3 %copy-start.48 = (f32[64]{0:T(128)S(1)}, f32[64]{0:T(128)}, u32[]{:S(2)}) copy-start(f32[64]{0:T(128)} %param.26) | copy-start | bytes 772
  15.7 4.4 %copy-start.49 = (f32[64]{0:T(128)S(1)}, f32[64]{0:T(128)}, u32[]{:S(2)}) copy-start(f32[64]{0:T(128)} %param.27) | copy-start | bytes 772
  15.7 4.5 %copy-start.13 = (f32[4,4096]{1,0:T(4,128)S(1)}, f32[4,4096]{1,0:T(4,128)}, u32[]{:S(2)}) copy-start(f32[4,4096]{1,0:T(4,128)} %refs_8_.1) | copy-start | bytes 196612
  15.7 4.5 %copy-start.40 = (f32[4,2,512]{2,1,0:T(2,128)S(1)}, f32[4,2,512]{2,1,0:T(2,128)}, u32[]{:S(2)}) copy-start(f32[4,2,512]{2,1,0:T(2,128)} %param.30) | copy-start | bytes 49156
  15.7 4.5 %copy-start.14 = (f32[4096]{0:T(1024)S(1)}, f32[4096]{0:T(1024)}, u32[]{:S(2)}) copy-start(f32[4096]{0:T(1024)} %param.31) | copy-start | bytes 49156
  16.1 4.1 %copy-start.43 = (f32[2,512]{1,0:T(2,128)S(1)}, f32[2,512]{1,0:T(2,128)}, u32[]{:S(2)}) copy-start(f32[2,512]{1,0:T(2,128)} %param.32) | copy-start | bytes 12292
  16.2 4.1 %copy-start.50 = (f32[64]{0:T(128)S(1)}, f32[64]{0:T(128)}, u32[]{:S(2)}) copy-start(f32[64]{0:T(128)} %param.28) | copy-start | bytes 772
  16.2 4.4 %copy-start.38 = (bf16[2,3,4096]{2,0,1:T(2,128)(2,1)S(1)}, bf16[2,3,4096]{2,0,1:T(2,128)(2,1)}, u32[]{:S(2)}) copy-start(bf16[2,3,4096]{2,0,1:T(2,128)(2,1)} %param.35) | copy-start | bytes 147460
  16.2 4.6 %copy-start.42 = (bf16[2,3,2,512]{3,2,1,0:T(2,128)(2,1)S(1)}, bf16[2,3,2,512]{3,2,1,0:T(2,128)(2,1)}, u32[]{:S(2)}) copy-start(bf16[2,3,2,512]{3,2,1,0:T(2,128)(2,1)} %param.36) | copy-start | bytes 36868
  16.2 5.4 %copy-start.37 = (f32[2,64,128]{2,1,0:T(8,128)S(1)}, f32[2,64,128]{2,1,0:T(8,128)}, u32[]{:S(2)}) copy-start(f32[2,64,128]{2,1,0:T(8,128)} %param.25) | copy-start | bytes 196612
  16.9 7.8 %copy-start.47 = (s32[2]{0:T(128)S(1)}, s32[2]{0:T(128)}, u32[]{:S(2)}) copy-start(s32[2]{0:T(128)} %param.37) | copy-start | bytes 28
  16.9 7.9 %collective-permute-start.14 = (s32[8]{0:T(128)S(1)}, s32[8]{0:T(128)S(1)}, u32[]{:S(2)}, u32[]{:S(2)}) collective-permute-start(s32[8]{0:T(128)S(1)} %copy-done.45), channel_id=1, source_target_pairs={{0,4},{4,0},{8,12},{12,8},{16,20},{20,16},{24,28},{28,24},{1,5},{5... | collective-permute-start | bytes 104 | tf_op jit(solution)/shard_map/ppermute | solution.py:285
  18.5 58.7 %collective-permute-start.1 = (bf16[2,128,2048]{2,1,0:T(8,128)(2,1)}, bf16[2,128,2048]{2,1,0:T(8,128)(2,1)}, u32[]{:S(2)}, u32[]{:S(2)}) collective-permute-start(bf16[2,128,2048]{2,1,0:T(8,128)(2,1)} %constant_dynamic-slice_fusion.20), channel_id=1, source_target_pairs={{0,4},{4,0},{8,12},{12,8},{16,20},{20,16},{24,28},{28,24},{1,5},{5... | collective-permute-start | bytes 3145736 | tf_op jit(solution)/shard_map/ppermute | solution.py:285
  19.2 12.5 %collective-permute-start.3 = (bf16[2,3,2560]{2,1,0:T(4,128)(2,1)}, bf16[2,3,2560]{2,1,0:T(4,128)(2,1)S(1)}, u32[]{:S(2)}, u32[]{:S(2)}) collective-permute-start(bf16[2,3,2560]{2,1,0:T(4,128)(2,1)} %pad_maximum_fusion.9), channel_id=1, source_target_pairs={{4,12},{12,20},{20,28},{5,13},{13,21},{21,29},{6,14},{14,22},{22,3... | collective-permute-start | bytes 92168 | tf_op jit(solution)/shard_map/ppermute | solution.py:320
  24.8 7.0 %collective-permute-start.4 = (bf16[2,3,2560]{2,1,0:T(4,128)(2,1)}, bf16[2,3,2560]{2,1,0:T(4,128)(2,1)S(1)}, u32[]{:S(2)}, u32[]{:S(2)}) collective-permute-start(bf16[2,3,2560]{2,1,0:T(4,128)(2,1)} %pad_maximum_fusion.10), channel_id=1, source_target_pairs={{4,8},{12,16},{20,24},{5,9},{13,17},{21,25},{6,10},{14,18},{22,26}... | collective-permute-start | bytes 92168 | tf_op jit(solution)/shard_map/ppermute | solution.py:320
  26.2 50.2 %collective-permute-start.2 = (bf16[2,128,512]{2,1,0:T(8,128)(2,1)}, bf16[2,128,512]{2,1,0:T(8,128)(2,1)S(1)}, u32[]{:S(2)}, u32[]{:S(2)}) collective-permute-start(bf16[2,128,512]{2,1,0:T(8,128)(2,1)} %constant_dynamic-slice_fusion.19), channel_id=1, source_target_pairs={{0,4},{4,0},{8,12},{12,8},{16,20},{20,16},{24,28},{28,24},{1,5},{5... | collective-permute-start | bytes 786440 | tf_op jit(solution)/shard_map/ppermute | solution.py:285
  31.7 1.5 collective-permute-start.5
  78.2 20.3 %copy-start.44 = (f32[64]{0:T(128)S(1)}, f32[64]{0:T(128)}, u32[]{:S(2)}) copy-start(f32[64]{0:T(128)} %broadcast_in_dim.77) | copy-start | bytes 772
  98.3 12.0 %copy-start.10 = (bf16[4,256,1024]{2,1,0:T(8,128)(2,1)}, bf16[4,256,1024]{2,1,0:T(8,128)(2,1)S(1)}, u32[]{:S(2)}) copy-start(bf16[4,256,1024]{2,1,0:T(8,128)(2,1)S(1)} %get-tuple-element.14) | copy-start | bytes 6291460
  98.3 17.4 %copy-start.8 = (f32[2,256,512]{2,1,0:T(8,128)}, f32[2,256,512]{2,1,0:T(8,128)S(1)}, u32[]{:S(2)}) copy-start(f32[2,256,512]{2,1,0:T(8,128)S(1)} %get-tuple-element.15.bc.refs_3_) | copy-start | bytes 3145732
  98.3 17.4 %copy-start.18 = (f32[2,32,256]{2,1,0:T(8,128)}, f32[2,32,256]{2,1,0:T(8,128)S(1)}, u32[]{:S(2)}) copy-start(f32[2,32,256]{2,1,0:T(8,128)S(1)} %get-tuple-element.18.run) | copy-start | bytes 196612
  98.3 17.4 %copy-start.22 = (f32[2,32,256]{2,1,0:T(8,128)}, f32[2,32,256]{2,1,0:T(8,128)S(1)}, u32[]{:S(2)}) copy-start(f32[2,32,256]{2,1,0:T(8,128)S(1)} %get-tuple-element.19.step) | copy-start | bytes 196612
  98.6 9.2 %collective-permute-start.17 = (f32[72,384]{1,0:T(8,128)S(1)}, f32[72,384]{1,0:T(8,128)S(1)}, u32[]{:S(2)}, u32[]{:S(2)}) collective-permute-start(f32[72,384]{1,0:T(8,128)S(1)} %select_maximum_fusion), channel_id=1, source_target_pairs={{0,8},{4,12},{8,16},{12,20},{16,24},{20,28},{24,0},{28,4},{1,9},{5... | collective-permute-start | bytes 331784 | tf_op jit(solution)/shard_map/ppermute | solution.py:305
  101.0 9.3 %collective-permute-start.18 = (f32[72,384]{1,0:T(8,128)S(1)}, f32[72,384]{1,0:T(8,128)S(1)}, u32[]{:S(2)}, u32[]{:S(2)}) collective-permute-start(f32[72,384]{1,0:T(8,128)S(1)} %select_maximum_fusion), channel_id=1, source_target_pairs={{0,16},{4,20},{8,24},{12,28},{16,0},{20,4},{24,8},{28,12},{1,17},{... | collective-permute-start | bytes 331784 | tf_op jit(solution)/shard_map/ppermute | solution.py:305
  102.4 7.8 %collective-permute-start.19 = (f32[72,384]{1,0:T(8,128)S(1)}, f32[72,384]{1,0:T(8,128)S(1)}, u32[]{:S(2)}, u32[]{:S(2)}) collective-permute-start(f32[72,384]{1,0:T(8,128)S(1)} %select_maximum_fusion), channel_id=1, source_target_pairs={{0,24},{4,28},{8,0},{12,4},{16,8},{20,12},{24,16},{28,20},{1,25},{... | collective-permute-start | bytes 331784 | tf_op jit(solution)/shard_map/ppermute | solution.py:305
  106.1 44.2 %collective-permute-start.6 = (bf16[256,1024]{1,0:T(8,128)(2,1)S(1)}, bf16[256,1024]{1,0:T(8,128)(2,1)S(1)}, u32[]{:S(2)}, u32[]{:S(2)}) collective-permute-start(bf16[256,1024]{1,0:T(8,128)(2,1)S(1)} %fusion.9), channel_id=1, source_target_pairs={{0,8},{4,12},{8,16},{12,20},{16,24},{20,28},{1,9},{5,13},{9,17},{1... | collective-permute-start | bytes 1572872 | tf_op jit(solution)/shard_map/ppermute | solution.py:437
  110.3 2.2 copy-start.2
  115.7 5.9 %copy-start.31 = (f32[1,16,32]{2,1,0:T(8,128)S(1)}, f32[1,16,32]{2,1,0:T(8,128)}, u32[]{:S(2)}) copy-start(f32[1,16,32]{2,1,0:T(8,128)} %copy-done.30) | copy-start | bytes 6148
  115.8 5.9 %copy-start.36 = (f32[1,16,32]{2,1,0:T(8,128)S(1)}, f32[1,16,32]{2,1,0:T(8,128)}, u32[]{:S(2)}) copy-start(f32[1,16,32]{2,1,0:T(8,128)} %copy-done.35) | copy-start | bytes 6148
  115.8 5.9 %copy-start.41 = (f32[1,16,32]{2,1,0:T(8,128)S(1)}, f32[1,16,32]{2,1,0:T(8,128)}, u32[]{:S(2)}) copy-start(f32[1,16,32]{2,1,0:T(8,128)} %get-tuple-element.66) | copy-start | bytes 6148
  115.9 11.9 %collective-permute-start.20 = (bf16[64,2048]{1,0:T(8,128)(2,1)S(1)}, bf16[64,2048]{1,0:T(8,128)(2,1)S(1)}, u32[]{:S(2)}, u32[]{:S(2)}) collective-permute-start(bf16[64,2048]{1,0:T(8,128)(2,1)S(1)} %get-tuple-element.44), channel_id=1, source_target_pairs={{0,24},{4,28},{8,0},{12,4},{16,8},{20,12},{24,16},{28,20},{1,25},{... | collective-permute-start | bytes 786440 | tf_op jit(solution)/shard_map/ppermute | solution.py:305
  121.0 21.8 %collective-permute-start.21 = (bf16[64,2048]{1,0:T(8,128)(2,1)S(1)}, bf16[64,2048]{1,0:T(8,128)(2,1)S(1)}, u32[]{:S(2)}, u32[]{:S(2)}) collective-permute-start(bf16[64,2048]{1,0:T(8,128)(2,1)S(1)} %get-tuple-element.43), channel_id=1, source_target_pairs={{0,16},{4,20},{8,24},{12,28},{16,0},{20,4},{24,8},{28,12},{1,17},{... | collective-permute-start | bytes 786440 | tf_op jit(solution)/shard_map/ppermute | solution.py:305
  121.0 21.8 %collective-permute-start.22 = (bf16[64,2048]{1,0:T(8,128)(2,1)S(1)}, bf16[64,2048]{1,0:T(8,128)(2,1)S(1)}, u32[]{:S(2)}, u32[]{:S(2)}) collective-permute-start(bf16[64,2048]{1,0:T(8,128)(2,1)S(1)} %get-tuple-element.42), channel_id=1, source_target_pairs={{0,8},{4,12},{8,16},{12,20},{16,24},{20,28},{24,0},{28,4},{1,9},{5... | collective-permute-start | bytes 786440 | tf_op jit(solution)/shard_map/ppermute | solution.py:305
  143.4 11.2 %collective-permute-start.23 = (bf16[4,16,2048]{2,1,0:T(8,128)(2,1)S(1)}, bf16[4,16,2048]{2,1,0:T(8,128)(2,1)S(1)}, u32[]{:S(2)}, u32[]{:S(2)}) collective-permute-start(bf16[4,16,2048]{2,1,0:T(8,128)(2,1)S(1)} %bitcast.195), channel_id=1, source_target_pairs={{0,8},{4,12},{8,16},{12,20},{16,24},{20,28},{24,0},{28,4},{1,9},{5... | collective-permute-start | bytes 786440 | tf_op jit(solution)/shard_map/ppermute | solution.py:305
  145.5 18.1 %collective-permute-start.24 = (bf16[4,16,2048]{2,1,0:T(8,128)(2,1)S(1)}, bf16[4,16,2048]{2,1,0:T(8,128)(2,1)S(1)}, u32[]{:S(2)}, u32[]{:S(2)}) collective-permute-start(bf16[4,16,2048]{2,1,0:T(8,128)(2,1)S(1)} %bitcast.196), channel_id=1, source_target_pairs={{0,16},{4,20},{8,24},{12,28},{16,0},{20,4},{24,8},{28,12},{1,17},{... | collective-permute-start | bytes 786440 | tf_op jit(solution)/shard_map/ppermute | solution.py:305
  147.5 16.1 %collective-permute-start.25 = (bf16[4,16,2048]{2,1,0:T(8,128)(2,1)S(1)}, bf16[4,16,2048]{2,1,0:T(8,128)(2,1)S(1)}, u32[]{:S(2)}, u32[]{:S(2)}) collective-permute-start(bf16[4,16,2048]{2,1,0:T(8,128)(2,1)S(1)} %bitcast.197), channel_id=1, source_target_pairs={{0,24},{4,28},{8,0},{12,4},{16,8},{20,12},{24,16},{28,20},{1,25},{... | collective-permute-start | bytes 786440 | tf_op jit(solution)/shard_map/ppermute | solution.py:305
  150.3 14.0 %copy-start.24 = (bf16[256,1024]{1,0:T(8,128)(2,1)}, bf16[256,1024]{1,0:T(8,128)(2,1)S(1)}, u32[]{:S(2)}) copy-start(bf16[256,1024]{1,0:T(8,128)(2,1)S(1)} %collective-permute-done.6) | copy-start | bytes 1572868
  151.9 20.7 %collective-permute-start.7 = (bf16[256,1024]{1,0:T(8,128)(2,1)S(1)}, bf16[256,1024]{1,0:T(8,128)(2,1)S(1)}, u32[]{:S(2)}, u32[]{:S(2)}) collective-permute-start(bf16[256,1024]{1,0:T(8,128)(2,1)S(1)} %fusion.8), channel_id=1, source_target_pairs={{0,8},{4,12},{8,16},{12,20},{16,24},{20,28},{1,9},{5,13},{9,17},{1... | collective-permute-start | bytes 1572872 | tf_op jit(solution)/shard_map/ppermute | solution.py:437
  154.6 9.0 %copy-start.32 = (bf16[4,16,2048]{2,1,0:T(8,128)(2,1)}, bf16[4,16,2048]{2,1,0:T(8,128)(2,1)S(1)}, u32[]{:S(2)}) copy-start(bf16[4,16,2048]{2,1,0:T(8,128)(2,1)S(1)} %collective-permute-done.23) | copy-start | bytes 786436
  165.7 27.7 %copy-start.3 = (f32[4,256,1024]{2,1,0:T(8,128)S(1)}, f32[4,256,1024]{2,1,0:T(8,128)}, u32[]{:S(2)}) copy-start(f32[4,256,1024]{2,1,0:T(8,128)} %get-tuple-element.13) | copy-start | bytes 12582916
  166.1 31.9 %collective-permute-start.26 = (bf16[4,4,16,2048]{3,2,0,1:T(8,128)(2,1)S(1)}, bf16[4,4,16,2048]{3,2,0,1:T(8,128)(2,1)S(1)}, u32[]{:S(2)}, u32[]{:S(2)}) collective-permute-start(bf16[4,4,16,2048]{3,2,0,1:T(8,128)(2,1)S(1)} %fusion.3), channel_id=1, source_target_pairs={{0,4},{4,0},{8,12},{12,8},{16,20},{20,16},{24,28},{28,24},{1,5},{5... | collective-permute-start | bytes 3145736 | tf_op jit(solution)/shard_map/ppermute | solution.py:285
  172.6 21.0 %copy-start.25 = (bf16[256,1024]{1,0:T(8,128)(2,1)}, bf16[256,1024]{1,0:T(8,128)(2,1)S(1)}, u32[]{:S(2)}) copy-start(bf16[256,1024]{1,0:T(8,128)(2,1)S(1)} %collective-permute-done.7) | copy-start | bytes 1572868
  174.2 19.3 %collective-permute-start.8 = (bf16[256,1024]{1,0:T(8,128)(2,1)S(1)}, bf16[256,1024]{1,0:T(8,128)(2,1)S(1)}, u32[]{:S(2)}, u32[]{:S(2)}) collective-permute-start(bf16[256,1024]{1,0:T(8,128)(2,1)S(1)} %fusion.7), channel_id=1, source_target_pairs={{0,8},{4,12},{8,16},{12,20},{16,24},{20,28},{1,9},{5,13},{9,17},{1... | collective-permute-start | bytes 1572872 | tf_op jit(solution)/shard_map/ppermute | solution.py:437
  193.4 5.1 %copy-start.26 = (bf16[256,1024]{1,0:T(8,128)(2,1)}, bf16[256,1024]{1,0:T(8,128)(2,1)S(1)}, u32[]{:S(2)}) copy-start(bf16[256,1024]{1,0:T(8,128)(2,1)S(1)} %collective-permute-done.8) | copy-start | bytes 1572868
  193.6 12.7 %collective-permute-start.9 = (bf16[256,1024]{1,0:T(8,128)(2,1)S(1)}, bf16[256,1024]{1,0:T(8,128)(2,1)S(1)}, u32[]{:S(2)}, u32[]{:S(2)}) collective-permute-start(bf16[256,1024]{1,0:T(8,128)(2,1)S(1)} %fusion.6), channel_id=1, source_target_pairs={{0,8},{4,12},{8,16},{12,20},{16,24},{20,28},{1,9},{5,13},{9,17},{1... | collective-permute-start | bytes 1572872 | tf_op jit(solution)/shard_map/ppermute | solution.py:437
  206.4 4.6 %copy-start.27 = (bf16[256,1024]{1,0:T(8,128)(2,1)}, bf16[256,1024]{1,0:T(8,128)(2,1)S(1)}, u32[]{:S(2)}) copy-start(bf16[256,1024]{1,0:T(8,128)(2,1)S(1)} %collective-permute-done.9) | copy-start | bytes 1572868
  206.6 15.6 %collective-permute-start.11 = (bf16[256,1024]{1,0:T(8,128)(2,1)S(1)}, bf16[256,1024]{1,0:T(8,128)(2,1)S(1)}, u32[]{:S(2)}, u32[]{:S(2)}) collective-permute-start(bf16[256,1024]{1,0:T(8,128)(2,1)S(1)} %fusion.5), channel_id=1, source_target_pairs={{0,8},{4,12},{8,16},{12,20},{16,24},{20,28},{1,9},{5,13},{9,17},{1... | collective-permute-start | bytes 1572872 | tf_op jit(solution)/shard_map/ppermute | solution.py:437
  217.8 12.8 %copy-start.7 = (bf16[2,128,4096]{2,1,0:T(8,128)(2,1)S(1)}, bf16[2,128,4096]{2,1,0:T(8,128)(2,1)}, u32[]{:S(2)}) copy-start(bf16[2,128,4096]{2,1,0:T(8,128)(2,1)} %refs_0_.5) | copy-start | bytes 6291460
  217.8 34.8 %all-to-all-start = ((f32[4,4,16,1024]{3,2,0,1:T(8,128)}), f32[4,4,16,1024]{3,2,0,1:T(8,128)}, u32[]{:S(2)}, u32[]{:S(2)}) async-start(f32[4,4,16,1024]{3,2,0,1:T(8,128)} %fusion), calls=%async_computation | async-start | bytes 2097152 | tf_op jit(solution)/shard_map/all_to_all | solution.py:553
  223.0 8.6 %copy-start.9 = (f32[2,256,512]{2,1,0:T(8,128)S(1)}, f32[2,256,512]{2,1,0:T(8,128)}, u32[]{:S(2)}) copy-start(f32[2,256,512]{2,1,0:T(8,128)} %copy-done.8) | copy-start | bytes 3145732
  223.0 8.6 %copy-start.19 = (f32[2,32,256]{2,1,0:T(8,128)S(1)}, f32[2,32,256]{2,1,0:T(8,128)}, u32[]{:S(2)}) copy-start(f32[2,32,256]{2,1,0:T(8,128)} %copy-done.18) | copy-start | bytes 196612
  225.4 29.2 %collective-permute-start.12 = (bf16[256,1024]{1,0:T(8,128)(2,1)}, bf16[256,1024]{1,0:T(8,128)(2,1)}, u32[]{:S(2)}, u32[]{:S(2)}) collective-permute-start(bf16[256,1024]{1,0:T(8,128)(2,1)} %fusion.4), channel_id=1, source_target_pairs={{0,8},{4,12},{8,16},{12,20},{16,24},{20,28},{1,9},{5,13},{9,17},{1... | collective-permute-start | bytes 1572872 | tf_op jit(solution)/shard_map/ppermute | solution.py:437
  231.6 25.6 %collective-permute-start = (bf16[2,128,2048]{2,1,0:T(8,128)(2,1)}, bf16[2,128,2048]{2,1,0:T(8,128)(2,1)}, u32[]{:S(2)}, u32[]{:S(2)}) collective-permute-start(bf16[2,128,2048]{2,1,0:T(8,128)(2,1)} %constant_dynamic-slice_fusion.21), channel_id=1, source_target_pairs={{0,4},{4,0},{8,12},{12,8},{16,20},{20,16},{24,28},{28,24},{1,5},{5... | collective-permute-start | bytes 3145736 | tf_op jit(solution)/shard_map/ppermute | solution.py:285
  231.6 2.2 copy-start.21
  254.6 3.4 %copy-start.5 = (f32[2,256,2048]{2,1,0:T(8,128)S(1)}, f32[2,256,2048]{2,1,0:T(8,128)}, u32[]{:S(2)}) copy-start(f32[2,256,2048]{2,1,0:T(8,128)} %copy-done.4) | copy-start | bytes 12582916
  262.7 5.5 %collective-permute-start.10 = (bf16[128,2048]{1,0:T(8,128)(2,1)S(1)}, bf16[128,2048]{1,0:T(8,128)(2,1)S(1)}, u32[]{:S(2)}, u32[]{:S(2)}) collective-permute-start(bf16[128,2048]{1,0:T(8,128)(2,1)S(1)} %slice_bitcast_fusion.2), channel_id=1, source_target_pairs={{0,4},{4,0},{8,12},{12,8},{16,20},{20,16},{24,28},{28,24},{1,5},{5... | collective-permute-start | bytes 1572872 | tf_op jit(solution)/shard_map/ppermute | solution.py:285
  268.1 2.0 collective-permute-start.13
  (16 other events, 21.3 us)
Sparse Core Ops, SparseCore 0:
  17.0 54.7 all-reduce.6
where the time goes:
time: 280 us; the launch traced here: 279 us
  waiting for transfers between devices  97.7 us (35%)
  starting transfers between devices  58.1 us (21%)
  Pallas kernels  48.4 us (17%)
  local copies, waits for them, and re-layouts  27.6 us (10%)
  other arithmetic  24.2 us (9%)
  between operations  15.2 us (5%)
  matrix products  7.43 us (3%)
    psum x1, waiting for transfers between devices, shards(): tails = lax.psum(tails, 'ctx')  37.9 us
    ppermute x9, waiting for transfers between devices, shift(): return lax.ppermute(arr, 'ctx', [(i, (i + k * per) % n) for i in range(n)])  33.9 us
    ppermute x6, starting transfers between devices, shards(): carry = lax.ppermute(leave, 'ctx', along)  27 us
    ppermute x6, waiting for transfers between devices, shards(): carry = lax.ppermute(leave, 'ctx', along)  23.4 us
    ppermute x9, starting transfers between devices, shift(): return lax.ppermute(arr, 'ctx', [(i, (i + k * per) % n) for i in range(n)])  18.8 us
    pallas_call x1, Pallas kernels, shards(): pl.pallas_call(functools.partial(front_kernel, per, hd), grid_spec=pltpu....  18.1 us
    pallas_call x1, Pallas kernels, shards(): pl.pallas_call(functools.partial(local_kernel, hd), grid=(prompts, per_pr...  15.9 us
    unnamed x106, local copies, waits for them, and re-layouts  15.2 us
  transfers between devices with their start and end apart: 29, of which 11 were waited for; matrix products, arithmetic and copies ran while one was open for 15% of the time, Pallas kernels for 9%

commit v1 on v0

v1 whole, which is shorter than its diff:
```python
import functools

import jax
import jax.numpy as jnp
from jax import lax
from jax.experimental import pallas as pl
from jax.experimental.pallas import tpu as pltpu
from jax.sharding import PartitionSpec as P

epsilon = 1e-05
highest = lax.Precision.HIGHEST
f32, bf16 = jnp.float32, jnp.bfloat16
lanes = 128
vmem = 40 * 1024 * 1024


def silu(v):
    return v * (1.0 / (1.0 + jnp.exp(-v)))


def softplus(v):
    return jnp.maximum(v, 0.0) + jnp.log1p(jnp.exp(-jnp.abs(v)))


def exact(a, b):
    return jnp.dot(a, b, precision=highest, preferred_element_type=f32)


def exact_t(a, b):
    return lax.dot_general(
        a, b, (((1,), (1,)), ((), ())), precision=highest, preferred_element_type=f32
    )


def one_pass(a, b):
    return jnp.dot(a, b, preferred_element_type=f32)


def halves(a):
    high = a.astype(bf16)
    return high, (a - high.astype(f32)).astype(bf16)


def to_channels(columns, hd, first):
    row = lax.broadcasted_iota(jnp.int32, (lanes, columns), 0)
    col = lax.broadcasted_iota(jnp.int32, (lanes, columns), 1)
    return (row == col // hd + first).astype(f32)


def joined(refs, c, axis=0):
    if len(refs) == 1:
        return refs[0][0]
    a, b = refs[0][0], refs[1][0]
    return jnp.concatenate([jnp.where(c == 0, a, b), jnp.where(c == 0, b, a)], axis=axis)


def convolved(scratch, rim, body, taps_ref, bias_ref):
    rows = body.shape[0]
    taps = taps_ref.shape[0]
    scratch[0:8] = rim
    scratch[8 : 8 + rows] = body
    total = bias_ref[...]
    for k in range(taps):
        start = 8 - (taps - 1) + k
        total = total + taps_ref[k : k + 1] * scratch[start : start + rows]
    return silu(total)


def front_kernel(per, hd, prompt, sc, *refs):
    x_refs, refs = refs[:per], refs[per:]
    bc_refs, refs = refs[:per], refs[per:]
    dt_refs, refs = refs[:per], refs[per:]
    (rim_x, rim_bc, col, cx, cbc, bx, bbc, start) = refs[:8]
    (act_o, bc_o, run_o, step_o, pack_o, own_o, dec_o, start_o) = refs[8:16]
    xs, bs, bt = refs[16:]
    half = pl.program_id(0)
    c, u = sc[0], sc[1]
    _, heads, rows = run_o.shape
    n = bt.shape[0]
    bw = act_o.shape[2]

    @pl.when(half == 0)
    def _():
        at = u * rows + lax.broadcasted_iota(jnp.int32, (heads, rows), 1)
        live = jnp.where(at < sc[2 + prompt], 1.0, 0.0)
        step = softplus(joined(dt_refs, c, 1) + col[:, 1:2]) * live
        i = lax.broadcasted_iota(jnp.int32, (rows, rows), 0)
        j = lax.broadcasted_iota(jnp.int32, (rows, rows), 1)
        run = exact(-col[:, 0:1] * step, (i <= j).astype(f32))
        to_end = jnp.exp(run[:, rows - 1 :] - run) * step
        run_o[0] = run
        step_o[0] = step
        pack_o[0] = jnp.transpose(jnp.concatenate([to_end, jnp.exp(run), run, step], axis=0))
        bc = convolved(bs, rim_bc[0], joined(bc_refs, c).astype(f32), cbc, bbc)
        bc_o[0] = bc
        bt[...] = jnp.transpose(bc[:, :n])

    act = convolved(xs, rim_x[0], joined(x_refs, c).astype(f32), cx, bx)
    act_o[0] = act
    first = half * (bw // hd)
    weighted = act * exact(pack_o[0], to_channels(bw, hd, first))
    own = exact(bt[...], weighted)
    decay = exact(pack_o[0, rows - 8 :, :], to_channels(bw, hd, first + heads))[7:8]
    dec_o[0] = jnp.broadcast_to(decay, (8, bw))

    @pl.when(u == 0)
    def _():
        begin = jnp.transpose(start[0])
        own_o[0] = own + decay * begin
        start_o[0] = begin.astype(bf16)

    @pl.when(u != 0)
    def _():
        own_o[0] = own
        start_o[0] = jnp.zeros(start_o.shape[1:], bf16)


def local_kernel(hd, at_part, act, bc, run, step, pack, skip, y_o, scores):
    half = pl.program_id(0) + at_part
    heads, rows = run.shape[1:]
    bw = act.shape[2]
    n = bc.shape[2] // 2

    scores[...] = exact_t(bc[0, :, n:], bc[0, :, :n])

    i = lax.broadcasted_iota(jnp.int32, (rows, rows), 0)
    j = lax.broadcasted_iota(jnp.int32, (rows, rows), 1)
    lower = i >= j
    lane = lax.broadcasted_iota(jnp.int32, (rows, lanes), 1)
    each = lanes // hd
    first = half * (bw // hd)

    def block(q, carry):
        at = pl.ds(pl.multiple_of(q * lanes, lanes), lanes)
        x = act[0, :, at]
        x_hi, x_lo = halves(x)
        y = skip[:, at] * x
        for e in range(each):
            h = first + q * each + e
            column = jnp.sum(jnp.where(lane == h + 2 * heads, pack[0], 0.0), axis=1, keepdims=True)
            gap = column - run[0, pl.ds(h, 1), :]
            mixing = jnp.exp(jnp.where(lower, gap, -1e30)) * (scores[...] * step[0, pl.ds(h, 1), :])
            m_hi, m_lo = halves(mixing)
            got = one_pass(m_hi, x_hi) + (one_pass(m_lo, x_hi) + one_pass(m_hi, x_lo))
            y = y + jnp.where(lane // hd == e, got, 0.0)
        y_o[0, :, at] = y
        return carry

    lax.fori_loop(0, bw // lanes, block, 0)


def back_kernel(per, hd, heads, sc, *refs):
    g_refs, refs = refs[:per], refs[per:]
    *rest, out_o, mixed = refs
    parts = (len(rest) - 3) // 2
    entry, (bc, pack, gain), local = rest[:parts], rest[parts : parts + 3], rest[parts + 3 :]
    token_block = pl.program_id(0)
    c = sc[0]
    _, n, bw = entry[0].shape
    gate = g_refs[0][0]
    if per == 2:
        gate = jnp.where(token_block == c, gate, g_refs[1][0])
    c_hi, c_lo = halves(bc[0, :, n:])
    total = None
    for k in range(parts):
        at = slice(k * bw, (k + 1) * bw)
        seen = one_pass(c_hi, entry[k][0]) + one_pass(c_lo, entry[k][0])
        grow = exact(pack[0], to_channels(bw, hd, heads + k * (bw // hd)))
        y = local[k][0] + grow * seen
        v = y * silu(gate[:, at].astype(f32))
        mixed[:, at] = v
        square = jnp.sum(v * v, axis=1, keepdims=True)
        total = square if total is None else total + square
    scale = lax.rsqrt(total / (parts * bw) + epsilon)
    out_o[0] = (mixed[...] * scale * gain[...]).astype(bf16)


def rows_of(refs, i, at, c):
    a = refs[0][i][:, at[0]].astype(f32)
    if len(refs) == 1:
        return a
    b = refs[1][i][:, at[1]].astype(f32)
    return jnp.concatenate([jnp.where(c == 0, a, b), jnp.where(c == 0, b, a)], axis=0)


def window_kernel(per, hd, heads, sc, *refs):
    x_ref, bc_ref, refs = refs[0], refs[1], refs[2:]
    other, refs = refs[: per - 1], refs[per - 1 :]
    small, refs = refs[:per], refs[per:]
    *tails, last0, last1, par, cx, cbc, bx, bbc, local_o, grow_o, pay_o = refs
    c = sc[0]
    taps = cx.shape[0]
    steps, batch, gwidth = x_ref.shape
    pair = bc_ref.shape[2]
    ns = pair // 2
    rows = per * batch
    whole = slice(None)
    tail = sum(t[...].astype(f32) for t in tails)
    prompt = rows_of(small, steps, (whole, whole), c)
    body_x = [rows_of([x_ref, *other], i, (whole, slice(0, gwidth)), c) for i in range(steps)]
    body_bc = [
        rows_of([bc_ref, *other], i, (whole, slice(gwidth, gwidth + pair)), c) for i in range(steps)
    ]

    def window(lo, hi, body):
        out = []
        for j in range(taps - 1):
            first, second = tail[j : j + 1, lo:hi], tail[8 + j : 9 + j, lo:hi]
            out.append(jnp.where(prompt[:, :1] == 0.0, first, second))
        return out + body

    def conv(full, taps_ref, bias):
        acts = []
        for i in range(steps):
            total = bias
            for k in range(taps):
                total = total + taps_ref[k : k + 1] * full[i + k]
            acts.append(silu(total))
        return acts

    xd = conv(window(0, gwidth, body_x), cx, bx[...])
    mix = conv(window(gwidth, gwidth + pair, body_bc), cbc, bbc[...])
    rate, dtb, skip = par[0:1], par[1:2], par[2:3]
    step = [softplus(rows_of(small, i, (whole, whole), c) + dtb) for i in range(steps)]
    upto = []
    for i in range(steps):
        upto.append((upto[-1] if upto else 0.0) - rate * step[i])
    coef = [jnp.broadcast_to(skip, (8, lanes))]
    for i in range(steps):
        read = mix[i][:, ns:]
        pay_o[i * rows : (i + 1) * rows, :ns] = read
        pay_o[i * rows : (i + 1) * rows, ns:] = prompt
        grow_o[i * rows : (i + 1) * rows] = jnp.exp(upto[i])
        for j in range(i + 1):
            both = jnp.sum(read * mix[j][:, :ns], axis=1, keepdims=True)
            coef.append(both * (jnp.exp(upto[i] - upto[j]) * step[j]))
    wide = exact(jnp.concatenate(coef, axis=0), to_channels(gwidth, hd, c * heads))
    at = 8
    for i in range(steps):
        y = wide[0:1] * xd[i]
        for j in range(i + 1):
            y = y + wide[at : at + rows] * xd[j]
            at += rows
        local_o[i * rows : (i + 1) * rows] = y
    pay_o[steps * rows :, :ns] = jnp.zeros((8, ns), f32)
    pay_o[steps * rows :, ns:] = jnp.concatenate(
        [last0[0, 7:8], last1[0, 7:8], jnp.zeros((6, lanes), f32)], axis=0
    )


def read_kernel(hd, heads, m, sc, *refs):
    blocks, own, outs = refs[:m], refs[m:-m], refs[-m:]
    half = pl.program_id(0)
    _, ns, bw = own[0].shape
    u = sc[1]
    rows = blocks[0].shape[0] - 8
    after = jnp.zeros((8, lanes), f32)
    for k in range(1, m):
        after = after + jnp.where(k > u, blocks[k][rows:, ns:], 0.0)
    spread = exact(jnp.exp(after), to_channels(bw, hd, 2 * heads + half * (bw // hd)))
    asked = jnp.concatenate([b[:rows, :ns] for b in blocks], axis=0)
    prompt = jnp.concatenate([b[:rows, ns : ns + 1] for b in blocks], axis=0)
    total = None
    for s in range(len(own)):
        c_hi, c_lo = halves(jnp.where(prompt == s, asked, 0.0))
        s_hi, s_lo = halves(own[s][0] * spread[s : s + 1])
        got = one_pass(c_hi, s_hi) + (one_pass(c_lo, s_hi) + one_pass(c_hi, s_lo))
        total = got if total is None else total + got
    for k in range(m):
        outs[k][...] = total[k * rows : (k + 1) * rows].astype(bf16)


def finish_kernel(per, hd, heads, m, sc, *refs):
    sums, local, grow, z_ref, refs = refs[:m], refs[m], refs[m + 1], refs[m + 2], refs[m + 3 :]
    *other, gain, out_o = refs
    c = sc[0]
    steps = z_ref.shape[0]
    gwidth = out_o.shape[1]
    total = sums[0][...].astype(f32)
    for r in sums[1:]:
        total = total + r[...].astype(f32)
    y = exact(grow[...], to_channels(gwidth, hd, c * heads)) * total + local[...]
    at = (slice(None), slice(other[0].shape[2] - gwidth, None) if other else None)
    gate = jnp.concatenate([rows_of([z_ref, *other], i, at, c) for i in range(steps)], axis=0)
    v = y * silu(gate)
    scale = lax.rsqrt(jnp.mean(v * v, axis=1, keepdims=True) + epsilon)
    out_o[...] = (v * scale * gain[...]).astype(bf16)


def project_kernel(per, m, sc, *refs):
    mine, other, w, out_o = refs[:m], refs[m:-2], refs[-2], refs[-1]
    c, u = sc[0], sc[1]
    tp, steps, rows_tp, cols = out_o.shape
    a = jnp.concatenate([r[...] for r in mine], axis=0)
    gwidth = a.shape[1]
    if per == 2:
        b = jnp.concatenate([r[...] for r in other], axis=0)
        total = one_pass(jnp.where(c == 0, a, b), w[:gwidth])
        total = total + one_pass(jnp.where(c == 0, b, a), w[gwidth:])
    else:
        total = one_pass(a, w[...])
    rows = a.shape[0] // (m * steps)
    each = m // tp
    for k in range(m):
        v = lax.rem(u - k + m, m)
        at = pl.ds(pl.multiple_of(lax.rem(v, each) * rows, rows), rows)
        for i in range(steps):
            first = (k * steps + i) * rows
            out_o[v // each, i, at, :] = total[first : first + rows]


def params(limit=vmem):
    return pltpu.CompilerParams(vmem_limit_bytes=limit)


def cost(us):
    return pl.CostEstimate(flops=int(us * 1.1e9), bytes_accessed=int(us * 3e6), transcendentals=0)


def tied(first, then):
    return lax.optimization_barrier((first, then))


def shards(
    inner_x,
    gate_z,
    proj_bc,
    dt_raw,
    a_log,
    dt_bias,
    d_skip,
    conv_x,
    conv_bc,
    bias_x,
    bias_bc,
    norm_gain,
    init_state,
    init_conv_x,
    init_conv_bc,
    lengths,
    dec_x,
    dec_z,
    dec_bc,
    dec_dt,
    row_prompt,
    w_out,
):
    prompts, tokens, width = inner_x.shape
    groups, pair = proj_bc.shape[2:]
    ns = pair // 2
    heads = dt_raw.shape[1] // groups
    gwidth = width // groups
    hd = gwidth // heads
    taps = conv_x.shape[0]
    steps, batch = dec_x.shape[:2]
    cols = w_out.shape[1]
    n = lax.axis_size("ctx")
    tp = lax.axis_size("tp")
    assert groups in (1, 2) and n % groups == 0 and 4 * heads == lanes
    per = groups
    m = n // per
    device = lax.axis_index("ctx")
    u, c = device // per, device % per
    unit_tokens = per * tokens
    rows_u = per * batch
    per_prompt = 2
    bw = gwidth // per_prompt
    parts = prompts * per_prompt

    def mine(arr, axis):
        return lax.dynamic_index_in_dim(arr, c, axis, keepdims=False)

    def swap(arr):
        return lax.ppermute(arr, "ctx", [(i, i ^ 1) for i in range(n)])

    def in_order(own, other, axis):
        first = jnp.where(c == 0, own, other)
        second = jnp.where(c == 0, other, own)
        return jnp.concatenate([first, second], axis=axis)

    def other_group(arr, size):
        if per == 1:
            return None
        at = [0] * (arr.ndim - 1) + [(1 - c) * size]
        return swap(lax.dynamic_slice(arr, at, arr.shape[:-1] + (size,)))

    def pair_up(arr, gaxis, taxis):
        if per == 1:
            return jnp.squeeze(arr, gaxis)
        other = swap(lax.dynamic_index_in_dim(arr, 1 - c, gaxis, keepdims=False))
        return in_order(mine(arr, gaxis), other, taxis)

    def shift(arr, k):
        return lax.ppermute(arr, "ctx", [(i, (i + k * per) % n) for i in range(n)])

    bc_flat = proj_bc.reshape(prompts, tokens, groups * pair)
    x_other = bc_other = None
    if per == 2:
        x_send = lax.dynamic_slice_in_dim(inner_x, (1 - c) * gwidth, gwidth, 2)
        x_other = swap(x_send)
        bc_other = other_group(bc_flat, pair)
    last_x = inner_x[:, tokens - taps + 1 :]
    last_bc = bc_flat[:, tokens - taps + 1 :]
    wide = gwidth + pair
    rim = jnp.zeros((prompts, taps - 1, wide), bf16)
    for g in range(per):
        pairs = [(v * per + per - 1, (v + 1) * per + g) for v in range(m - 1)]
        send = jnp.concatenate(
            [last_x[..., g * gwidth : (g + 1) * gwidth], last_bc[..., g * pair : (g + 1) * pair]],
            axis=-1,
        )
        got = lax.ppermute(send, "ctx", pairs)
        rim = jnp.where(c == g, got, rim)
    dt_in = [dt_raw]
    if per == 2:
        given = lax.dynamic_slice_in_dim(dt_raw, (1 - c) * heads, heads, 1)
        dt_in.append(swap(given))

    rate = jnp.exp(mine(a_log.reshape(groups, heads), 0))
    dtb = mine(dt_bias.reshape(groups, heads), 0)
    skip = jnp.repeat(mine(d_skip.reshape(groups, heads), 0), hd)[None]
    gain = mine(norm_gain.reshape(groups, 1, gwidth), 0)
    col = jnp.pad(jnp.stack([rate, dtb], axis=1), ((0, 0), (0, lanes - 2)))
    cbc = conv_bc.reshape(taps, groups * pair)
    bbc = bias_bc.reshape(1, groups * pair)
    bx = bias_x.reshape(1, width)
    start_rim = jnp.concatenate(
        [
            mine(init_conv_x.reshape(prompts, taps - 1, groups, gwidth), 2),
            mine(init_conv_bc, 2),
        ],
        axis=-1,
    )
    rim = jnp.where(u == 0, start_rim, rim).astype(f32)
    rim = jnp.pad(rim, ((0, 0), (8 - (taps - 1), 0), (0, 0)))
    start = init_state.reshape(prompts, groups * gwidth, ns)
    sc = jnp.concatenate([jnp.stack([c, u]).astype(jnp.int32), lengths])

    x_in = [inner_x] + ([x_other] if per == 2 else [])
    bc_in = [bc_flat] + ([bc_other] if per == 2 else [])
    T = unit_tokens
    spec = pl.BlockSpec

    def front(s, dts):
        in_specs = [spec((1, tokens, bw), lambda k, sc: (s, 0, sc[0] * per_prompt + k))]
        in_specs += [spec((1, tokens, bw), lambda k, sc: (s, 0, k))] * (per - 1)
        in_specs += [spec((1, tokens, pair), lambda k, sc: (s, 0, sc[0]))]
        in_specs += [spec((1, tokens, pair), lambda k, sc: (s, 0, 0))] * (per - 1)
        in_specs += [spec((1, heads, tokens), lambda k, sc: (s, sc[0], 0))]
        in_specs += [spec((1, heads, tokens), lambda k, sc: (s, 0, 0))] * (per - 1)
        in_specs += [
            spec((1, 8, bw), lambda k, sc: (s, 0, k)),
            spec((1, 8, pair), lambda k, sc: (s, 0, 0)),
            spec((heads, lanes), lambda k, sc: (0, 0)),
            spec((taps, bw), lambda k, sc: (0, sc[0] * per_prompt + k)),
            spec((taps, pair), lambda k, sc: (0, sc[0])),
            spec((1, bw), lambda k, sc: (0, sc[0] * per_prompt + k)),
            spec((1, pair), lambda k, sc: (0, sc[0])),
            spec((1, bw, ns), lambda k, sc: (s, sc[0] * per_prompt + k, 0)),
        ]
        chunk = lambda k, sc: (k, 0, 0)
        whole = lambda k, sc: (0, 0, 0)
        return pl.pallas_call(
            functools.partial(front_kernel, per, hd, s),
            grid_spec=pltpu.PrefetchScalarGridSpec(
                num_scalar_prefetch=1,
                grid=(per_prompt,),
                in_specs=in_specs,
                out_specs=[
                    spec((1, T, bw), lambda k, sc: (0, 0, k)),
                    spec((1, T, pair), whole),
                    spec((1, heads, T), whole),
                    spec((1, heads, T), whole),
                    spec((1, T, lanes), whole),
                    spec((1, ns, bw), chunk),
                    spec((1, 8, bw), chunk),
                    spec((1, ns, bw), chunk),
                ],
                scratch_shapes=[
                    pltpu.VMEM((T + 8, bw), f32),
                    pltpu.VMEM((T + 8, pair), f32),
                    pltpu.VMEM((ns, T), f32),
                ],
            ),
            out_shape=[
                jax.ShapeDtypeStruct((1, T, gwidth), f32),
                jax.ShapeDtypeStruct((1, T, pair), f32),
                jax.ShapeDtypeStruct((1, heads, T), f32),
                jax.ShapeDtypeStruct((1, heads, T), f32),
                jax.ShapeDtypeStruct((1, T, lanes), f32),
                jax.ShapeDtypeStruct((per_prompt, ns, bw), f32),
                jax.ShapeDtypeStruct((per_prompt, 8, bw), f32),
                jax.ShapeDtypeStruct((per_prompt, ns, bw), bf16),
            ],
            compiler_params=params(),
            cost_estimate=cost(9),
            name="front",
        )(sc, *x_in, *bc_in, *dts, rim[..., :gwidth], rim[..., gwidth:], col, conv_x, cbc, bx, bbc, start)

    def local_part(s, k, act):
        _, bc, run, step, pack = fronts[s][:5]
        return pl.pallas_call(
            functools.partial(local_kernel, hd, k),
            grid=(1,),
            in_specs=[
                spec((1, T, bw), lambda i: (0, 0, k)),
                spec((1, T, pair), lambda i: (0, 0, 0)),
                spec((1, heads, T), lambda i: (0, 0, 0)),
                spec((1, heads, T), lambda i: (0, 0, 0)),
                spec((1, T, lanes), lambda i: (0, 0, 0)),
                spec((1, bw), lambda i: (0, k)),
            ],
            out_specs=spec((1, T, bw), lambda i: (0, 0, 0)),
            out_shape=jax.ShapeDtypeStruct((1, T, bw), f32),
            scratch_shapes=[pltpu.VMEM((T, T), f32)],
            compiler_params=params(),
            cost_estimate=cost(5),
            name="local",
        )(act, bc, run, step, pack, skip)

    fronts = [list(front(0, dt_in))]
    after_front = fronts[0][5]
    _, lengths_late = tied(after_front, lengths)
    _, dec_x = tied(after_front, dec_x)
    _, dec_bc = tied(after_front, dec_bc)
    _, dec_z = tied(after_front, dec_z)
    _, dec_dt = tied(after_front, dec_dt)
    _, row_prompt = tied(after_front, row_prompt)
    want = jnp.arange(8, dtype=jnp.int32)
    target = lengths_late[:, None] - (taps - 1) + want
    target = jnp.where(want < taps - 1, target, -1)
    places = device * tokens + jnp.arange(tokens, dtype=jnp.int32)
    hit = places[None, None, :] == target[:, :, None]
    same = jnp.arange(prompts)[:, None] == jnp.arange(prompts)[None, :]
    picker = (hit[:, :, None, :] & same[:, None, :, None]).astype(bf16)
    picker = picker.reshape(prompts * 8, prompts * tokens)
    tail_x = jnp.dot(picker, inner_x.reshape(-1, width), preferred_element_type=f32).astype(bf16)
    tail_bc = jnp.dot(
        picker, bc_flat.reshape(-1, groups * pair), preferred_element_type=f32
    ).astype(bf16)

    def tail_of(g):
        return jnp.concatenate(
            [
                lax.dynamic_slice_in_dim(tail_x, g * gwidth, gwidth, 1),
                lax.dynamic_slice_in_dim(tail_bc, g * pair, pair, 1),
            ],
            axis=1,
        )

    tails = tail_of(c)
    dec_bc = dec_bc.reshape(steps, batch, groups * pair)
    small = jnp.concatenate(
        [
            jnp.pad(jnp.transpose(dec_dt, (0, 2, 1)), ((0, 0), (0, 0), (0, lanes - groups * heads))),
            jnp.broadcast_to(row_prompt.astype(f32)[None, :, None], (1, batch, lanes)),
        ],
        axis=0,
    )
    small = [small]
    dec_other = []
    if per == 2:
        tails = tails + swap(tail_of(1 - c))
        small.append(swap(small[0]))
        dec_other = [
            swap(
                jnp.concatenate(
                    [
                        lax.dynamic_slice_in_dim(dec_x, (1 - c) * gwidth, gwidth, 2),
                        lax.dynamic_slice_in_dim(dec_bc, (1 - c) * pair, pair, 2),
                        lax.dynamic_slice_in_dim(dec_z, (1 - c) * gwidth, gwidth, 2),
                    ],
                    axis=2,
                )
            )
        ]
    tails = [tails] + [shift(tails, k) for k in range(1, m)]
    par = jnp.pad(
        jnp.stack([jnp.exp(a_log), dt_bias, d_skip]), ((0, 5), (0, lanes - groups * heads))
    )
    asked_rows = steps * rows_u

    def full_spec(arr):
        return spec(arr.shape, lambda *_: (0,) * arr.ndim)

    def window(first):
        _, late = tied(first, par)
        last = spec((1, 8, lanes), lambda i, sc: (0, T // 8 - 1, 0))
        return pl.pallas_call(
            functools.partial(window_kernel, per, hd, heads),
            grid_spec=pltpu.PrefetchScalarGridSpec(
                num_scalar_prefetch=1,
                grid=(1,),
                in_specs=[
                    spec((steps, batch, gwidth), lambda i, sc: (0, 0, sc[0])),
                    spec((steps, batch, pair), lambda i, sc: (0, 0, sc[0])),
                ]
                + [full_spec(a) for a in dec_other + small + tails]
                + [last, last, full_spec(par)]
                + [
                    spec((taps, gwidth), lambda i, sc: (0, sc[0])),
                    spec((taps, pair), lambda i, sc: (0, sc[0])),
                    spec((1, gwidth), lambda i, sc: (0, sc[0])),
                    spec((1, pair), lambda i, sc: (0, sc[0])),
                ],
                out_specs=[
                    spec((asked_rows, gwidth), lambda i, sc: (0, 0)),
                    spec((asked_rows, lanes), lambda i, sc: (0, 0)),
                    spec((asked_rows + 8, ns + lanes), lambda i, sc: (0, 0)),
                ],
            ),
            out_shape=[
                jax.ShapeDtypeStruct((asked_rows, gwidth), f32),
                jax.ShapeDtypeStruct((asked_rows, lanes), f32),
                jax.ShapeDtypeStruct((asked_rows + 8, ns + lanes), f32),
            ],
            compiler_params=params(),
            cost_estimate=cost(2),
            name="window",
        )(sc, dec_x, dec_bc, *dec_other, *small, *tails, fronts[0][4], fronts[1][4], late,
          conv_x, cbc, bx, bbc)

    def read(blocks, first):
        _, blocks[0] = tied(first, blocks[0])
        return pl.pallas_call(
            functools.partial(read_kernel, hd, heads, m),
            grid_spec=pltpu.PrefetchScalarGridSpec(
                num_scalar_prefetch=1,
                grid=(per_prompt,),
                in_specs=[full_spec(b) for b in blocks]
                + [spec((1, ns, bw), lambda k, sc: (k, 0, 0))] * prompts,
                out_specs=[spec((asked_rows, bw), lambda k, sc: (0, k))] * m,
            ),
            out_shape=[jax.ShapeDtypeStruct((asked_rows, gwidth), bf16)] * m,
            compiler_params=params(),
            cost_estimate=cost(4),
            name="read",
        )(sc, *blocks, *[f[5] for f in fronts])

    def finish(sums, local, grow):
        return pl.pallas_call(
            functools.partial(finish_kernel, per, hd, heads, m),
            grid_spec=pltpu.PrefetchScalarGridSpec(
                num_scalar_prefetch=1,
                grid=(1,),
                in_specs=[full_spec(a) for a in (*sums, local, grow)]
                + [spec((steps, batch, gwidth), lambda i, sc: (0, 0, sc[0]))]
                + [full_spec(a) for a in dec_other + [gain]],
                out_specs=spec((asked_rows, gwidth), lambda i, sc: (0, 0)),
            ),
            out_shape=jax.ShapeDtypeStruct((asked_rows, gwidth), bf16),
            compiler_params=params(),
            cost_estimate=cost(3),
            name="finish",
        )(sc, *sums, local, grow, dec_z, *dec_other, gain)

    def project(blocks):
        others = [swap(b) for b in blocks] if per == 2 else []
        cb = min(256, cols)
        return pl.pallas_call(
            functools.partial(project_kernel, per, m),
            grid_spec=pltpu.PrefetchScalarGridSpec(
                num_scalar_prefetch=1,
                grid=(cols // cb,),
                in_specs=[full_spec(b) for b in blocks + others]
                + [spec((width, cb), lambda i, sc: (0, i))],
                out_specs=spec((tp, steps, m * rows_u // tp, cb), lambda i, sc: (0, 0, 0, i)),
            ),
            out_shape=jax.ShapeDtypeStruct((tp, steps, m * rows_u // tp, cols), f32),
            compiler_params=params(),
            cost_estimate=cost(6),
            name="project",
        )(sc, *blocks, *others, w_out)

    arrived, y_local, outs = [], [], []

    def back(s, first):
        entry = []
        for k in range(s * per_prompt, (s + 1) * per_prompt):
            e = fronts[s][7][k % per_prompt]
            for v in range(1, m):
                e = jnp.where(u == v, arrived[k + v - 1], e)
            entry.append(e)
        _, pack = tied(first, fronts[s][4])
        z_in = [gate_z] + ([z_other] if per == 2 else [])
        z_specs = [spec((1, tokens, gwidth), lambda j, sc: (s, 0, sc[0]))]
        z_specs += [spec((1, tokens, gwidth), lambda j, sc: (s, 0, 0))] * (per - 1)
        return pl.pallas_call(
            functools.partial(back_kernel, per, hd, heads),
            grid_spec=pltpu.PrefetchScalarGridSpec(
                num_scalar_prefetch=1,
                grid=(per,),
                in_specs=z_specs
                + [spec((1, ns, bw), lambda j, sc: (0, 0, 0))] * per_prompt
                + [
                    spec((1, tokens, pair), lambda j, sc: (0, j, 0)),
                    spec((1, tokens, lanes), lambda j, sc: (0, j, 0)),
                    spec((1, gwidth), lambda j, sc: (0, 0)),
                ]
                + [spec((1, tokens, bw), lambda j, sc: (0, j, 0))] * per_prompt,
                out_specs=spec(
                    (1, tokens, gwidth), lambda j, sc: (jnp.where(j == sc[0], 0, 1), 0, 0)
                ),
                scratch_shapes=[pltpu.VMEM((tokens, gwidth), f32)],
            ),
            out_shape=jax.ShapeDtypeStruct((per, tokens, gwidth), bf16),
            compiler_params=params(60 * 1024 * 1024),
            cost_estimate=cost(5),
            name="back",
        )(
            sc,
            *z_in,
            *[e[None] for e in entry],
            fronts[s][1],
            pack,
            gain,
            *y_local[s * per_prompt : (s + 1) * per_prompt],
        )

    carry = jnp.zeros((ns, bw), bf16)
    along = [(i, i + per) for i in range(n - per)]

    def locals_after(first, count, moved):
        for _ in range(count):
            s, k = divmod(len(y_local), per_prompt)
            if s == prompts:
                break
            _, act = tied(first, fronts[s][0])
            first = local_part(s, k, act)
            y_local.append(first)
            moved, _ = tied(moved, first)
        return moved

    for t in range(parts + m - 2):
        at_k = jnp.clip(t - u, 0, parts - 1)
        leave = None
        for s in range(prompts - 1, -1, -1):
            if t < s * per_prompt:
                continue
            at_s = jnp.clip(at_k - s * per_prompt, 0, per_prompt - 1)
            own_t = lax.dynamic_index_in_dim(fronts[s][5], at_s, 0, keepdims=False)
            decay_t = lax.dynamic_index_in_dim(fronts[s][6], at_s, 0, keepdims=False)[:1]
            new = (decay_t * carry.astype(f32) + own_t).astype(bf16)
            leave = new if leave is None else jnp.where(at_k < (s + 1) * per_prompt, new, leave)
        moved = lax.ppermute(leave, "ctx", along)
        if t == 0:
            for s in range(1, prompts):
                _, sc = tied(leave, sc)
                fronts.append(list(front(s, dt_in)))
            moved, _ = tied(moved, fronts[-1][5])
        if t == 1:
            moved = locals_after(leave, 1, moved)
            local, grow, payload = window(y_local[-1])
            blocks = [payload] + [shift(payload, k) for k in range(1, m)]
            moved = locals_after(payload, 1, moved)
        if t == 2:
            sends = list(read(blocks, leave))
            sums = sends[:1] + [shift(sends[k], -k) for k in range(1, m)]
            _, gate_late = tied(sends[-1], gate_z)
            z_other = other_group(gate_late, gwidth)
            moved = locals_after(sends[-1], 1, moved)
        if t == 3:
            moved = locals_after(leave, 1, moved)
            _, sums[0] = tied(y_local[-1], sums[0])
            hidden = finish(sums, local, grow)
            moved, _ = tied(moved, hidden)
            if per == 2:
                moved, _ = tied(moved, z_other)
        if t == 4:
            around = [hidden] + [shift(hidden, k) for k in range(1, m)]
            for got in around:
                moved, _ = tied(moved, got)
        if t == 5:
            _, around[0] = tied(leave, around[0])
            product = project(around)
            terms = lax.all_to_all(product, "tp", 0, 0)
        if t == per_prompt + m - 2:
            outs.append(back(0, leave))
            moved, _ = tied(moved, outs[0])
        if t == parts + m - 3:
            moved, _ = tied(moved, product)
        carry = moved
        arrived.append(carry)
    while len(y_local) < parts:
        done = len(y_local)
        y_local.append(local_part(done // per_prompt, done % per_prompt, fronts[done // per_prompt][0]))

    layer_out = jnp.sum(terms, axis=0).astype(bf16)
    for s in range(1, prompts):
        outs.append(back(s, carry))
    full_outs = []
    for out in outs:
        if per == 1:
            full_outs.append(out[0])
            continue
        given = swap(out[1])
        _, kept = tied(layer_out, out[0])
        full_outs.append(in_order(kept, given, 1))
    return (jnp.stack(full_outs), layer_out)


def solution(mesh):
    in_specs = (
        P(None, "ctx", "tp"),
        P(None, "ctx", "tp"),
        P(None, "ctx", "tp", None),
        P(None, "tp", "ctx"),
        P("tp"),
        P("tp"),
        P("tp"),
        P(None, "tp"),
        P(None, "tp", None),
        P("tp"),
        P("tp", None),
        P("tp"),
        P(None, "tp", None, None),
        P(None, None, "tp"),
        P(None, None, "tp", None),
        P(),
        P(None, "ctx", "tp"),
        P(None, "ctx", "tp"),
        P(None, "ctx", "tp", None),
        P(None, "tp", "ctx"),
        P("ctx"),
        P("tp", "ctx"),
    )
    out_specs = (P(None, "ctx", "tp"), P(None, "tp", "ctx"))
    return jax.shard_map(shards, mesh=mesh, in_specs=in_specs, out_specs=out_specs, check_vma=False)
```

time: 280 us -> 208 us (0.74)
  waiting for transfers between devices: 97.7 us -> 15.1 us
  starting transfers between devices: 58.1 us -> 85.9 us
  between operations: 15.2 us -> 1.88 us
  Pallas kernels: 48.4 us -> 60.5 us
  matrix products: 7.43 us -> 0.64 us
  other arithmetic: 24.2 us -> 19.2 us
  local copies, waits for them, and re-layouts: 27.6 us -> 23.4 us
    psum x1 -> x0, waiting for transfers between devices: 37.9 us -> none  [shards(): tails = lax.psum(tails, 'ctx')]
    ppermute x9 -> x12, waiting for transfers between devices: 33.9 us -> 9.32 us  [shift(): return lax.ppermute(arr, 'ctx', [(i, (i + k * per) % n) for i in range(n)])]
    ppermute x6, waiting for transfers between devices: 23.4 us -> 2.29 us  [shards(): moved = lax.ppermute(leave, 'ctx', along)]
    ppermute x6, starting transfers between devices: 27 us -> 46.7 us  [shards(): moved = lax.ppermute(leave, 'ctx', along)]
    pallas_call x7 -> x12, Pallas kernels: 48.4 us -> 60.5 us  [the longest x2 18.7 us: front(): pl.pallas_call(functools.partial(front_kernel, per, hd, s), grid_spec=plt...]
    ppermute x9 -> x12, starting transfers between devices: 18.8 us -> 26.7 us  [shift(): return lax.ppermute(arr, 'ctx', [(i, (i + k * per) % n) for i in range(n)])]
    dot_general x3 -> x2, matrix products: 7.43 us -> 0.64 us  [the longest x1 0.42 us: shards(): jnp.dot(picker, inner_x.reshape(-1, width), preferred_element_type=f32)]
    convert_element_type x8 -> x3, other arithmetic: 7.36 us -> 3.2 us  [the longest x2 2.54 us: shards(): new = (decay_t * carry.astype(f32) + own_t).astype(bf16)]
  transfers between devices with their start and end apart: 29 -> 34, of which waited for: 11 -> 5; matrix products, arithmetic and copies ran while one was open for 15% -> 12% of each run, Pallas kernels for 9% -> 25%
where the time goes in v1:
time: 208 us; the launch traced here: 207 us
  starting transfers between devices  85.9 us (41%)
  Pallas kernels  60.5 us (29%)
  local copies, waits for them, and re-layouts  23.4 us (11%)
  other arithmetic  19.2 us (9%)
  waiting for transfers between devices  15.1 us (7%)
    ppermute x6, starting transfers between devices, shards(): moved = lax.ppermute(leave, 'ctx', along)  46.7 us
    ppermute x12, starting transfers between devices, shift(): return lax.ppermute(arr, 'ctx', [(i, (i + k * per) % n) for i in range(n)])  26.7 us
    pallas_call x2, Pallas kernels, front(): pl.pallas_call(functools.partial(front_kernel, per, hd, s), grid_spec=plt...  18.7 us
    pallas_call x4, Pallas kernels, local_part(): pl.pallas_call(functools.partial(local_kernel, hd, k), grid=(1,), in_spec...  16.3 us
    unnamed x140, local copies, waits for them, and re-layouts  14.3 us
    pallas_call x2, Pallas kernels, back(): pl.pallas_call(functools.partial(back_kernel, per, hd, heads), grid_spec=...  13.1 us
    ppermute x12, waiting for transfers between devices, shift(): return lax.ppermute(arr, 'ctx', [(i, (i + k * per) % n) for i in range(n)])  9.32 us
    ppermute x13, starting transfers between devices, swap(): return lax.ppermute(arr, 'ctx', [(i, i ^ 1) for i in range(n)])  7.25 us
  transfers between devices with their start and end apart: 34, of which 5 were waited for; matrix products, arithmetic and copies ran while one was open for 12% of the time, Pallas kernels for 25%

profile of v1, /device:TPU:0, one launch (start us, length us, event | category | flops | bytes accessed | tf_op | source)
XLA Modules:
  0.0 206.5 jit_solution(6283911158153726414)
XLA Ops:
  0.8 2.4 %constant_dynamic-slice_fusion.26 = bf16[2,128,2048]{2,1,0:T(8,128)(2,1)} fusion(bf16[2,128,4096]{2,1,0:T(8,128)(2,1)} %refs_0_.5, s32[]{:T(128)S(6)} %select_n.197), kind=kLoop, calls=%fused_computation.102 | loop fusion | bytes 2097156 | tf_op jit(solution)/shard_map/dynamic_slice | solution.py:399
  3.6 0.9 fusion.48
  5.0 0.7 collective-permute-start.3
  5.7 0.7 collective-permute-start.4
  6.4 4.7 %collective-permute-start.1 = (bf16[2,128,512]{2,1,0:T(8,128)(2,1)S(1)}, bf16[2,128,512]{2,1,0:T(8,128)(2,1)S(1)}, u32[]{:S(2)}, u32[]{:S(2)}) collective-permute-start(bf16[2,128,512]{2,1,0:T(8,128)(2,1)S(1)} %constant_dynamic-slice_fusion.25), channel_id=1, source_target_pairs={{0,4},{4,0},{8,12},{12,8},{16,20},{20,16},{24,28},{28,24},{1,5},{5... | collective-permute-start | bytes 786440 | tf_op jit(solution)/shard_map/ppermute | solution.py:374
  13.7 0.9 copy.39
  14.9 1.0 copy-done.16
  15.9 1.6 copy-done.3
  17.5 1.2 copy-done.17
  18.7 9.3 %front.2 = (f32[1,256,2048]{2,1,0:T(8,128)S(1)}, f32[1,256,512]{2,1,0:T(8,128)S(1)}, f32[1,32,256]{2,1,0:T(8,128)S(1)}, f32[1,32,256]{2,1,0:T(8,128)S(1)}, f32[1...) custom-call(s32[4]{0:T(128)S(1)} %pad_add_fusion.sc, ...), custom_call_target="tpu_custom_call" | custom-call | flops 9900000256 | bytes 27000000 | tf_op jit(solution)/shard_map/front/pallas_call | solution.py:463
  28.1 0.7 copy-done.19
  29.4 0.7 constant_dynamic-slice_fusion.18
  30.2 1.3 fusion.17
  31.5 4.1 %collective-permute-start.5 = (bf16[256,1024]{1,0:T(8,128)(2,1)}, bf16[256,1024]{1,0:T(8,128)(2,1)}, u32[]{:S(2)}, u32[]{:S(2)}) collective-permute-start(bf16[256,1024]{1,0:T(8,128)(2,1)} %fusion.17), channel_id=1, source_target_pairs={{0,8},{4,12},{8,16},{12,20},{16,24},{20,28},{1,9},{5,13},{9,17},{1... | collective-permute-start | bytes 1572872 | tf_op jit(solution)/shard_map/ppermute | solution.py:745
  36.4 0.6 constant_dynamic-slice_fusion.8
  37.0 0.6 constant_dynamic-slice_fusion.9
  37.7 0.6 pad_maximum_fusion.2
  38.4 0.9 reshape.152.refs_1_
  39.8 0.7 convert_element_type.76
  40.6 0.7 select_maximum_fusion.refs_3_
  41.5 1.6 copy-done.4
  43.0 1.2 copy-done.18
  44.3 0.9 copy-done.20
  45.2 0.8 copy-done.22
  46.1 9.3 %front.3 = (f32[1,256,2048]{2,1,0:T(8,128)S(1)}, f32[1,256,512]{2,1,0:T(8,128)S(1)}, f32[1,32,256]{2,1,0:T(8,128)S(1)}, f32[1,32,256]{2,1,0:T(8,128)S(1)}, f32[1...) custom-call(s32[4]{0:T(128)S(1)} %pad_add_fusion.sc, ...), custom_call_target="tpu_custom_call" | custom-call | flops 9900000256 | bytes 27000000 | tf_op jit(solution)/shard_map/front/pallas_call | solution.py:463
  55.6 1.4 maximum_add_fusion.refs_5_
  57.5 3.4 %collective-permute-start.12 = (bf16[16,2560]{1,0:T(8,128)(2,1)S(1)}, bf16[16,2560]{1,0:T(8,128)(2,1)S(1)}, u32[]{:S(2)}, u32[]{:S(2)}) collective-permute-start(bf16[16,2560]{1,0:T(8,128)(2,1)S(1)} %maximum_add_fusion.refs_5_), channel_id=1, source_target_pairs={{0,24},{4,28},{8,0},{12,4},{16,8},{20,12},{24,16},{28,20},{1,25},{... | collective-permute-start | bytes 245768 | tf_op jit(solution)/shard_map/ppermute | solution.py:394
  60.9 1.2 fusion.16
  62.1 4.1 %local.4.refs_7_ = f32[1,256,1024]{2,1,0:T(8,128)S(1)} custom-call(f32[1,256,2048]{2,1,0:T(8,128)S(1)} %copy-done.25, f32[1,256,512]{2,1,0:T(8,128)S(1)} %copy-done.32, f32[1,32,256]{2,1,0:T(8,128)S(1)} %copy-done.37, f32[1,32,256]{2,1,0:T(8,128)S(1)} %copy-done.39, f32[1,256,128]{2,1,0:T(8,128)S(1)} %copy-done.35, f32[1,2048]{1,0:T(1,128)S(1)} %broadcast_in_dim_reshape.3.skip), custom_call_target="tpu_custom_call" | custom-call | flops 5500000256 | bytes 15000000 | tf_op jit(solution)/shard_map/local/pallas_call | solution.py:502
  66.2 2.5 %collective-permute-start.6 = (bf16[256,1024]{1,0:T(8,128)(2,1)S(1)}, bf16[256,1024]{1,0:T(8,128)(2,1)S(1)}, u32[]{:S(2)}, u32[]{:S(2)}) collective-permute-start(bf16[256,1024]{1,0:T(8,128)(2,1)S(1)} %fusion.16), channel_id=1, source_target_pairs={{0,8},{4,12},{8,16},{12,20},{16,24},{20,28},{1,9},{5,13},{9,17},{1... | collective-permute-start | bytes 1572872 | tf_op jit(solution)/shard_map/ppermute | solution.py:745
  68.8 2.1 %window.1 = (f32[64,2048]{1,0:T(8,128)S(1)}, f32[64,128]{1,0:T(8,128)S(1)}, f32[72,384]{1,0:T(8,128)S(1)}) custom-call(s32[4]{0:T(128)S(1)} %pad_add_fusion.sc, bf16[4,8,4096]{2,1,0:T(8,128)(2,1)S(1)} %copy-done.9, bf16[4,8,1024]{2,1,0:T(8,128)(2,1)S(1)} %reshape.152.refs_1_, bf16[4,8,4608]{2,1,0:T(8,128)(2,1)S(1)} %collective-permute-done.7.refs_2_.refs_7_, ...), custom_call_target="tpu_custom_call" | custom-call | flops 2200000000 | bytes 6000000 | tf_op jit(solution)/shard_map/window/pallas_call | solution.py:589
  71.0 2.0 collective-permute-start.14
  73.0 2.4 %collective-permute-start.16 = (f32[72,384]{1,0:T(8,128)S(1)}, f32[72,384]{1,0:T(8,128)S(1)}, u32[]{:S(2)}, u32[]{:S(2)}) collective-permute-start(f32[72,384]{1,0:T(8,128)S(1)} %get-tuple-element.82.refs_0_), channel_id=1, source_target_pairs={{0,24},{4,28},{8,0},{12,4},{16,8},{20,12},{24,16},{28,20},{1,25},{... | collective-permute-start | bytes 331784 | tf_op jit(solution)/shard_map/ppermute | solution.py:394
  75.5 4.1 %local.5.refs_8_ = f32[1,256,1024]{2,1,0:T(8,128)S(1)} custom-call(f32[1,256,2048]{2,1,0:T(8,128)S(1)} %copy-done.25, f32[1,256,512]{2,1,0:T(8,128)S(1)} %copy-done.32, f32[1,32,256]{2,1,0:T(8,128)S(1)} %copy-done.37, f32[1,32,256]{2,1,0:T(8,128)S(1)} %copy-done.39, f32[1,256,128]{2,1,0:T(8,128)S(1)} %copy-done.35, f32[1,2048]{1,0:T(1,128)S(1)} %broadcast_in_dim_reshape.3.skip), custom_call_target="tpu_custom_call" | custom-call | flops 5500000256 | bytes 15000000 | tf_op jit(solution)/shard_map/local/pallas_call | solution.py:502
  79.5 1.5 collective-permute-done.6
  81.4 4.5 %collective-permute-start.13 = (bf16[256,1024]{1,0:T(8,128)(2,1)S(1)}, bf16[256,1024]{1,0:T(8,128)(2,1)S(1)}, u32[]{:S(2)}, u32[]{:S(2)}) collective-permute-start(bf16[256,1024]{1,0:T(8,128)(2,1)S(1)} %fusion.21), channel_id=1, source_target_pairs={{0,8},{4,12},{8,16},{12,20},{16,24},{20,28},{1,9},{5,13},{9,17},{1... | collective-permute-start | bytes 1572872 | tf_op jit(solution)/shard_map/ppermute | solution.py:745
  85.9 2.3 %collective-permute-done.16.refs_3_ = f32[72,384]{1,0:T(8,128)S(1)} collective-permute-done((f32[72,384]{1,0:T(8,128)S(1)}, f32[72,384]{1,0:T(8,128)S(1)}, u32[]{:S(2)}, u32[]{:S(2)}) %collective-permute-start.16) | collective-permute-done | bytes 110624 | tf_op jit(solution)/shard_map/ppermute | solution.py:394
  88.2 3.5 %read.1 = (bf16[64,2048]{1,0:T(8,128)(2,1)S(1)}, bf16[64,2048]{1,0:T(8,128)(2,1)S(1)}, bf16[64,2048]{1,0:T(8,128)(2,1)S(1)}, bf16[64,2048]{1,0:T(8,128)(2,1)S(1)}) custom-call(s32[4]{0:T(128)S(1)} %pad_add_fusion.sc, f32[72,384]{1,0:T(8,128)S(1)} %get-tuple-element.82.refs_0_, f32[72,384]{1,0:T(8,128)S(1)} %collective-permute-done.14.refs_1_, ...), custom_call_target="tpu_custom_call" | custom-call | flops 4400000000 | bytes 12000000 | tf_op jit(solution)/shard_map/read/pallas_call | solution.py:625
  91.7 4.4 %collective-permute-start.20 = (bf16[64,2048]{1,0:T(8,128)(2,1)S(1)}, bf16[64,2048]{1,0:T(8,128)(2,1)S(1)}, u32[]{:S(2)}, u32[]{:S(2)}) collective-permute-start(bf16[64,2048]{1,0:T(8,128)(2,1)S(1)} %get-tuple-element.83), channel_id=1, source_target_pairs={{0,8},{4,12},{8,16},{12,20},{16,24},{20,28},{24,0},{28,4},{1,9},{5... | collective-permute-start | bytes 786440 | tf_op jit(solution)/shard_map/ppermute | solution.py:394
  96.2 2.9 %collective-permute-start.18 = (bf16[64,2048]{1,0:T(8,128)(2,1)S(1)}, bf16[64,2048]{1,0:T(8,128)(2,1)S(1)}, u32[]{:S(2)}, u32[]{:S(2)}) collective-permute-start(bf16[64,2048]{1,0:T(8,128)(2,1)S(1)} %get-tuple-element.94), channel_id=1, source_target_pairs={{0,24},{4,28},{8,0},{12,4},{16,8},{20,12},{24,16},{28,20},{1,25},{... | collective-permute-start | bytes 786440 | tf_op jit(solution)/shard_map/ppermute | solution.py:394
  99.7 4.1 %local.6.refs_7_ = f32[1,256,1024]{2,1,0:T(8,128)S(1)} custom-call(f32[1,256,2048]{2,1,0:T(8,128)S(1)} %get-tuple-element.90.act, f32[1,256,512]{2,1,0:T(8,128)S(1)} %get-tuple-element.86.bc.refs_4_, f32[1,32,256]{2,1,0:T(8,128)S(1)} %get-tuple-element.87.run, f32[1,32,256]{2,1,0:T(8,128)S(1)} %get-tuple-element.88.step, ...), custom_call_target="tpu_custom_call" | custom-call | flops 5500000256 | bytes 15000000 | tf_op jit(solution)/shard_map/local/pallas_call | solution.py:502
  104.1 4.0 %collective-permute-start.17 = (bf16[256,1024]{1,0:T(8,128)(2,1)S(1)}, bf16[256,1024]{1,0:T(8,128)(2,1)S(1)}, u32[]{:S(2)}, u32[]{:S(2)}) collective-permute-start(bf16[256,1024]{1,0:T(8,128)(2,1)S(1)} %fusion.20), channel_id=1, source_target_pairs={{0,8},{4,12},{8,16},{12,20},{16,24},{20,28},{1,9},{5,13},{9,17},{1... | collective-permute-start | bytes 1572872 | tf_op jit(solution)/shard_map/ppermute | solution.py:745
  108.1 4.1 %local.7.refs_8_ = f32[1,256,1024]{2,1,0:T(8,128)S(1)} custom-call(f32[1,256,2048]{2,1,0:T(8,128)S(1)} %get-tuple-element.90.act, f32[1,256,512]{2,1,0:T(8,128)S(1)} %get-tuple-element.86.bc.refs_4_, f32[1,32,256]{2,1,0:T(8,128)S(1)} %get-tuple-element.87.run, f32[1,32,256]{2,1,0:T(8,128)S(1)} %get-tuple-element.88.step, ...), custom_call_target="tpu_custom_call" | custom-call | flops 5500000256 | bytes 15000000 | tf_op jit(solution)/shard_map/local/pallas_call | solution.py:502
  112.2 7.0 %collective-permute-done.19.refs_2_ = bf16[64,2048]{1,0:T(8,128)(2,1)S(1)} collective-permute-done((bf16[64,2048]{1,0:T(8,128)(2,1)S(1)}, bf16[64,2048]{1,0:T(8,128)(2,1)S(1)}, u32[]{:S(2)}, u32[]{:S(2)}) %collective-permute-start.19) | collective-permute-done | bytes 262176 | tf_op jit(solution)/shard_map/ppermute | solution.py:394
  119.3 1.5 finish.1.refs_0_
  120.9 7.1 %collective-permute-start.23 = (bf16[64,2048]{1,0:T(8,128)(2,1)S(1)}, bf16[64,2048]{1,0:T(8,128)(2,1)S(1)}, u32[]{:S(2)}, u32[]{:S(2)}) collective-permute-start(bf16[64,2048]{1,0:T(8,128)(2,1)S(1)} %finish.1.refs_0_), channel_id=1, source_target_pairs={{0,8},{4,12},{8,16},{12,20},{16,24},{20,28},{24,0},{28,4},{1,9},{5... | collective-permute-start | bytes 786440 | tf_op jit(solution)/shard_map/ppermute | solution.py:394
  128.0 3.4 %collective-permute-start.24 = (bf16[64,2048]{1,0:T(8,128)(2,1)S(1)}, bf16[64,2048]{1,0:T(8,128)(2,1)S(1)}, u32[]{:S(2)}, u32[]{:S(2)}) collective-permute-start(bf16[64,2048]{1,0:T(8,128)(2,1)S(1)} %finish.1.refs_0_), channel_id=1, source_target_pairs={{0,16},{4,20},{8,24},{12,28},{16,0},{20,4},{24,8},{28,12},{1,17},{... | collective-permute-start | bytes 786440 | tf_op jit(solution)/shard_map/ppermute | solution.py:394
  131.4 1.7 fusion.30
  133.1 21.4 %collective-permute-start.22 = (bf16[256,1024]{1,0:T(8,128)(2,1)}, bf16[256,1024]{1,0:T(8,128)(2,1)}, u32[]{:S(2)}, u32[]{:S(2)}) collective-permute-start(bf16[256,1024]{1,0:T(8,128)(2,1)} %get-tuple-element.128), channel_id=1, source_target_pairs={{0,8},{4,12},{8,16},{12,20},{16,24},{20,28},{1,9},{5,13},{9,17},{1... | collective-permute-start | bytes 1572872 | tf_op jit(solution)/shard_map/ppermute | solution.py:745
  155.1 6.6 %back.2 = bf16[2,128,2048]{2,1,0:T(8,128)(2,1)} custom-call(s32[4]{0:T(128)} %copy-done.13, bf16[2,128,4096]{2,1,0:T(8,128)(2,1)} %refs_0_.8, bf16[2,128,2048]{2,1,0:T(8,128)(2,1)} %copy-done.66, bf16[1,256,1024]{2,1,0:T(8,128)(2,1)} %get-tuple-element.117.refs_2_, bf16[1,256,1024]{2,1,0:T(8,128)(2,1)} %get-tuple-element.116.refs_3_, ...), custom_call_target="tpu_custom_call" | custom-call | flops 5500000256 | bytes 15000000 | tf_op jit(solution)/shard_map/back/pallas_call | solution.py:688
  161.6 0.8 collective-permute-done.22
  162.4 2.5 %fusion.18 = bf16[256,1024]{1,0:T(8,128)(2,1)} fusion(f32[2,256,1024]{2,1,0:T(8,128)} %copy-done.2, s32[]{:T(128)S(6)} %min.64, bf16[256,1024]{1,0:T(8,128)(2,1)} %collective-permute-done.22, f32[2,256,1024]{2,1,0:T(8,128)S(1)} %get-tuple-element.59.refs_4_, s32[]{:T(128)S(6)} %min.52, f32[1024]{0:T(1024)S(1)} %bitcast.160, f32[1024]{0:T(1024)S(1)} %bitcast.159, ...), kind=kLoop, calls=%fused_computation.33 | loop fusion | flops 2097152 | bytes 3153929 | tf_op jit(solution)/shard_map/jit(_where)/select_n | solution.py:744
  164.9 1.1 slice_bitcast_fusion.3
  166.5 10.3 %collective-permute-start.31 = (bf16[256,1024]{1,0:T(8,128)(2,1)}, bf16[256,1024]{1,0:T(8,128)(2,1)}, u32[]{:S(2)}, u32[]{:S(2)}) collective-permute-start(bf16[256,1024]{1,0:T(8,128)(2,1)} %fusion.18), channel_id=1, source_target_pairs={{0,8},{4,12},{8,16},{12,20},{16,24},{20,28},{1,9},{5,13},{9,17},{1... | collective-permute-start | bytes 1572872 | tf_op jit(solution)/shard_map/ppermute | solution.py:745
  176.8 3.4 %copy-done.15 = bf16[4096,1024]{1,0:T(8,128)(2,1)S(1)} copy-done((bf16[4096,1024]{1,0:T(8,128)(2,1)S(1)}, bf16[4096,1024]{1,0:T(8,128)(2,1)}, u32[]{:S(2)}) %copy-start.15) | copy-done | bytes 8388632
  180.2 5.3 %project.1 = f32[4,4,16,1024]{3,2,1,0:T(8,128)} custom-call(s32[4]{0:T(128)S(1)} %copy-done.14, bf16[64,2048]{1,0:T(8,128)(2,1)S(1)} %finish.1.refs_0_, bf16[64,2048]{1,0:T(8,128)(2,1)S(1)} %collective-permute-done.23.refs_1_, bf16[64,2048]{1,0:T(8,128)(2,1)S(1)} %collective-permute-done.24.refs_2_, bf16[64,2048]{1,0:T(8,128)(2,1)S(1)} %collective-permute-done.25.refs_3_, ...), custom_call_target="tpu_custom_call" | custom-call | flops 6600000000 | bytes 18000000 | tf_op jit(solution)/shard_map/project/pallas_call | solution.py:660
  185.5 3.9 %all-to-all-start = ((f32[4,4,16,1024]{3,2,1,0:T(8,128)}), f32[4,4,16,1024]{3,2,1,0:T(8,128)S(1)}, u32[]{:S(2)}, u32[]{:S(2)}) async-start(f32[4,4,16,1024]{3,2,1,0:T(8,128)} %project.1), calls=%async_computation | async-start | bytes 2097152 | tf_op jit(solution)/shard_map/all_to_all | solution.py:776
  189.3 2.2 %fusion.24 = (bf16[1,256,1024]{2,1,0:T(8,128)(2,1)}, bf16[1,256,1024]{2,1,0:T(8,128)(2,1)}) fusion(bf16[256,1024]{1,0:T(8,128)(2,1)} %collective-permute-done.31, bf16[256,1024]{1,0:T(8,128)(2,1)} %collective-permute-done.22, bf16[256,1024]{1,0:T(8,128)(2,1)S(1)} %copy-done.46, bf16[2,256,1024]{2,1,0:T(8,128)(2,1)S(1)} %copy-done.6, pred[]{:T(512)S(6)} %eq.78, ...), kind=kLoop, calls=%fused_computation.44 | loop fusion | flops 1572864 | bytes 4194307 | tf_op jit(solution)/shard_map/broadcast_in_dim | solution.py:713
  191.5 6.5 %back.3 = bf16[2,128,2048]{2,1,0:T(8,128)(2,1)} custom-call(s32[4]{0:T(128)} %copy-done.13, bf16[2,128,4096]{2,1,0:T(8,128)(2,1)} %refs_0_.8, bf16[2,128,2048]{2,1,0:T(8,128)(2,1)} %copy-done.66, bf16[1,256,1024]{2,1,0:T(8,128)(2,1)} %get-tuple-element.115.refs_2_, bf16[1,256,1024]{2,1,0:T(8,128)(2,1)} %get-tuple-element.114.refs_3_, ...), custom_call_target="tpu_custom_call" | custom-call | flops 5500000256 | bytes 15000000 | tf_op jit(solution)/shard_map/back/pallas_call | solution.py:688
  198.1 1.3 slice_bitcast_fusion.1
  199.5 3.4 %all-to-all-done = f32[4,4,16,1024]{3,2,1,0:T(8,128)S(1)} async-done(((f32[4,4,16,1024]{3,2,1,0:T(8,128)}), f32[4,4,16,1024]{3,2,1,0:T(8,128)S(1)}, u32[]{:S(2)}, u32[]{:S(2)}) %all-to-all-start) | async-done | bytes 1048608 | tf_op jit(solution)/shard_map/all_to_all | solution.py:776
  202.9 0.7 reduce_sum.9
  203.6 1.1 broadcast_select_fusion.3
  205.0 1.5 pad_maximum_fusion
  (225 shorter events, 9.3 us)
Async XLA Ops:
  0.6 12.7 %copy-start = (f32[4096]{0:T(1024)S(1)}, f32[4096]{0:T(1024)}, u32[]{:S(2)}) copy-start(f32[4096]{0:T(1024)} %param.33) | copy-start | bytes 49156
  0.7 10.5 %copy-start.11 = (f32[2,64,128]{2,1,0:T(8,128)S(1)}, f32[2,64,128]{2,1,0:T(8,128)}, u32[]{:S(2)}) copy-start(f32[2,64,128]{2,1,0:T(8,128)} %refs_4_.3) | copy-start | bytes 196612
  0.7 11.6 %copy-start.67 = (f32[64]{0:T(128)S(1)}, f32[64]{0:T(128)}, u32[]{:S(2)}) copy-start(f32[64]{0:T(128)} %param.26) | copy-start | bytes 772
  0.7 11.7 %copy-start.51 = (bf16[2,3,4096]{2,0,1:T(2,128)(2,1)S(1)}, bf16[2,3,4096]{2,0,1:T(2,128)(2,1)}, u32[]{:S(2)}) copy-start(bf16[2,3,4096]{2,0,1:T(2,128)(2,1)} %param.35) | copy-start | bytes 147460
  0.7 11.8 %copy-start.57 = (bf16[2,3,2,512]{3,2,1,0:T(2,128)(2,1)S(1)}, bf16[2,3,2,512]{3,2,1,0:T(2,128)(2,1)}, u32[]{:S(2)}) copy-start(bf16[2,3,2,512]{3,2,1,0:T(2,128)(2,1)} %param.36) | copy-start | bytes 36868
  0.7 11.8 %copy-start.64 = (f32[64]{0:T(128)S(1)}, f32[64]{0:T(128)}, u32[]{:S(2)}) copy-start(f32[64]{0:T(128)} %param.27) | copy-start | bytes 772
  0.7 12.5 %copy-start.65 = (f32[64]{0:T(128)S(1)}, f32[64]{0:T(128)}, u32[]{:S(2)}) copy-start(f32[64]{0:T(128)} %param.28) | copy-start | bytes 772
  0.7 12.7 %copy-start.61 = (s32[2]{0:T(128)S(1)}, s32[2]{0:T(128)}, u32[]{:S(2)}) copy-start(s32[2]{0:T(128)} %param.37) | copy-start | bytes 28
  0.8 12.9 %copy-start.55 = (f32[4,2,512]{2,1,0:T(2,128)S(1)}, f32[4,2,512]{2,1,0:T(2,128)}, u32[]{:S(2)}) copy-start(f32[4,2,512]{2,1,0:T(2,128)} %param.30) | copy-start | bytes 49156
  0.8 12.9 %copy-start.58 = (f32[2,512]{1,0:T(2,128)S(1)}, f32[2,512]{1,0:T(2,128)}, u32[]{:S(2)}) copy-start(f32[2,512]{1,0:T(2,128)} %param.32) | copy-start | bytes 12292
  3.2 11.7 %collective-permute-start = (bf16[2,128,2048]{2,1,0:T(8,128)(2,1)}, bf16[2,128,2048]{2,1,0:T(8,128)(2,1)S(1)}, u32[]{:S(2)}, u32[]{:S(2)}) collective-permute-start(bf16[2,128,2048]{2,1,0:T(8,128)(2,1)} %constant_dynamic-slice_fusion.26), channel_id=1, source_target_pairs={{0,4},{4,0},{8,12},{12,8},{16,20},{20,16},{24,28},{28,24},{1,5},{5... | collective-permute-start | bytes 3145736 | tf_op jit(solution)/shard_map/ppermute | solution.py:374
  4.5 11.4 %copy-start.21 = (f32[4,4096]{1,0:T(4,128)S(1)}, f32[4,4096]{1,0:T(4,128)}, u32[]{:S(2)}) copy-start(f32[4,4096]{1,0:T(4,128)} %refs_12_.1) | copy-start | bytes 196612
  4.6 11.3 %copy-start.23 = (f32[4096]{0:T(1024)S(1)}, f32[4096]{0:T(1024)}, u32[]{:S(2)}) copy-start(f32[4096]{0:T(1024)} %param.31) | copy-start | bytes 49156
  5.0 9.8 %collective-permute-start.3 = (bf16[2,3,2560]{2,1,0:T(4,128)(2,1)S(1)}, bf16[2,3,2560]{2,1,0:T(4,128)(2,1)S(1)}, u32[]{:S(2)}, u32[]{:S(2)}) collective-permute-start(bf16[2,3,2560]{2,1,0:T(4,128)(2,1)S(1)} %pad_maximum_fusion.3), channel_id=1, source_target_pairs={{4,12},{12,20},{20,28},{5,13},{13,21},{21,29},{6,14},{14,22},{22,3... | collective-permute-start | bytes 92168 | tf_op jit(solution)/shard_map/ppermute | solution.py:412
  5.7 9.1 %collective-permute-start.4 = (bf16[2,3,2560]{2,1,0:T(4,128)(2,1)S(1)}, bf16[2,3,2560]{2,1,0:T(4,128)(2,1)S(1)}, u32[]{:S(2)}, u32[]{:S(2)}) collective-permute-start(bf16[2,3,2560]{2,1,0:T(4,128)(2,1)S(1)} %pad_maximum_fusion.4), channel_id=1, source_target_pairs={{4,8},{12,16},{20,24},{5,9},{13,17},{21,25},{6,10},{14,18},{22,26}... | collective-permute-start | bytes 92168 | tf_op jit(solution)/shard_map/ppermute | solution.py:412
  6.4 8.5 %collective-permute-start.1 = (bf16[2,128,512]{2,1,0:T(8,128)(2,1)S(1)}, bf16[2,128,512]{2,1,0:T(8,128)(2,1)S(1)}, u32[]{:S(2)}, u32[]{:S(2)}) collective-permute-start(bf16[2,128,512]{2,1,0:T(8,128)(2,1)S(1)} %constant_dynamic-slice_fusion.25), channel_id=1, source_target_pairs={{0,4},{4,0},{8,12},{12,8},{16,20},{20,16},{24,28},{28,24},{1,5},{5... | collective-permute-start | bytes 786440 | tf_op jit(solution)/shard_map/ppermute | solution.py:374
  11.1 3.7 %collective-permute-start.2 = (f32[2,32,128]{2,1,0:T(8,128)S(1)}, f32[2,32,128]{2,1,0:T(8,128)S(1)}, u32[]{:S(2)}, u32[]{:S(2)}) collective-permute-start(f32[2,32,128]{2,1,0:T(8,128)S(1)} %constant_dynamic-slice_fusion.24), channel_id=1, source_target_pairs={{0,4},{4,0},{8,12},{12,8},{16,20},{20,16},{24,28},{28,24},{1,5},{5... | collective-permute-start | bytes 98312 | tf_op jit(solution)/shard_map/ppermute | solution.py:374
  13.4 105.9 %copy-start.12 = (f32[1,2048]{1,0:T(1,128)}, f32[1,2048]{1,0:T(1,128)S(1)}, u32[]{:S(2)}) copy-start(f32[1,2048]{1,0:T(1,128)S(1)} %fusion.38.refs_8_.refs_6_) | copy-start | bytes 24580
  13.5 105.8 %copy-start.13 = (s32[4]{0:T(128)}, s32[4]{0:T(128)S(1)}, u32[]{:S(2)}) copy-start(s32[4]{0:T(128)S(1)} %pad_add_fusion.sc) | copy-start | bytes 52
  18.7 16.8 %copy-start.62 = (s32[2]{0:T(128)S(1)}, s32[2]{0:T(128)}, u32[]{:S(2)}) copy-start(s32[2]{0:T(128)} %param.37) | copy-start | bytes 28
  18.7 16.8 %copy-start.63 = (pred[8]{0:T(512)(128)(4,1)S(1)}, pred[8]{0:T(512)(128)(4,1)}, u32[]{:S(2)}) copy-start(pred[8]{0:T(512)(128)(4,1)} %iota_compare_fusion.4) | copy-start | bytes 28
  18.7 16.9 %copy-start.60 = (s32[128]{0:T(128)S(1)}, s32[128]{0:T(128)}, u32[]{:S(2)}) copy-start(s32[128]{0:T(128)} %iota_add_fusion) | copy-start | bytes 1540
  18.7 17.0 %copy-start.42 = (bf16[32,8,2,512]{3,1,2,0:T(8,128)(2,1)S(1)}, bf16[32,8,2,512]{3,1,2,0:T(8,128)(2,1)}, u32[]{:S(2)}) copy-start(bf16[32,8,2,512]{3,1,2,0:T(8,128)(2,1)} %copy.39) | copy-start | bytes 1572868
  18.7 17.0 %copy-start.59 = (pred[2,2]{1,0:T(4,128)(4,1)S(1)}, pred[2,2]{1,0:T(4,128)(4,1)}, u32[]{:S(2)}) copy-start(pred[2,2]{1,0:T(4,128)(4,1)} %iota_compare_fusion.3) | copy-start | bytes 16
  31.5 26.0 %collective-permute-start.5 = (bf16[256,1024]{1,0:T(8,128)(2,1)}, bf16[256,1024]{1,0:T(8,128)(2,1)}, u32[]{:S(2)}, u32[]{:S(2)}) collective-permute-start(bf16[256,1024]{1,0:T(8,128)(2,1)} %fusion.17), channel_id=1, source_target_pairs={{0,8},{4,12},{8,16},{12,20},{16,24},{20,28},{1,9},{5,13},{9,17},{1... | collective-permute-start | bytes 1572872 | tf_op jit(solution)/shard_map/ppermute | solution.py:745
  38.3 17.2 %collective-permute-start.9 = (bf16[16,2560]{1,0:T(8,128)(2,1)}, bf16[16,2560]{1,0:T(8,128)(2,1)}, u32[]{:S(2)}, u32[]{:S(2)}) collective-permute-start(bf16[16,2560]{1,0:T(8,128)(2,1)} %pad_maximum_fusion.2), channel_id=1, source_target_pairs={{0,4},{4,0},{8,12},{12,8},{16,20},{20,16},{24,28},{28,24},{1,5},{5... | collective-permute-start | bytes 245768 | tf_op jit(solution)/shard_map/ppermute | solution.py:374
  39.4 29.4 %collective-permute-start.7 = (bf16[4,8,4608]{2,1,0:T(8,128)(2,1)S(1)}, bf16[4,8,4608]{2,1,0:T(8,128)(2,1)S(1)}, u32[]{:S(2)}, u32[]{:S(2)}) collective-permute-start(bf16[4,8,4608]{2,1,0:T(8,128)(2,1)S(1)} %pad_maximum_fusion.1), channel_id=1, source_target_pairs={{0,4},{4,0},{8,12},{12,8},{16,20},{20,16},{24,28},{28,24},{1,5},{5... | collective-permute-start | bytes 884744 | tf_op jit(solution)/shard_map/ppermute | solution.py:374
  41.3 24.9 %collective-permute-start.8 = (f32[5,8,128]{2,1,0:T(8,128)S(1)}, f32[5,8,128]{2,1,0:T(8,128)S(1)}, u32[]{:S(2)}, u32[]{:S(2)}) collective-permute-start(f32[5,8,128]{2,1,0:T(8,128)S(1)} %select_maximum_fusion.refs_3_), channel_id=1, source_target_pairs={{0,4},{4,0},{8,12},{12,8},{16,20},{20,16},{24,28},{28,24},{1,5},{5... | collective-permute-start | bytes 61448 | tf_op jit(solution)/shard_map/ppermute | solution.py:374
  46.1 14.8 %copy-start.54 = (f32[1,1,1024]{2,1,0:T(1,128)S(1)}, f32[1,1,1024]{2,1,0:T(1,128)}, u32[]{:S(2)}) copy-start(f32[1,1,1024]{2,1,0:T(1,128)} %get-tuple-element.134) | copy-start | bytes 12292
  46.1 16.0 %copy-start.32 = (f32[1,256,512]{2,1,0:T(8,128)S(1)}, f32[1,256,512]{2,1,0:T(8,128)}, u32[]{:S(2)}) copy-start(f32[1,256,512]{2,1,0:T(8,128)} %copy-done.31) | copy-start | bytes 1572868
  55.4 10.8 %copy-start.5 = (bf16[2,256,1024]{2,1,0:T(8,128)(2,1)}, bf16[2,256,1024]{2,1,0:T(8,128)(2,1)S(1)}, u32[]{:S(2)}) copy-start(bf16[2,256,1024]{2,1,0:T(8,128)(2,1)S(1)} %get-tuple-element.110) | copy-start | bytes 3145732
  55.4 52.7 %copy-start.30 = (f32[1,256,512]{2,1,0:T(8,128)}, f32[1,256,512]{2,1,0:T(8,128)S(1)}, u32[]{:S(2)}) copy-start(f32[1,256,512]{2,1,0:T(8,128)S(1)} %get-tuple-element.86.bc.refs_4_) | copy-start | bytes 1572868
  55.4 52.7 %copy-start.33 = (f32[1,256,128]{2,1,0:T(8,128)}, f32[1,256,128]{2,1,0:T(8,128)S(1)}, u32[]{:S(2)}) copy-start(f32[1,256,128]{2,1,0:T(8,128)S(1)} %get-tuple-element.112.refs_10_.pack.refs_5_) | copy-start | bytes 393220
  55.4 75.9 %copy-start.2 = (f32[2,256,1024]{2,1,0:T(8,128)}, f32[2,256,1024]{2,1,0:T(8,128)S(1)}, u32[]{:S(2)}) copy-start(f32[2,256,1024]{2,1,0:T(8,128)S(1)} %get-tuple-element.61.refs_5_) | copy-start | bytes 6291460
  57.0 11.8 %collective-permute-start.10 = (bf16[16,2560]{1,0:T(8,128)(2,1)S(1)}, bf16[16,2560]{1,0:T(8,128)(2,1)S(1)}, u32[]{:S(2)}, u32[]{:S(2)}) collective-permute-start(bf16[16,2560]{1,0:T(8,128)(2,1)S(1)} %maximum_add_fusion.refs_5_), channel_id=1, source_target_pairs={{0,8},{4,12},{8,16},{12,20},{16,24},{20,28},{24,0},{28,4},{1,9},{5... | collective-permute-start | bytes 245768 | tf_op jit(solution)/shard_map/ppermute | solution.py:394
  57.5 11.3 %collective-permute-start.11 = (bf16[16,2560]{1,0:T(8,128)(2,1)S(1)}, bf16[16,2560]{1,0:T(8,128)(2,1)S(1)}, u32[]{:S(2)}, u32[]{:S(2)}) collective-permute-start(bf16[16,2560]{1,0:T(8,128)(2,1)S(1)} %maximum_add_fusion.refs_5_), channel_id=1, source_target_pairs={{0,16},{4,20},{8,24},{12,28},{16,0},{20,4},{24,8},{28,12},{1,17},{... | collective-permute-start | bytes 245768 | tf_op jit(solution)/shard_map/ppermute | solution.py:394
  57.5 11.3 %collective-permute-start.12 = (bf16[16,2560]{1,0:T(8,128)(2,1)S(1)}, bf16[16,2560]{1,0:T(8,128)(2,1)S(1)}, u32[]{:S(2)}, u32[]{:S(2)}) collective-permute-start(bf16[16,2560]{1,0:T(8,128)(2,1)S(1)} %maximum_add_fusion.refs_5_), channel_id=1, source_target_pairs={{0,24},{4,28},{8,0},{12,4},{16,8},{20,12},{24,16},{28,20},{1,25},{... | collective-permute-start | bytes 245768 | tf_op jit(solution)/shard_map/ppermute | solution.py:394
  66.2 14.8 %collective-permute-start.6 = (bf16[256,1024]{1,0:T(8,128)(2,1)S(1)}, bf16[256,1024]{1,0:T(8,128)(2,1)S(1)}, u32[]{:S(2)}, u32[]{:S(2)}) collective-permute-start(bf16[256,1024]{1,0:T(8,128)(2,1)S(1)} %fusion.16), channel_id=1, source_target_pairs={{0,8},{4,12},{8,16},{12,20},{16,24},{20,28},{1,9},{5,13},{9,17},{1... | collective-permute-start | bytes 1572872 | tf_op jit(solution)/shard_map/ppermute | solution.py:745
  71.0 14.9 %collective-permute-start.14 = (f32[72,384]{1,0:T(8,128)S(1)}, f32[72,384]{1,0:T(8,128)S(1)}, u32[]{:S(2)}, u32[]{:S(2)}) collective-permute-start(f32[72,384]{1,0:T(8,128)S(1)} %get-tuple-element.82.refs_0_), channel_id=1, source_target_pairs={{0,8},{4,12},{8,16},{12,20},{16,24},{20,28},{24,0},{28,4},{1,9},{5... | collective-permute-start | bytes 331784 | tf_op jit(solution)/shard_map/ppermute | solution.py:394
  73.0 12.9 %collective-permute-start.15 = (f32[72,384]{1,0:T(8,128)S(1)}, f32[72,384]{1,0:T(8,128)S(1)}, u32[]{:S(2)}, u32[]{:S(2)}) collective-permute-start(f32[72,384]{1,0:T(8,128)S(1)} %get-tuple-element.82.refs_0_), channel_id=1, source_target_pairs={{0,16},{4,20},{8,24},{12,28},{16,0},{20,4},{24,8},{28,12},{1,17},{... | collective-permute-start | bytes 331784 | tf_op jit(solution)/shard_map/ppermute | solution.py:394
  73.0 15.2 %collective-permute-start.16 = (f32[72,384]{1,0:T(8,128)S(1)}, f32[72,384]{1,0:T(8,128)S(1)}, u32[]{:S(2)}, u32[]{:S(2)}) collective-permute-start(f32[72,384]{1,0:T(8,128)S(1)} %get-tuple-element.82.refs_0_), channel_id=1, source_target_pairs={{0,24},{4,28},{8,0},{12,4},{16,8},{20,12},{24,16},{28,20},{1,25},{... | collective-permute-start | bytes 331784 | tf_op jit(solution)/shard_map/ppermute | solution.py:394
  81.3 18.2 %copy-start.48 = (bf16[2,128,4096]{2,1,0:T(8,128)(2,1)S(1)}, bf16[2,128,4096]{2,1,0:T(8,128)(2,1)}, u32[]{:S(2)}) copy-start(bf16[2,128,4096]{2,1,0:T(8,128)(2,1)} %refs_0_.8) | copy-start | bytes 6291460
  81.4 22.5 %collective-permute-start.13 = (bf16[256,1024]{1,0:T(8,128)(2,1)S(1)}, bf16[256,1024]{1,0:T(8,128)(2,1)S(1)}, u32[]{:S(2)}, u32[]{:S(2)}) collective-permute-start(bf16[256,1024]{1,0:T(8,128)(2,1)S(1)} %fusion.21), channel_id=1, source_target_pairs={{0,8},{4,12},{8,16},{12,20},{16,24},{20,28},{1,9},{5,13},{9,17},{1... | collective-permute-start | bytes 1572872 | tf_op jit(solution)/shard_map/ppermute | solution.py:745
  91.7 27.5 %collective-permute-start.20 = (bf16[64,2048]{1,0:T(8,128)(2,1)S(1)}, bf16[64,2048]{1,0:T(8,128)(2,1)S(1)}, u32[]{:S(2)}, u32[]{:S(2)}) collective-permute-start(bf16[64,2048]{1,0:T(8,128)(2,1)S(1)} %get-tuple-element.83), channel_id=1, source_target_pairs={{0,8},{4,12},{8,16},{12,20},{16,24},{20,28},{24,0},{28,4},{1,9},{5... | collective-permute-start | bytes 786440 | tf_op jit(solution)/shard_map/ppermute | solution.py:394
  96.2 16.1 %collective-permute-start.18 = (bf16[64,2048]{1,0:T(8,128)(2,1)S(1)}, bf16[64,2048]{1,0:T(8,128)(2,1)S(1)}, u32[]{:S(2)}, u32[]{:S(2)}) collective-permute-start(bf16[64,2048]{1,0:T(8,128)(2,1)S(1)} %get-tuple-element.94), channel_id=1, source_target_pairs={{0,24},{4,28},{8,0},{12,4},{16,8},{20,12},{24,16},{28,20},{1,25},{... | collective-permute-start | bytes 786440 | tf_op jit(solution)/shard_map/ppermute | solution.py:394
  99.0 20.2 %collective-permute-start.19 = (bf16[64,2048]{1,0:T(8,128)(2,1)S(1)}, bf16[64,2048]{1,0:T(8,128)(2,1)S(1)}, u32[]{:S(2)}, u32[]{:S(2)}) collective-permute-start(bf16[64,2048]{1,0:T(8,128)(2,1)S(1)} %get-tuple-element.95), channel_id=1, source_target_pairs={{0,16},{4,20},{8,24},{12,28},{16,0},{20,4},{24,8},{28,12},{1,17},{... | collective-permute-start | bytes 786440 | tf_op jit(solution)/shard_map/ppermute | solution.py:394
  99.7 31.7 %collective-permute-start.21 = (bf16[2,128,2048]{2,1,0:T(8,128)(2,1)S(1)}, bf16[2,128,2048]{2,1,0:T(8,128)(2,1)S(1)}, u32[]{:S(2)}, u32[]{:S(2)}) collective-permute-start(bf16[2,128,2048]{2,1,0:T(8,128)(2,1)S(1)} %constant_dynamic-slice_fusion.2), channel_id=1, source_target_pairs={{0,4},{4,0},{8,12},{12,8},{16,20},{20,16},{24,28},{28,24},{1,5},{5... | collective-permute-start | bytes 3145736 | tf_op jit(solution)/shard_map/ppermute | solution.py:374
  103.8 27.6 %copy-start.40 = (bf16[256,1024]{1,0:T(8,128)(2,1)}, bf16[256,1024]{1,0:T(8,128)(2,1)S(1)}, u32[]{:S(2)}) copy-start(bf16[256,1024]{1,0:T(8,128)(2,1)S(1)} %collective-permute-done.13) | copy-start | bytes 1572868
  104.1 27.2 %collective-permute-start.17 = (bf16[256,1024]{1,0:T(8,128)(2,1)S(1)}, bf16[256,1024]{1,0:T(8,128)(2,1)S(1)}, u32[]{:S(2)}, u32[]{:S(2)}) collective-permute-start(bf16[256,1024]{1,0:T(8,128)(2,1)S(1)} %fusion.20), channel_id=1, source_target_pairs={{0,8},{4,12},{8,16},{12,20},{16,24},{20,28},{1,9},{5,13},{9,17},{1... | collective-permute-start | bytes 1572872 | tf_op jit(solution)/shard_map/ppermute | solution.py:745
  119.3 12.1 %copy-start.8 = (bf16[2,256,1024]{2,1,0:T(8,128)(2,1)S(1)}, bf16[2,256,1024]{2,1,0:T(8,128)(2,1)}, u32[]{:S(2)}) copy-start(bf16[2,256,1024]{2,1,0:T(8,128)(2,1)} %copy-done.7) | copy-start | bytes 3145732
  119.3 12.1 %copy-start.56 = (f32[1,1,1024]{2,1,0:T(1,128)S(1)}, f32[1,1,1024]{2,1,0:T(1,128)}, u32[]{:S(2)}) copy-start(f32[1,1,1024]{2,1,0:T(1,128)} %get-tuple-element.137) | copy-start | bytes 12292
  120.9 33.6 %collective-permute-start.23 = (bf16[64,2048]{1,0:T(8,128)(2,1)S(1)}, bf16[64,2048]{1,0:T(8,128)(2,1)S(1)}, u32[]{:S(2)}, u32[]{:S(2)}) collective-permute-start(bf16[64,2048]{1,0:T(8,128)(2,1)S(1)} %finish.1.refs_0_), channel_id=1, source_target_pairs={{0,8},{4,12},{8,16},{12,20},{16,24},{20,28},{24,0},{28,4},{1,9},{5... | collective-permute-start | bytes 786440 | tf_op jit(solution)/shard_map/ppermute | solution.py:394
  128.0 26.5 %collective-permute-start.24 = (bf16[64,2048]{1,0:T(8,128)(2,1)S(1)}, bf16[64,2048]{1,0:T(8,128)(2,1)S(1)}, u32[]{:S(2)}, u32[]{:S(2)}) collective-permute-start(bf16[64,2048]{1,0:T(8,128)(2,1)S(1)} %finish.1.refs_0_), channel_id=1, source_target_pairs={{0,16},{4,20},{8,24},{12,28},{16,0},{20,4},{24,8},{28,12},{1,17},{... | collective-permute-start | bytes 786440 | tf_op jit(solution)/shard_map/ppermute | solution.py:394
  131.4 23.6 %collective-permute-start.25 = (bf16[64,2048]{1,0:T(8,128)(2,1)S(1)}, bf16[64,2048]{1,0:T(8,128)(2,1)S(1)}, u32[]{:S(2)}, u32[]{:S(2)}) collective-permute-start(bf16[64,2048]{1,0:T(8,128)(2,1)S(1)} %finish.1.refs_0_), channel_id=1, source_target_pairs={{0,24},{4,28},{8,0},{12,4},{16,8},{20,12},{24,16},{28,20},{1,25},{... | collective-permute-start | bytes 786440 | tf_op jit(solution)/shard_map/ppermute | solution.py:394
  133.1 29.3 %collective-permute-start.22 = (bf16[256,1024]{1,0:T(8,128)(2,1)}, bf16[256,1024]{1,0:T(8,128)(2,1)}, u32[]{:S(2)}, u32[]{:S(2)}) collective-permute-start(bf16[256,1024]{1,0:T(8,128)(2,1)} %get-tuple-element.128), channel_id=1, source_target_pairs={{0,8},{4,12},{8,16},{12,20},{16,24},{20,28},{1,9},{5,13},{9,17},{1... | collective-permute-start | bytes 1572872 | tf_op jit(solution)/shard_map/ppermute | solution.py:745
  154.5 12.0 %collective-permute-start.27 = (bf16[64,2048]{1,0:T(8,128)(2,1)S(1)}, bf16[64,2048]{1,0:T(8,128)(2,1)S(1)}, u32[]{:S(2)}, u32[]{:S(2)}) collective-permute-start(bf16[64,2048]{1,0:T(8,128)(2,1)S(1)} %collective-permute-done.23.refs_1_), channel_id=1, source_target_pairs={{0,4},{4,0},{8,12},{12,8},{16,20},{20,16},{24,28},{28,24},{1,5},{5... | collective-permute-start | bytes 786440 | tf_op jit(solution)/shard_map/ppermute | solution.py:374
  154.5 22.3 %collective-permute-start.28 = (bf16[64,2048]{1,0:T(8,128)(2,1)S(1)}, bf16[64,2048]{1,0:T(8,128)(2,1)S(1)}, u32[]{:S(2)}, u32[]{:S(2)}) collective-permute-start(bf16[64,2048]{1,0:T(8,128)(2,1)S(1)} %collective-permute-done.24.refs_2_), channel_id=1, source_target_pairs={{0,4},{4,0},{8,12},{12,8},{16,20},{20,16},{24,28},{28,24},{1,5},{5... | collective-permute-start | bytes 786440 | tf_op jit(solution)/shard_map/ppermute | solution.py:374
  155.0 21.8 %collective-permute-start.29 = (bf16[64,2048]{1,0:T(8,128)(2,1)S(1)}, bf16[64,2048]{1,0:T(8,128)(2,1)S(1)}, u32[]{:S(2)}, u32[]{:S(2)}) collective-permute-start(bf16[64,2048]{1,0:T(8,128)(2,1)S(1)} %collective-permute-done.25.refs_3_), channel_id=1, source_target_pairs={{0,4},{4,0},{8,12},{12,8},{16,20},{20,16},{24,28},{28,24},{1,5},{5... | collective-permute-start | bytes 786440 | tf_op jit(solution)/shard_map/ppermute | solution.py:374
  162.4 14.4 %copy-start.14 = (s32[4]{0:T(128)S(1)}, s32[4]{0:T(128)}, u32[]{:S(2)}) copy-start(s32[4]{0:T(128)} %copy-done.13) | copy-start | bytes 52
  164.9 11.9 %collective-permute-start.26 = (bf16[64,2048]{1,0:T(8,128)(2,1)S(1)}, bf16[64,2048]{1,0:T(8,128)(2,1)S(1)}, u32[]{:S(2)}, u32[]{:S(2)}) collective-permute-start(bf16[64,2048]{1,0:T(8,128)(2,1)S(1)} %finish.1.refs_0_), channel_id=1, source_target_pairs={{0,4},{4,0},{8,12},{12,8},{16,20},{20,16},{24,28},{28,24},{1,5},{5... | collective-permute-start | bytes 786440 | tf_op jit(solution)/shard_map/ppermute | solution.py:374
  166.0 37.7 %collective-permute-start.30 = (bf16[128,2048]{1,0:T(8,128)(2,1)}, bf16[128,2048]{1,0:T(8,128)(2,1)}, u32[]{:S(2)}, u32[]{:S(2)}) collective-permute-start(bf16[128,2048]{1,0:T(8,128)(2,1)} %get-tuple-element.123), channel_id=1, source_target_pairs={{0,4},{4,0},{8,12},{12,8},{16,20},{20,16},{24,28},{28,24},{1,5},{5... | collective-permute-start | bytes 1572872 | tf_op jit(solution)/shard_map/ppermute | solution.py:374
  166.5 22.8 %collective-permute-start.31 = (bf16[256,1024]{1,0:T(8,128)(2,1)}, bf16[256,1024]{1,0:T(8,128)(2,1)}, u32[]{:S(2)}, u32[]{:S(2)}) collective-permute-start(bf16[256,1024]{1,0:T(8,128)(2,1)} %fusion.18), channel_id=1, source_target_pairs={{0,8},{4,12},{8,16},{12,20},{16,24},{20,28},{1,9},{5,13},{9,17},{1... | collective-permute-start | bytes 1572872 | tf_op jit(solution)/shard_map/ppermute | solution.py:745
  185.5 17.4 %all-to-all-start = ((f32[4,4,16,1024]{3,2,1,0:T(8,128)}), f32[4,4,16,1024]{3,2,1,0:T(8,128)S(1)}, u32[]{:S(2)}, u32[]{:S(2)}) async-start(f32[4,4,16,1024]{3,2,1,0:T(8,128)} %project.1), calls=%async_computation | async-start | bytes 2097152 | tf_op jit(solution)/shard_map/all_to_all | solution.py:776
  199.4 5.4 %collective-permute-start.32 = (bf16[128,2048]{1,0:T(8,128)(2,1)S(1)}, bf16[128,2048]{1,0:T(8,128)(2,1)S(1)}, u32[]{:S(2)}, u32[]{:S(2)}) collective-permute-start(bf16[128,2048]{1,0:T(8,128)(2,1)S(1)} %get-tuple-element.127), channel_id=1, source_target_pairs={{0,4},{4,0},{8,12},{12,8},{16,20},{20,16},{24,28},{28,24},{1,5},{5... | collective-permute-start | bytes 1572872 | tf_op jit(solution)/shard_map/ppermute | solution.py:374
  (38 other events, 181.0 us)

commit v2 on v1

--- a/solution.py
+++ b/solution.py
@@ -41,10 +41,21 @@
     return high, (a - high.astype(f32)).astype(bf16)
 
 
+def three_pass(a, b):
+    a_hi, a_lo = halves(a)
+    b_hi, b_lo = halves(b)
+    return one_pass(a_hi, b_hi) + (one_pass(a_lo, b_hi) + one_pass(a_hi, b_lo))
+
+
+def spread_out(a, picks):
+    high, low = halves(a)
+    return one_pass(high, picks) + one_pass(low, picks)
+
+
 def to_channels(columns, hd, first):
     row = lax.broadcasted_iota(jnp.int32, (lanes, columns), 0)
     col = lax.broadcasted_iota(jnp.int32, (lanes, columns), 1)
-    return (row == col // hd + first).astype(f32)
+    return (row == col // hd + first).astype(bf16)
 
 
 def joined(refs, c, axis=0):
@@ -98,9 +109,9 @@
     act = convolved(xs, rim_x[0], joined(x_refs, c).astype(f32), cx, bx)
     act_o[0] = act
     first = half * (bw // hd)
-    weighted = act * exact(pack_o[0], to_channels(bw, hd, first))
-    own = exact(bt[...], weighted)
-    decay = exact(pack_o[0, rows - 8 :, :], to_channels(bw, hd, first + heads))[7:8]
+    weighted = act * spread_out(pack_o[0], to_channels(bw, hd, first))
+    own = three_pass(bt[...], weighted)
+    decay = spread_out(pack_o[0, rows - 8 :, :], to_channels(bw, hd, first + heads))[7:8]
     dec_o[0] = jnp.broadcast_to(decay, (8, bw))
 
     @pl.when(u == 0)
@@ -151,7 +162,8 @@
 
 def back_kernel(per, hd, heads, sc, *refs):
     g_refs, refs = refs[:per], refs[per:]
-    *rest, out_o, mixed = refs
+    outs, mixed = refs[-1 - per : -1], refs[-1]
+    rest = refs[: -1 - per]
     parts = (len(rest) - 3) // 2
     entry, (bc, pack, gain), local = rest[:parts], rest[parts : parts + 3], rest[parts + 3 :]
     token_block = pl.program_id(0)
@@ -165,14 +177,25 @@
     for k in range(parts):
         at = slice(k * bw, (k + 1) * bw)
         seen = one_pass(c_hi, entry[k][0]) + one_pass(c_lo, entry[k][0])
-        grow = exact(pack[0], to_channels(bw, hd, heads + k * (bw // hd)))
+        grow = spread_out(pack[0], to_channels(bw, hd, heads + k * (bw // hd)))
         y = local[k][0] + grow * seen
         v = y * silu(gate[:, at].astype(f32))
         mixed[:, at] = v
         square = jnp.sum(v * v, axis=1, keepdims=True)
         total = square if total is None else total + square
     scale = lax.rsqrt(total / (parts * bw) + epsilon)
-    out_o[0] = (mixed[...] * scale * gain[...]).astype(bf16)
+    out = (mixed[...] * scale * gain[...]).astype(bf16)
+    if per == 1:
+        outs[0][...] = out
+        return
+
+    @pl.when(token_block == c)
+    def _():
+        outs[0][...] = out
+
+    @pl.when(token_block != c)
+    def _():
+        outs[1][...] = out
 
 
 def rows_of(refs, i, at, c):
@@ -234,7 +257,7 @@
         for j in range(i + 1):
             both = jnp.sum(read * mix[j][:, :ns], axis=1, keepdims=True)
             coef.append(both * (jnp.exp(upto[i] - upto[j]) * step[j]))
-    wide = exact(jnp.concatenate(coef, axis=0), to_channels(gwidth, hd, c * heads))
+    wide = spread_out(jnp.concatenate(coef, axis=0), to_channels(gwidth, hd, c * heads))
     at = 8
     for i in range(steps):
         y = wide[0:1] * xd[i]
@@ -248,16 +271,17 @@
     )
 
 
-def read_kernel(hd, heads, m, sc, *refs):
-    blocks, own, outs = refs[:m], refs[m:-m], refs[-m:]
+def read_kernel(hd, heads, order, sc, *refs):
+    m = len(order)
+    blocks, own, outs = refs[:m], refs[m:-2], refs[-2:]
     half = pl.program_id(0)
     _, ns, bw = own[0].shape
     u = sc[1]
     rows = blocks[0].shape[0] - 8
     after = jnp.zeros((8, lanes), f32)
-    for k in range(1, m):
-        after = after + jnp.where(k > u, blocks[k][rows:, ns:], 0.0)
-    spread = exact(jnp.exp(after), to_channels(bw, hd, 2 * heads + half * (bw // hd)))
+    for k, block in zip(order[1:], blocks[1:]):
+        after = after + jnp.where((u ^ k) > u, block[rows:, ns:], 0.0)
+    spread = spread_out(jnp.exp(after), to_channels(bw, hd, 2 * heads + half * (bw // hd)))
     asked = jnp.concatenate([b[:rows, :ns] for b in blocks], axis=0)
     prompt = jnp.concatenate([b[:rows, ns : ns + 1] for b in blocks], axis=0)
     total = None
@@ -266,11 +290,12 @@
         s_hi, s_lo = halves(own[s][0] * spread[s : s + 1])
         got = one_pass(c_hi, s_hi) + (one_pass(c_lo, s_hi) + one_pass(c_hi, s_lo))
         total = got if total is None else total + got
-    for k in range(m):
-        outs[k][...] = total[k * rows : (k + 1) * rows].astype(bf16)
-
-
-def finish_kernel(per, hd, heads, m, sc, *refs):
+    outs[0][...] = total[: m // 2 * rows].astype(bf16)
+    outs[1][...] = total[m // 2 * rows :].astype(bf16)
+
+
+def finish_kernel(per, hd, heads, sc, *refs):
+    m = 2
     sums, local, grow, z_ref, refs = refs[:m], refs[m], refs[m + 1], refs[m + 2], refs[m + 3 :]
     *other, gain, out_o = refs
     c = sc[0]
@@ -279,7 +304,7 @@
     total = sums[0][...].astype(f32)
     for r in sums[1:]:
         total = total + r[...].astype(f32)
-    y = exact(grow[...], to_channels(gwidth, hd, c * heads)) * total + local[...]
+    y = spread_out(grow[...], to_channels(gwidth, hd, c * heads)) * total + local[...]
     at = (slice(None), slice(other[0].shape[2] - gwidth, None) if other else None)
     gate = jnp.concatenate([rows_of([z_ref, *other], i, at, c) for i in range(steps)], axis=0)
     v = y * silu(gate)
@@ -287,7 +312,8 @@
     out_o[...] = (v * scale * gain[...]).astype(bf16)
 
 
-def project_kernel(per, m, sc, *refs):
+def project_kernel(per, order, sc, *refs):
+    m = len(order)
     mine, other, w, out_o = refs[:m], refs[m:-2], refs[-2], refs[-1]
     c, u = sc[0], sc[1]
     tp, steps, rows_tp, cols = out_o.shape
@@ -301,11 +327,11 @@
         total = one_pass(a, w[...])
     rows = a.shape[0] // (m * steps)
     each = m // tp
-    for k in range(m):
-        v = lax.rem(u - k + m, m)
+    for place, k in enumerate(order):
+        v = u ^ k
         at = pl.ds(pl.multiple_of(lax.rem(v, each) * rows, rows), rows)
         for i in range(steps):
-            first = (k * steps + i) * rows
+            first = (place * steps + i) * rows
             out_o[v // each, i, at, :] = total[first : first + rows]
 
 
@@ -390,8 +416,15 @@
         other = swap(lax.dynamic_index_in_dim(arr, 1 - c, gaxis, keepdims=False))
         return in_order(mine(arr, gaxis), other, taxis)
 
-    def shift(arr, k):
-        return lax.ppermute(arr, "ctx", [(i, (i + k * per) % n) for i in range(n)])
+    def trade(arr, k):
+        return lax.ppermute(arr, "ctx", [(i, (i // per ^ k) * per + i % per) for i in range(n)])
+
+    assert m & (m - 1) == 0
+    bits = [1 << b for b in range(m.bit_length() - 1)]
+    order = [0]
+    for b in reversed(bits):
+        order = order + [k | b for k in order]
+    order = sorted(order, key=lambda k: [k >> b & 1 for b in range(len(bits))])
 
     bc_flat = proj_bc.reshape(prompts, tokens, groups * pair)
     x_other = bc_other = None
@@ -411,6 +444,32 @@
         )
         got = lax.ppermute(send, "ctx", pairs)
         rim = jnp.where(c == g, got, rim)
+    lengths_late = tied(x_send, lengths)[1] if per == 2 else lengths
+    want = jnp.arange(8, dtype=jnp.int32)
+    target = lengths_late[:, None] - (taps - 1) + want
+    target = jnp.where(want < taps - 1, target, -1)
+    places = device * tokens + jnp.arange(tokens, dtype=jnp.int32)
+    hit = places[None, None, :] == target[:, :, None]
+    same = jnp.arange(prompts)[:, None] == jnp.arange(prompts)[None, :]
+    picker = (hit[:, :, None, :] & same[:, None, :, None]).astype(bf16)
+    picker = picker.reshape(prompts * 8, prompts * tokens)
+    tail_x = jnp.dot(picker, inner_x.reshape(-1, width), preferred_element_type=f32).astype(bf16)
+    tail_bc = jnp.dot(
+        picker, bc_flat.reshape(-1, groups * pair), preferred_element_type=f32
+    ).astype(bf16)
+
+    def tail_of(g):
+        return jnp.concatenate(
+            [
+                lax.dynamic_slice_in_dim(tail_x, g * gwidth, gwidth, 1),
+                lax.dynamic_slice_in_dim(tail_bc, g * pair, pair, 1),
+            ],
+            axis=1,
+        )
+
+    tails = tail_of(c)
+    if per == 2:
+        tails = tails + swap(tail_of(1 - c))
     dt_in = [dt_raw]
     if per == 2:
         given = lax.dynamic_slice_in_dim(dt_raw, (1 - c) * heads, heads, 1)
@@ -520,35 +579,11 @@
 
     fronts = [list(front(0, dt_in))]
     after_front = fronts[0][5]
-    _, lengths_late = tied(after_front, lengths)
     _, dec_x = tied(after_front, dec_x)
     _, dec_bc = tied(after_front, dec_bc)
     _, dec_z = tied(after_front, dec_z)
     _, dec_dt = tied(after_front, dec_dt)
     _, row_prompt = tied(after_front, row_prompt)
-    want = jnp.arange(8, dtype=jnp.int32)
-    target = lengths_late[:, None] - (taps - 1) + want
-    target = jnp.where(want < taps - 1, target, -1)
-    places = device * tokens + jnp.arange(tokens, dtype=jnp.int32)
-    hit = places[None, None, :] == target[:, :, None]
-    same = jnp.arange(prompts)[:, None] == jnp.arange(prompts)[None, :]
-    picker = (hit[:, :, None, :] & same[:, None, :, None]).astype(bf16)
-    picker = picker.reshape(prompts * 8, prompts * tokens)
-    tail_x = jnp.dot(picker, inner_x.reshape(-1, width), preferred_element_type=f32).astype(bf16)
-    tail_bc = jnp.dot(
-        picker, bc_flat.reshape(-1, groups * pair), preferred_element_type=f32
-    ).astype(bf16)
-
-    def tail_of(g):
-        return jnp.concatenate(
-            [
-                lax.dynamic_slice_in_dim(tail_x, g * gwidth, gwidth, 1),
-                lax.dynamic_slice_in_dim(tail_bc, g * pair, pair, 1),
-            ],
-            axis=1,
-        )
-
-    tails = tail_of(c)
     dec_bc = dec_bc.reshape(steps, batch, groups * pair)
     small = jnp.concatenate(
         [
@@ -560,7 +595,6 @@
     small = [small]
     dec_other = []
     if per == 2:
-        tails = tails + swap(tail_of(1 - c))
         small.append(swap(small[0]))
         dec_other = [
             swap(
@@ -574,7 +608,8 @@
                 )
             )
         ]
-    tails = [tails] + [shift(tails, k) for k in range(1, m)]
+    _, tails = tied(after_front, tails)
+    tails = [tails] + [trade(tails, k) for k in range(1, m)]
     par = jnp.pad(
         jnp.stack([jnp.exp(a_log), dt_bias, d_skip]), ((0, 5), (0, lanes - groups * heads))
     )
@@ -623,15 +658,15 @@
     def read(blocks, first):
         _, blocks[0] = tied(first, blocks[0])
         return pl.pallas_call(
-            functools.partial(read_kernel, hd, heads, m),
+            functools.partial(read_kernel, hd, heads, order),
             grid_spec=pltpu.PrefetchScalarGridSpec(
                 num_scalar_prefetch=1,
                 grid=(per_prompt,),
                 in_specs=[full_spec(b) for b in blocks]
                 + [spec((1, ns, bw), lambda k, sc: (k, 0, 0))] * prompts,
-                out_specs=[spec((asked_rows, bw), lambda k, sc: (0, k))] * m,
+                out_specs=[spec((m // 2 * asked_rows, bw), lambda k, sc: (0, k))] * 2,
             ),
-            out_shape=[jax.ShapeDtypeStruct((asked_rows, gwidth), bf16)] * m,
+            out_shape=[jax.ShapeDtypeStruct((m // 2 * asked_rows, gwidth), bf16)] * 2,
             compiler_params=params(),
             cost_estimate=cost(4),
             name="read",
@@ -639,7 +674,7 @@
 
     def finish(sums, local, grow):
         return pl.pallas_call(
-            functools.partial(finish_kernel, per, hd, heads, m),
+            functools.partial(finish_kernel, per, hd, heads),
             grid_spec=pltpu.PrefetchScalarGridSpec(
                 num_scalar_prefetch=1,
                 grid=(1,),
@@ -658,7 +693,7 @@
         others = [swap(b) for b in blocks] if per == 2 else []
         cb = min(256, cols)
         return pl.pallas_call(
-            functools.partial(project_kernel, per, m),
+            functools.partial(project_kernel, per, order),
             grid_spec=pltpu.PrefetchScalarGridSpec(
                 num_scalar_prefetch=1,
                 grid=(cols // cb,),
@@ -667,7 +702,7 @@
                 out_specs=spec((tp, steps, m * rows_u // tp, cb), lambda i, sc: (0, 0, 0, i)),
             ),
             out_shape=jax.ShapeDtypeStruct((tp, steps, m * rows_u // tp, cols), f32),
-            compiler_params=params(),
+            compiler_params=params(60 * 1024 * 1024),
             cost_estimate=cost(6),
             name="project",
         )(sc, *blocks, *others, w_out)
@@ -698,12 +733,10 @@
                     spec((1, gwidth), lambda j, sc: (0, 0)),
                 ]
                 + [spec((1, tokens, bw), lambda j, sc: (0, j, 0))] * per_prompt,
-                out_specs=spec(
-                    (1, tokens, gwidth), lambda j, sc: (jnp.where(j == sc[0], 0, 1), 0, 0)
-                ),
+                out_specs=[spec((tokens, gwidth), lambda j, sc: (0, 0))] * per,
                 scratch_shapes=[pltpu.VMEM((tokens, gwidth), f32)],
             ),
-            out_shape=jax.ShapeDtypeStruct((per, tokens, gwidth), bf16),
+            out_shape=[jax.ShapeDtypeStruct((tokens, gwidth), bf16)] * per,
             compiler_params=params(60 * 1024 * 1024),
             cost_estimate=cost(5),
             name="back",
@@ -749,25 +782,32 @@
                 fronts.append(list(front(s, dt_in)))
             moved, _ = tied(moved, fronts[-1][5])
         if t == 1:
-            moved = locals_after(leave, 1, moved)
-            local, grow, payload = window(y_local[-1])
-            blocks = [payload] + [shift(payload, k) for k in range(1, m)]
+            local, grow, payload = window(leave)
+            blocks = [payload] + [trade(payload, k) for k in order[1:]]
             moved = locals_after(payload, 1, moved)
+            keep, give = read(blocks, y_local[-1])
+            got = trade(give, bits[0])
+            moved = locals_after(give, 1, moved)
         if t == 2:
-            sends = list(read(blocks, leave))
-            sums = sends[:1] + [shift(sends[k], -k) for k in range(1, m)]
-            _, gate_late = tied(sends[-1], gate_z)
+            for b in bits[1:]:
+                both = (keep.astype(f32) + got.astype(f32)).astype(bf16)
+                keep, give = jnp.split(both, 2)
+                got = trade(give, b)
+            _, gate_late = tied(give, gate_z)
             z_other = other_group(gate_late, gwidth)
-            moved = locals_after(sends[-1], 1, moved)
+            moved = locals_after(give, 1, moved)
         if t == 3:
             moved = locals_after(leave, 1, moved)
-            _, sums[0] = tied(y_local[-1], sums[0])
-            hidden = finish(sums, local, grow)
+            _, keep = tied(y_local[-1], keep)
+            hidden = finish([keep, got], local, grow)
             moved, _ = tied(moved, hidden)
             if per == 2:
                 moved, _ = tied(moved, z_other)
         if t == 4:
-            around = [hidden] + [shift(hidden, k) for k in range(1, m)]
+            around = {0: hidden}
+            for b in reversed(bits):
+                around.update({k | b: trade(part, b) for k, part in around.items()})
+            around = [around[k] for k in order]
             for got in around:
                 moved, _ = tied(moved, got)
         if t == 5:
@@ -776,7 +816,7 @@
             terms = lax.all_to_all(product, "tp", 0, 0)
         if t == per_prompt + m - 2:
             outs.append(back(0, leave))
-            moved, _ = tied(moved, outs[0])
+            moved, _ = tied(moved, outs[0][0])
         if t == parts + m - 3:
             moved, _ = tied(moved, product)
         carry = moved

time: 208 us -> 199 us (0.957)
  starting transfers between devices: 85.9 us -> 55.8 us
  waiting for transfers between devices: 15.1 us -> 33.2 us
  local copies, waits for them, and re-layouts: 23.4 us -> 27.2 us
    ppermute x6, starting transfers between devices: 46.7 us -> 20.1 us  [shards(): moved = lax.ppermute(leave, 'ctx', along)]
    ppermute x12 -> x11, waiting for transfers between devices: 9.32 us -> 21.7 us  [trade(): lax.ppermute(arr, 'ctx', [(i, (i // per ^ k) * per + i % per) for i in ra...]
    unnamed x140 -> x146, local copies, waits for them, and re-layouts: 14.3 us -> 18 us
    ppermute x12 -> x11, starting transfers between devices: 26.7 us -> 23.1 us  [trade(): lax.ppermute(arr, 'ctx', [(i, (i // per ^ k) * per + i % per) for i in ra...]
    ppermute x6, waiting for transfers between devices: 2.29 us -> 5.43 us  [shards(): moved = lax.ppermute(leave, 'ctx', along)]
    pallas_call x2, Pallas kernels: 18.7 us -> 15.6 us  [front(): pl.pallas_call(functools.partial(front_kernel, per, hd, s), grid_spec=plt...]
    squeeze x2 -> x0, local copies, waits for them, and re-layouts: 2.43 us -> none  [shards(): _, kept = tied(layer_out, out[0])]
    pallas_call x3, Pallas kernels: 10.3 us -> 12.6 us  [the longest x1 7.56 us: project(): pl.pallas_call(functools.partial(project_kernel, per, order), grid_spec=p...]
  transfers between devices with their start and end apart: 34 -> 33, of which waited for: 5 -> 9; matrix products, arithmetic and copies ran while one was open for 12% -> 13% of each run, Pallas kernels for 25% -> 26%
where the time goes in v2:
time: 199 us; the launch traced here: 197 us
  Pallas kernels  59.4 us (30%)
  starting transfers between devices  55.8 us (28%)
  waiting for transfers between devices  33.2 us (17%)
  local copies, waits for them, and re-layouts  27.2 us (14%)
  other arithmetic  18.3 us (9%)
    ppermute x11, starting transfers between devices, trade(): lax.ppermute(arr, 'ctx', [(i, (i // per ^ k) * per + i % per) for i in ra...  23.1 us
    ppermute x11, waiting for transfers between devices, trade(): lax.ppermute(arr, 'ctx', [(i, (i // per ^ k) * per + i % per) for i in ra...  21.7 us
    ppermute x6, starting transfers between devices, shards(): moved = lax.ppermute(leave, 'ctx', along)  20.1 us
    unnamed x146, local copies, waits for them, and re-layouts  18 us
    pallas_call x4, Pallas kernels, local_part(): pl.pallas_call(functools.partial(local_kernel, hd, k), grid=(1,), in_spec...  16.3 us
    pallas_call x2, Pallas kernels, front(): pl.pallas_call(functools.partial(front_kernel, per, hd, s), grid_spec=plt...  15.6 us
    pallas_call x2, Pallas kernels, back(): pl.pallas_call(functools.partial(back_kernel, per, hd, heads), grid_spec=...  12.2 us
    pallas_call x1, Pallas kernels, project(): pl.pallas_call(functools.partial(project_kernel, per, order), grid_spec=p...  7.56 us
  transfers between devices with their start and end apart: 33, of which 9 were waited for; matrix products, arithmetic and copies ran while one was open for 13% of the time, Pallas kernels for 26%

profile of v2, /device:TPU:0, one launch (start us, length us, event | category | flops | bytes accessed | tf_op | source)
XLA Modules:
  0.0 197.4 jit_solution(11694842299286909269)
XLA Ops:
  0.7 2.4 %constant_dynamic-slice_fusion.26 = bf16[2,128,2048]{2,1,0:T(8,128)(2,1)} fusion(bf16[2,128,4096]{2,1,0:T(8,128)(2,1)} %refs_0_.5, s32[]{:T(128)S(6)} %select_n.197), kind=kLoop, calls=%fused_computation.99 | loop fusion | bytes 2097156 | tf_op jit(solution)/shard_map/dynamic_slice | solution.py:432
  3.6 1.4 reshape.143.refs_2_
  5.0 0.7 constant_dynamic-slice_fusion.25
  10.0 1.9 copy.39
  12.1 1.3 convolution_convert_fusion.1
  16.3 4.7 %collective-permute-start.9 = (bf16[16,2560]{1,0:T(8,128)(2,1)S(1)}, bf16[16,2560]{1,0:T(8,128)(2,1)S(1)}, u32[]{:S(2)}, u32[]{:S(2)}) collective-permute-start(bf16[16,2560]{1,0:T(8,128)(2,1)S(1)} %pad_maximum_fusion.2), channel_id=1, source_target_pairs={{0,4},{4,0},{8,12},{12,8},{16,20},{20,16},{24,28},{28,24},{1,5},{5... | collective-permute-start | bytes 245768 | tf_op jit(solution)/shard_map/ppermute | solution.py:400
  21.1 0.8 collective-permute-done.9
  22.7 1.6 copy-done.4
  24.3 0.9 copy-done.21
  25.2 0.8 copy-done.23
  26.1 7.8 %front.2 = (f32[1,256,2048]{2,1,0:T(8,128)S(1)}, f32[1,256,512]{2,1,0:T(8,128)S(1)}, f32[1,32,256]{2,1,0:T(8,128)S(1)}, f32[1,32,256]{2,1,0:T(8,128)S(1)}, f32[1...) custom-call(s32[4]{0:T(128)S(1)} %pad_add_fusion.sc, ...), custom_call_target="tpu_custom_call" | custom-call | flops 9900000256 | bytes 27000000 | tf_op jit(solution)/shard_map/front/pallas_call | solution.py:522
  33.9 1.0 copy-done.8
  35.5 1.3 copy-done.29
  37.5 0.9 fusion.17
  38.4 3.8 %collective-permute-start.5 = (bf16[256,1024]{1,0:T(8,128)(2,1)}, bf16[256,1024]{1,0:T(8,128)(2,1)}, u32[]{:S(2)}, u32[]{:S(2)}) collective-permute-start(bf16[256,1024]{1,0:T(8,128)(2,1)} %fusion.17), channel_id=1, source_target_pairs={{0,8},{4,12},{8,16},{12,20},{16,24},{20,28},{1,9},{5,13},{9,17},{1... | collective-permute-start | bytes 1572872 | tf_op jit(solution)/shard_map/ppermute | solution.py:778
  42.2 0.8 collective-permute-start.10
  43.1 3.6 %collective-permute-start.12 = (bf16[16,2560]{1,0:T(8,128)(2,1)S(1)}, bf16[16,2560]{1,0:T(8,128)(2,1)}, u32[]{:S(2)}, u32[]{:S(2)}) collective-permute-start(bf16[16,2560]{1,0:T(8,128)(2,1)S(1)} %maximum_add_fusion.refs_5_), channel_id=1, source_target_pairs={{0,24},{4,28},{8,16},{12,20},{16,8},{20,12},{24,0},{28,4},{1,25},{... | collective-permute-start | bytes 245768 | tf_op jit(solution)/shard_map/ppermute | solution.py:420
  46.7 0.9 reshape.151.refs_1_
  47.8 1.6 copy-done.5
  50.7 0.9 copy-done.22
  51.6 0.8 copy-done.24
  52.5 0.8 copy-done.26
  53.2 0.7 copy-done.28
  54.0 7.8 %front.3 = (f32[1,256,2048]{2,1,0:T(8,128)S(1)}, f32[1,256,512]{2,1,0:T(8,128)S(1)}, f32[1,32,256]{2,1,0:T(8,128)S(1)}, f32[1,32,256]{2,1,0:T(8,128)S(1)}, f32[1...) custom-call(s32[4]{0:T(128)S(1)} %copy-done.19, ...), custom_call_target="tpu_custom_call" | custom-call | flops 9900000256 | bytes 27000000 | tf_op jit(solution)/shard_map/front/pallas_call | solution.py:522
  62.5 1.6 fusion.16
  64.2 1.6 collective-permute-start.6
  65.8 2.7 %window.1 = (f32[64,2048]{1,0:T(8,128)S(1)}, f32[64,128]{1,0:T(8,128)S(1)}, f32[72,384]{1,0:T(8,128)S(1)}) custom-call(s32[4]{0:T(128)S(1)} %copy-done.19, bf16[4,8,4096]{2,1,0:T(8,128)(2,1)S(1)} %copy-done.10, bf16[4,8,1024]{2,1,0:T(8,128)(2,1)S(1)} %reshape.151.refs_1_, bf16[4,8,4608]{2,1,0:T(8,128)(2,1)S(1)} %collective-permute-done.7.refs_2_.refs_5_, ...), custom_call_target="tpu_custom_call" | custom-call | flops 2200000000 | bytes 6000000 | tf_op jit(solution)/shard_map/window/pallas_call | solution.py:624
  68.5 1.0 collective-permute-start.13
  69.5 3.5 %collective-permute-start.15 = (f32[72,384]{1,0:T(8,128)S(1)}, f32[72,384]{1,0:T(8,128)S(1)}, u32[]{:S(2)}, u32[]{:S(2)}) collective-permute-start(f32[72,384]{1,0:T(8,128)S(1)} %get-tuple-element.83.refs_0_), channel_id=1, source_target_pairs={{0,24},{4,28},{8,16},{12,20},{16,8},{20,12},{24,0},{28,4},{1,25},{... | collective-permute-start | bytes 331784 | tf_op jit(solution)/shard_map/ppermute | solution.py:420
  73.0 4.1 %local.4.refs_7_ = f32[1,256,1024]{2,1,0:T(8,128)S(1)} custom-call(f32[1,256,2048]{2,1,0:T(8,128)S(1)} %copy-done.30, f32[1,256,512]{2,1,0:T(8,128)S(1)} %copy-done.37, f32[1,32,256]{2,1,0:T(8,128)S(1)} %copy-done.42, f32[1,32,256]{2,1,0:T(8,128)S(1)} %copy-done.44, f32[1,256,128]{2,1,0:T(8,128)S(1)} %copy-done.40, f32[1,2048]{1,0:T(1,128)S(1)} %copy-done.13), custom_call_target="tpu_custom_call" | custom-call | flops 5500000256 | bytes 15000000 | tf_op jit(solution)/shard_map/local/pallas_call | solution.py:561
  77.1 3.1 %collective-permute-done.13.refs_1_ = f32[72,384]{1,0:T(8,128)S(1)} collective-permute-done((f32[72,384]{1,0:T(8,128)S(1)}, f32[72,384]{1,0:T(8,128)S(1)}, u32[]{:S(2)}, u32[]{:S(2)}) %collective-permute-start.13) | collective-permute-done | bytes 110624 | tf_op jit(solution)/shard_map/ppermute | solution.py:420
  80.2 2.4 %collective-permute-done.14.refs_2_ = f32[72,384]{1,0:T(8,128)S(1)} collective-permute-done((f32[72,384]{1,0:T(8,128)S(1)}, f32[72,384]{1,0:T(8,128)S(1)}, u32[]{:S(2)}, u32[]{:S(2)}) %collective-permute-start.14) | collective-permute-done | bytes 110624 | tf_op jit(solution)/shard_map/ppermute | solution.py:420
  82.6 1.8 collective-permute-done.15.refs_3_
  84.3 3.1 %read.1 = (bf16[128,2048]{1,0:T(8,128)(2,1)S(1)}, bf16[128,2048]{1,0:T(8,128)(2,1)S(1)}) custom-call(s32[4]{0:T(128)S(1)} %copy-done.19, f32[72,384]{1,0:T(8,128)S(1)} %get-tuple-element.83.refs_0_, f32[72,384]{1,0:T(8,128)S(1)} %collective-permute-done.13.refs_1_, f32[72,384]{1,0:T(8,128)S(1)} %collective-permute-done.14.refs_2_, ...), custom_call_target="tpu_custom_call" | custom-call | flops 4400000000 | bytes 12000000 | tf_op jit(solution)/shard_map/read/pallas_call | solution.py:660
  87.5 2.4 %collective-permute-start.17 = (bf16[128,2048]{1,0:T(8,128)(2,1)S(1)}, bf16[128,2048]{1,0:T(8,128)(2,1)S(1)}, u32[]{:S(2)}, u32[]{:S(2)}) collective-permute-start(bf16[128,2048]{1,0:T(8,128)(2,1)S(1)} %get-tuple-element.84), channel_id=1, source_target_pairs={{0,8},{4,12},{8,0},{12,4},{16,24},{20,28},{24,16},{28,20},{1,9},{5... | collective-permute-start | bytes 1572872 | tf_op jit(solution)/shard_map/ppermute | solution.py:420
  89.9 4.1 %local.5.refs_8_ = f32[1,256,1024]{2,1,0:T(8,128)S(1)} custom-call(f32[1,256,2048]{2,1,0:T(8,128)S(1)} %copy-done.30, f32[1,256,512]{2,1,0:T(8,128)S(1)} %copy-done.37, f32[1,32,256]{2,1,0:T(8,128)S(1)} %copy-done.42, f32[1,32,256]{2,1,0:T(8,128)S(1)} %copy-done.44, f32[1,256,128]{2,1,0:T(8,128)S(1)} %copy-done.40, f32[1,2048]{1,0:T(1,128)S(1)} %copy-done.13), custom_call_target="tpu_custom_call" | custom-call | flops 5500000256 | bytes 15000000 | tf_op jit(solution)/shard_map/local/pallas_call | solution.py:561
  94.3 2.2 %collective-permute-start.16 = (bf16[256,1024]{1,0:T(8,128)(2,1)S(1)}, bf16[256,1024]{1,0:T(8,128)(2,1)S(1)}, u32[]{:S(2)}, u32[]{:S(2)}) collective-permute-start(bf16[256,1024]{1,0:T(8,128)(2,1)S(1)} %fusion.21), channel_id=1, source_target_pairs={{0,8},{4,12},{8,16},{12,20},{16,24},{20,28},{1,9},{5,13},{9,17},{1... | collective-permute-start | bytes 1572872 | tf_op jit(solution)/shard_map/ppermute | solution.py:778
  96.5 5.7 %collective-permute-done.17 = bf16[128,2048]{1,0:T(8,128)(2,1)S(1)} collective-permute-done((bf16[128,2048]{1,0:T(8,128)(2,1)S(1)}, bf16[128,2048]{1,0:T(8,128)(2,1)S(1)}, u32[]{:S(2)}, u32[]{:S(2)}) %collective-permute-start.17) | collective-permute-done | bytes 524320 | tf_op jit(solution)/shard_map/ppermute | solution.py:420
  102.5 3.0 %collective-permute-start.19 = (bf16[64,2048]{1,0:T(8,128)(2,1)S(1)}, bf16[64,2048]{1,0:T(8,128)(2,1)S(1)}, u32[]{:S(2)}, u32[]{:S(2)}) collective-permute-start(bf16[64,2048]{1,0:T(8,128)(2,1)S(1)} %get-tuple-element.132), channel_id=1, source_target_pairs={{0,16},{4,20},{8,24},{12,28},{16,0},{20,4},{24,8},{28,12},{1,17},{... | collective-permute-start | bytes 786440 | tf_op jit(solution)/shard_map/ppermute | solution.py:420
  105.5 1.1 constant_dynamic-slice_fusion.2
  106.5 4.1 %local.6.refs_7_ = f32[1,256,1024]{2,1,0:T(8,128)S(1)} custom-call(f32[1,256,2048]{2,1,0:T(8,128)S(1)} %get-tuple-element.95.act, f32[1,256,512]{2,1,0:T(8,128)S(1)} %get-tuple-element.91.bc.refs_4_, f32[1,32,256]{2,1,0:T(8,128)S(1)} %get-tuple-element.92.run, f32[1,32,256]{2,1,0:T(8,128)S(1)} %get-tuple-element.93.step, ...), custom_call_target="tpu_custom_call" | custom-call | flops 5500000256 | bytes 15000000 | tf_op jit(solution)/shard_map/local/pallas_call | solution.py:561
  110.6 2.4 %collective-permute-done.16 = bf16[256,1024]{1,0:T(8,128)(2,1)S(1)} collective-permute-done((bf16[256,1024]{1,0:T(8,128)(2,1)S(1)}, bf16[256,1024]{1,0:T(8,128)(2,1)S(1)}, u32[]{:S(2)}, u32[]{:S(2)}) %collective-permute-start.16) | collective-permute-done | bytes 524320 | tf_op jit(solution)/shard_map/ppermute | solution.py:778
  113.0 1.1 fusion.20
  114.1 5.3 %collective-permute-start.18 = (bf16[256,1024]{1,0:T(8,128)(2,1)}, bf16[256,1024]{1,0:T(8,128)(2,1)}, u32[]{:S(2)}, u32[]{:S(2)}) collective-permute-start(bf16[256,1024]{1,0:T(8,128)(2,1)} %fusion.20), channel_id=1, source_target_pairs={{0,8},{4,12},{8,16},{12,20},{16,24},{20,28},{1,9},{5,13},{9,17},{1... | collective-permute-start | bytes 1572872 | tf_op jit(solution)/shard_map/ppermute | solution.py:778
  119.4 4.1 %local.7.refs_8_ = f32[1,256,1024]{2,1,0:T(8,128)S(1)} custom-call(f32[1,256,2048]{2,1,0:T(8,128)S(1)} %get-tuple-element.95.act, f32[1,256,512]{2,1,0:T(8,128)S(1)} %get-tuple-element.91.bc.refs_4_, f32[1,32,256]{2,1,0:T(8,128)S(1)} %get-tuple-element.92.run, f32[1,32,256]{2,1,0:T(8,128)S(1)} %get-tuple-element.93.step, ...), custom_call_target="tpu_custom_call" | custom-call | flops 5500000256 | bytes 15000000 | tf_op jit(solution)/shard_map/local/pallas_call | solution.py:561
  123.5 1.0 copy-done.32
  124.5 1.9 finish.1.refs_0_
  126.4 3.3 %collective-permute-start.22 = (bf16[64,2048]{1,0:T(8,128)(2,1)}, bf16[64,2048]{1,0:T(8,128)(2,1)S(1)}, u32[]{:S(2)}, u32[]{:S(2)}) collective-permute-start(bf16[64,2048]{1,0:T(8,128)(2,1)} %finish.1.refs_0_), channel_id=1, source_target_pairs={{0,16},{4,20},{8,24},{12,28},{16,0},{20,4},{24,8},{28,12},{1,17},{... | collective-permute-start | bytes 786440 | tf_op jit(solution)/shard_map/ppermute | solution.py:420
  130.2 8.7 %collective-permute-done.22.refs_1_ = bf16[64,2048]{1,0:T(8,128)(2,1)S(1)} collective-permute-done((bf16[64,2048]{1,0:T(8,128)(2,1)}, bf16[64,2048]{1,0:T(8,128)(2,1)S(1)}, u32[]{:S(2)}, u32[]{:S(2)}) %collective-permute-start.22) | collective-permute-done | bytes 262176 | tf_op jit(solution)/shard_map/ppermute | solution.py:420
  138.9 5.0 %collective-permute-start.24 = (bf16[64,2048]{1,0:T(8,128)(2,1)S(1)}, bf16[64,2048]{1,0:T(8,128)(2,1)}, u32[]{:S(2)}, u32[]{:S(2)}) collective-permute-start(bf16[64,2048]{1,0:T(8,128)(2,1)S(1)} %collective-permute-done.22.refs_1_), channel_id=1, source_target_pairs={{0,8},{4,12},{8,0},{12,4},{16,24},{20,28},{24,16},{28,20},{1,9},{5... | collective-permute-start | bytes 786440 | tf_op jit(solution)/shard_map/ppermute | solution.py:420
  143.9 3.2 %fusion.30 = (bf16[1,256,1024]{2,1,0:T(8,128)(2,1)}, bf16[1,256,1024]{2,1,0:T(8,128)(2,1)}, bf16[256,1024]{1,0:T(8,128)(2,1)}) fusion(bf16[256,1024]{1,0:T(8,128)(2,1)} %collective-permute-done.18, bf16[256,1024]{1,0:T(8,128)(2,1)} %copy-done.45, bf16[256,1024]{1,0:T(8,128)(2,1)} %copy-done.47, bf16[2,256,1024]{2,1,0:T(8,128)(2,1)S(1)} %copy-done.9, ...), kind=kLoop, calls=%fused_computation.49 | loop fusion | flops 3670016 | bytes 6823948 | tf_op jit(solution)/shard_map/broadcast_in_dim | solution.py:746
  147.1 2.1 %collective-permute-start.21 = (bf16[256,1024]{1,0:T(8,128)(2,1)}, bf16[256,1024]{1,0:T(8,128)(2,1)S(1)}, u32[]{:S(2)}, u32[]{:S(2)}) collective-permute-start(bf16[256,1024]{1,0:T(8,128)(2,1)} %get-tuple-element.130), channel_id=1, source_target_pairs={{0,8},{4,12},{8,16},{12,20},{16,24},{20,28},{1,9},{5,13},{9,17},{1... | collective-permute-start | bytes 1572872 | tf_op jit(solution)/shard_map/ppermute | solution.py:778
  149.9 6.1 %back.2 = (bf16[128,2048]{1,0:T(8,128)(2,1)}, bf16[128,2048]{1,0:T(8,128)(2,1)}) custom-call(s32[4]{0:T(128)} %copy-done.18, bf16[2,128,4096]{2,1,0:T(8,128)(2,1)} %refs_0_.8, bf16[2,128,2048]{2,1,0:T(8,128)(2,1)} %collective-permute-done.20.refs_1_, bf16[1,256,1024]{2,1,0:T(8,128)(2,1)} %get-tuple-element.123.refs_2_, ...), custom_call_target="tpu_custom_call" | custom-call | flops 5500000256 | bytes 15000000 | tf_op jit(solution)/shard_map/back/pallas_call | solution.py:723
  156.0 3.0 %collective-permute-done.21 = bf16[256,1024]{1,0:T(8,128)(2,1)S(1)} collective-permute-done((bf16[256,1024]{1,0:T(8,128)(2,1)}, bf16[256,1024]{1,0:T(8,128)(2,1)S(1)}, u32[]{:S(2)}, u32[]{:S(2)}) %collective-permute-start.21) | collective-permute-done | bytes 524320 | tf_op jit(solution)/shard_map/ppermute | solution.py:778
  159.1 2.3 %fusion.18 = bf16[256,1024]{1,0:T(8,128)(2,1)} fusion(f32[2,256,1024]{2,1,0:T(8,128)} %copy-done.2, s32[]{:T(128)S(6)} %min.64, bf16[256,1024]{1,0:T(8,128)(2,1)S(1)} %collective-permute-done.21, f32[2,256,1024]{2,1,0:T(8,128)S(1)} %get-tuple-element.62.refs_4_, s32[]{:T(128)S(6)} %min.52, f32[1024]{0:T(1024)S(1)} %bitcast.152, f32[1024]{0:T(1024)S(1)} %bitcast.151, ...), kind=kLoop, calls=%fused_computation.34 | loop fusion | flops 2097152 | bytes 3153929 | tf_op jit(solution)/shard_map/jit(_where)/select_n | solution.py:777
  161.4 5.1 %collective-permute-start.30 = (bf16[256,1024]{1,0:T(8,128)(2,1)}, bf16[256,1024]{1,0:T(8,128)(2,1)}, u32[]{:S(2)}, u32[]{:S(2)}) collective-permute-start(bf16[256,1024]{1,0:T(8,128)(2,1)} %fusion.18), channel_id=1, source_target_pairs={{0,8},{4,12},{8,16},{12,20},{16,24},{20,28},{1,9},{5,13},{9,17},{1... | collective-permute-start | bytes 1572872 | tf_op jit(solution)/shard_map/ppermute | solution.py:778
  168.1 7.6 %project.1 = f32[4,4,16,1024]{3,2,1,0:T(8,128)} custom-call(s32[4]{0:T(128)} %copy-done.18, bf16[64,2048]{1,0:T(8,128)(2,1)} %finish.1.refs_0_, bf16[64,2048]{1,0:T(8,128)(2,1)} %copy-done.64, bf16[64,2048]{1,0:T(8,128)(2,1)} %collective-permute-done.23.refs_2_, bf16[64,2048]{1,0:T(8,128)(2,1)} %collective-permute-done.24.refs_3_, ...), custom_call_target="tpu_custom_call" | custom-call | flops 6600000000 | bytes 18000000 | tf_op jit(solution)/shard_map/project/pallas_call | solution.py:695
  175.7 3.8 %all-to-all-start = ((f32[4,4,16,1024]{3,2,1,0:T(8,128)}), f32[4,4,16,1024]{3,2,1,0:T(8,128)S(1)}, u32[]{:S(2)}, u32[]{:S(2)}) async-start(f32[4,4,16,1024]{3,2,1,0:T(8,128)} %project.1), calls=%async_computation | async-start | bytes 2097152 | tf_op jit(solution)/shard_map/all_to_all | solution.py:816
  179.5 2.2 %fusion.24 = (bf16[1,256,1024]{2,1,0:T(8,128)(2,1)}, bf16[1,256,1024]{2,1,0:T(8,128)(2,1)}) fusion(bf16[256,1024]{1,0:T(8,128)(2,1)} %collective-permute-done.30, bf16[256,1024]{1,0:T(8,128)(2,1)S(1)} %collective-permute-done.21, bf16[256,1024]{1,0:T(8,128)(2,1)} %collective-permute-done.18, bf16[2,256,1024]{2,1,0:T(8,128)(2,1)S(1)} %copy-done.7, ...), kind=kLoop, calls=%fused_computation.41 | loop fusion | flops 1572864 | bytes 4194307 | tf_op jit(solution)/shard_map/broadcast_in_dim | solution.py:746
  181.7 6.1 %back.3 = (bf16[128,2048]{1,0:T(8,128)(2,1)}, bf16[128,2048]{1,0:T(8,128)(2,1)}) custom-call(s32[4]{0:T(128)} %copy-done.18, bf16[2,128,4096]{2,1,0:T(8,128)(2,1)} %refs_0_.8, bf16[2,128,2048]{2,1,0:T(8,128)(2,1)} %collective-permute-done.20.refs_1_, bf16[1,256,1024]{2,1,0:T(8,128)(2,1)} %get-tuple-element.121.refs_2_, ...), custom_call_target="tpu_custom_call" | custom-call | flops 5500000256 | bytes 15000000 | tf_op jit(solution)/shard_map/back/pallas_call | solution.py:723
  188.4 5.3 %all-to-all-done = f32[4,4,16,1024]{3,2,1,0:T(8,128)S(1)} async-done(((f32[4,4,16,1024]{3,2,1,0:T(8,128)}), f32[4,4,16,1024]{3,2,1,0:T(8,128)S(1)}, u32[]{:S(2)}, u32[]{:S(2)}) %all-to-all-start) | async-done | bytes 1048608 | tf_op jit(solution)/shard_map/all_to_all | solution.py:816
  193.6 0.7 reduce_sum.9
  194.4 1.2 broadcast_select_fusion.1
  195.9 1.5 pad_maximum_fusion
  (229 shorter events, 16.0 us)
Async XLA Ops:
  0.6 13.3 %copy-start = (f32[4096]{0:T(1024)S(1)}, f32[4096]{0:T(1024)}, u32[]{:S(2)}) copy-start(f32[4096]{0:T(1024)} %param.33) | copy-start | bytes 49156
  0.7 9.0 %copy-start.69 = (f32[64]{0:T(128)S(1)}, f32[64]{0:T(128)}, u32[]{:S(2)}) copy-start(f32[64]{0:T(128)} %param.26) | copy-start | bytes 772
  0.7 9.0 %copy-start.50 = (bf16[2,3,4096]{2,0,1:T(2,128)(2,1)S(1)}, bf16[2,3,4096]{2,0,1:T(2,128)(2,1)}, u32[]{:S(2)}) copy-start(bf16[2,3,4096]{2,0,1:T(2,128)(2,1)} %param.35) | copy-start | bytes 147460
  0.7 9.1 %copy-start.58 = (bf16[2,3,2,512]{3,2,1,0:T(2,128)(2,1)S(1)}, bf16[2,3,2,512]{3,2,1,0:T(2,128)(2,1)}, u32[]{:S(2)}) copy-start(bf16[2,3,2,512]{3,2,1,0:T(2,128)(2,1)} %param.36) | copy-start | bytes 36868
  0.7 9.2 %copy-start.61 = (f32[64]{0:T(128)S(1)}, f32[64]{0:T(128)}, u32[]{:S(2)}) copy-start(f32[64]{0:T(128)} %param.27) | copy-start | bytes 772
  3.2 8.8 %copy-start.60 = (s32[2]{0:T(128)S(1)}, s32[2]{0:T(128)}, u32[]{:S(2)}) copy-start(s32[2]{0:T(128)} %param.37) | copy-start | bytes 28
  3.2 19.5 %collective-permute-start = (bf16[2,128,2048]{2,1,0:T(8,128)(2,1)}, bf16[2,128,2048]{2,1,0:T(8,128)(2,1)}, u32[]{:S(2)}, u32[]{:S(2)}) collective-permute-start(bf16[2,128,2048]{2,1,0:T(8,128)(2,1)} %constant_dynamic-slice_fusion.26), channel_id=1, source_target_pairs={{0,4},{4,0},{8,12},{12,8},{16,20},{20,16},{24,28},{28,24},{1,5},{5... | collective-permute-start | bytes 3145736 | tf_op jit(solution)/shard_map/ppermute | solution.py:400
  5.8 16.2 %collective-permute-start.1 = (bf16[2,128,512]{2,1,0:T(8,128)(2,1)}, bf16[2,128,512]{2,1,0:T(8,128)(2,1)S(1)}, u32[]{:S(2)}, u32[]{:S(2)}) collective-permute-start(bf16[2,128,512]{2,1,0:T(8,128)(2,1)} %constant_dynamic-slice_fusion.25), channel_id=1, source_target_pairs={{0,4},{4,0},{8,12},{12,8},{16,20},{20,16},{24,28},{28,24},{1,5},{5... | collective-permute-start | bytes 786440 | tf_op jit(solution)/shard_map/ppermute | solution.py:400
  6.5 15.5 %collective-permute-start.2 = (f32[2,32,128]{2,1,0:T(8,128)}, f32[2,32,128]{2,1,0:T(8,128)S(1)}, u32[]{:S(2)}, u32[]{:S(2)}) collective-permute-start(f32[2,32,128]{2,1,0:T(8,128)} %constant_dynamic-slice_fusion.24), channel_id=1, source_target_pairs={{0,4},{4,0},{8,12},{12,8},{16,20},{20,16},{24,28},{28,24},{1,5},{5... | collective-permute-start | bytes 98312 | tf_op jit(solution)/shard_map/ppermute | solution.py:400
  7.6 8.6 %collective-permute-start.3 = (bf16[2,3,2560]{2,1,0:T(4,128)(2,1)}, bf16[2,3,2560]{2,1,0:T(4,128)(2,1)S(1)}, u32[]{:S(2)}, u32[]{:S(2)}) collective-permute-start(bf16[2,3,2560]{2,1,0:T(4,128)(2,1)} %pad_maximum_fusion.3), channel_id=1, source_target_pairs={{4,12},{12,20},{20,28},{5,13},{13,21},{21,29},{6,14},{14,22},{22,3... | collective-permute-start | bytes 92168 | tf_op jit(solution)/shard_map/ppermute | solution.py:445
  8.9 12.1 %collective-permute-start.4 = (bf16[2,3,2560]{2,1,0:T(4,128)(2,1)}, bf16[2,3,2560]{2,1,0:T(4,128)(2,1)S(1)}, u32[]{:S(2)}, u32[]{:S(2)}) collective-permute-start(bf16[2,3,2560]{2,1,0:T(4,128)(2,1)} %pad_maximum_fusion.4), channel_id=1, source_target_pairs={{4,8},{12,16},{20,24},{5,9},{13,17},{21,25},{6,10},{14,18},{22,26}... | collective-permute-start | bytes 92168 | tf_op jit(solution)/shard_map/ppermute | solution.py:445
  13.4 9.3 %copy-start.27 = (f32[4096]{0:T(1024)S(1)}, f32[4096]{0:T(1024)}, u32[]{:S(2)}) copy-start(f32[4096]{0:T(1024)} %param.31) | copy-start | bytes 49156
  15.2 18.7 %copy-start.18 = (s32[4]{0:T(128)}, s32[4]{0:T(128)S(1)}, u32[]{:S(2)}) copy-start(s32[4]{0:T(128)S(1)} %pad_add_fusion.sc) | copy-start | bytes 52
  15.4 18.5 %copy-start.16 = (f32[1,1,2,512]{3,1,2,0:T(1,128)}, f32[1,1,2,512]{3,1,2,0:T(1,128)S(1)}, u32[]{:S(2)}) copy-start(f32[1,1,2,512]{3,1,2,0:T(1,128)S(1)} %copy.38) | copy-start | bytes 12292
  16.3 5.7 %collective-permute-start.9 = (bf16[16,2560]{1,0:T(8,128)(2,1)S(1)}, bf16[16,2560]{1,0:T(8,128)(2,1)S(1)}, u32[]{:S(2)}, u32[]{:S(2)}) collective-permute-start(bf16[16,2560]{1,0:T(8,128)(2,1)S(1)} %pad_maximum_fusion.2), channel_id=1, source_target_pairs={{0,4},{4,0},{8,12},{12,8},{16,20},{20,16},{24,28},{28,24},{1,5},{5... | collective-permute-start | bytes 245768 | tf_op jit(solution)/shard_map/ppermute | solution.py:400
  26.1 21.6 %copy-start.10 = (bf16[4,8,4096]{2,1,0:T(8,128)(2,1)S(1)}, bf16[4,8,4096]{2,1,0:T(8,128)(2,1)}, u32[]{:S(2)}) copy-start(bf16[4,8,4096]{2,1,0:T(8,128)(2,1)} %refs_0_.6) | copy-start | bytes 786436
  26.1 21.6 %copy-start.11 = (bf16[4,8,4096]{2,1,0:T(8,128)(2,1)S(1)}, bf16[4,8,4096]{2,1,0:T(8,128)(2,1)}, u32[]{:S(2)}) copy-start(bf16[4,8,4096]{2,1,0:T(8,128)(2,1)} %refs_4_.4) | copy-start | bytes 786436
  38.4 23.6 %collective-permute-start.5 = (bf16[256,1024]{1,0:T(8,128)(2,1)}, bf16[256,1024]{1,0:T(8,128)(2,1)}, u32[]{:S(2)}, u32[]{:S(2)}) collective-permute-start(bf16[256,1024]{1,0:T(8,128)(2,1)} %fusion.17), channel_id=1, source_target_pairs={{0,8},{4,12},{8,16},{12,20},{16,24},{20,28},{1,9},{5,13},{9,17},{1... | collective-permute-start | bytes 1572872 | tf_op jit(solution)/shard_map/ppermute | solution.py:778
  42.2 23.5 %collective-permute-start.10 = (bf16[16,2560]{1,0:T(8,128)(2,1)S(1)}, bf16[16,2560]{1,0:T(8,128)(2,1)}, u32[]{:S(2)}, u32[]{:S(2)}) collective-permute-start(bf16[16,2560]{1,0:T(8,128)(2,1)S(1)} %maximum_add_fusion.refs_5_), channel_id=1, source_target_pairs={{0,8},{4,12},{8,0},{12,4},{16,24},{20,28},{24,16},{28,20},{1,9},{5... | collective-permute-start | bytes 245768 | tf_op jit(solution)/shard_map/ppermute | solution.py:420
  43.1 22.7 %collective-permute-start.11 = (bf16[16,2560]{1,0:T(8,128)(2,1)S(1)}, bf16[16,2560]{1,0:T(8,128)(2,1)}, u32[]{:S(2)}, u32[]{:S(2)}) collective-permute-start(bf16[16,2560]{1,0:T(8,128)(2,1)S(1)} %maximum_add_fusion.refs_5_), channel_id=1, source_target_pairs={{0,16},{4,20},{8,24},{12,28},{16,0},{20,4},{24,8},{28,12},{1,17},{... | collective-permute-start | bytes 245768 | tf_op jit(solution)/shard_map/ppermute | solution.py:420
  43.1 22.6 %collective-permute-start.12 = (bf16[16,2560]{1,0:T(8,128)(2,1)S(1)}, bf16[16,2560]{1,0:T(8,128)(2,1)}, u32[]{:S(2)}, u32[]{:S(2)}) collective-permute-start(bf16[16,2560]{1,0:T(8,128)(2,1)S(1)} %maximum_add_fusion.refs_5_), channel_id=1, source_target_pairs={{0,24},{4,28},{8,16},{12,20},{16,8},{20,12},{24,0},{28,4},{1,25},{... | collective-permute-start | bytes 245768 | tf_op jit(solution)/shard_map/ppermute | solution.py:420
  47.7 18.1 %collective-permute-start.7 = (bf16[4,8,4608]{2,1,0:T(8,128)(2,1)S(1)}, bf16[4,8,4608]{2,1,0:T(8,128)(2,1)S(1)}, u32[]{:S(2)}, u32[]{:S(2)}) collective-permute-start(bf16[4,8,4608]{2,1,0:T(8,128)(2,1)S(1)} %pad_maximum_fusion.1), channel_id=1, source_target_pairs={{0,4},{4,0},{8,12},{12,8},{16,20},{20,16},{24,28},{28,24},{1,5},{5... | collective-permute-start | bytes 884744 | tf_op jit(solution)/shard_map/ppermute | solution.py:400
  54.0 7.8 %copy-start.70 = (s32[8]{0:T(128)S(1)}, s32[8]{0:T(128)}, u32[]{:S(2)}) copy-start(s32[8]{0:T(128)} %param.42) | copy-start | bytes 100
  54.0 8.0 %copy-start.56 = (f32[4,64,8]{1,2,0:T(8,128)S(1)}, f32[4,64,8]{1,2,0:T(8,128)}, u32[]{:S(2)}) copy-start(f32[4,64,8]{1,2,0:T(8,128)} %param.41) | copy-start | bytes 24580
  54.0 8.6 %copy-start.54 = (f32[1,1,1024]{2,1,0:T(1,128)S(1)}, f32[1,1,1024]{2,1,0:T(1,128)}, u32[]{:S(2)}) copy-start(f32[1,1,1024]{2,1,0:T(1,128)} %get-tuple-element.138) | copy-start | bytes 12292
  61.8 51.2 %copy-start.2 = (f32[2,256,1024]{2,1,0:T(8,128)}, f32[2,256,1024]{2,1,0:T(8,128)S(1)}, u32[]{:S(2)}) copy-start(f32[2,256,1024]{2,1,0:T(8,128)S(1)} %get-tuple-element.64.refs_5_) | copy-start | bytes 6291460
  61.8 57.5 %copy-start.35 = (f32[1,256,512]{2,1,0:T(8,128)}, f32[1,256,512]{2,1,0:T(8,128)S(1)}, u32[]{:S(2)}) copy-start(f32[1,256,512]{2,1,0:T(8,128)S(1)} %get-tuple-element.91.bc.refs_4_) | copy-start | bytes 1572868
  61.8 57.5 %copy-start.38 = (f32[1,256,128]{2,1,0:T(8,128)}, f32[1,256,128]{2,1,0:T(8,128)S(1)}, u32[]{:S(2)}) copy-start(f32[1,256,128]{2,1,0:T(8,128)S(1)} %get-tuple-element.116.refs_10_.pack.refs_5_) | copy-start | bytes 393220
  62.0 2.2 %collective-permute-start.8 = (f32[5,8,128]{2,1,0:T(8,128)S(1)}, f32[5,8,128]{2,1,0:T(8,128)S(1)}, u32[]{:S(2)}, u32[]{:S(2)}) collective-permute-start(f32[5,8,128]{2,1,0:T(8,128)S(1)} %select_maximum_fusion.refs_3_), channel_id=1, source_target_pairs={{0,4},{4,0},{8,12},{12,8},{16,20},{20,16},{24,28},{28,24},{1,5},{5... | collective-permute-start | bytes 61448 | tf_op jit(solution)/shard_map/ppermute | solution.py:400
  64.2 29.8 %collective-permute-start.6 = (bf16[256,1024]{1,0:T(8,128)(2,1)S(1)}, bf16[256,1024]{1,0:T(8,128)(2,1)S(1)}, u32[]{:S(2)}, u32[]{:S(2)}) collective-permute-start(bf16[256,1024]{1,0:T(8,128)(2,1)S(1)} %fusion.16), channel_id=1, source_target_pairs={{0,8},{4,12},{8,16},{12,20},{16,24},{20,28},{1,9},{5,13},{9,17},{1... | collective-permute-start | bytes 1572872 | tf_op jit(solution)/shard_map/ppermute | solution.py:778
  65.8 7.2 %copy-start.13 = (f32[1,2048]{1,0:T(1,128)S(1)}, f32[1,2048]{1,0:T(1,128)}, u32[]{:S(2)}) copy-start(f32[1,2048]{1,0:T(1,128)} %broadcast_in_dim_reshape.3.skip) | copy-start | bytes 24580
  65.8 7.2 %copy-start.30 = (f32[1,256,2048]{2,1,0:T(8,128)S(1)}, f32[1,256,2048]{2,1,0:T(8,128)}, u32[]{:S(2)}) copy-start(f32[1,256,2048]{2,1,0:T(8,128)} %copy-done.29) | copy-start | bytes 6291460
  65.8 7.2 %copy-start.37 = (f32[1,256,512]{2,1,0:T(8,128)S(1)}, f32[1,256,512]{2,1,0:T(8,128)}, u32[]{:S(2)}) copy-start(f32[1,256,512]{2,1,0:T(8,128)} %copy-done.36) | copy-start | bytes 1572868
  65.8 7.2 %copy-start.42 = (f32[1,32,256]{2,1,0:T(8,128)S(1)}, f32[1,32,256]{2,1,0:T(8,128)}, u32[]{:S(2)}) copy-start(f32[1,32,256]{2,1,0:T(8,128)} %copy-done.41) | copy-start | bytes 98308
  68.5 11.7 %collective-permute-start.13 = (f32[72,384]{1,0:T(8,128)S(1)}, f32[72,384]{1,0:T(8,128)S(1)}, u32[]{:S(2)}, u32[]{:S(2)}) collective-permute-start(f32[72,384]{1,0:T(8,128)S(1)} %get-tuple-element.83.refs_0_), channel_id=1, source_target_pairs={{0,16},{4,20},{8,24},{12,28},{16,0},{20,4},{24,8},{28,12},{1,17},{... | collective-permute-start | bytes 331784 | tf_op jit(solution)/shard_map/ppermute | solution.py:420
  69.5 13.1 %collective-permute-start.14 = (f32[72,384]{1,0:T(8,128)S(1)}, f32[72,384]{1,0:T(8,128)S(1)}, u32[]{:S(2)}, u32[]{:S(2)}) collective-permute-start(f32[72,384]{1,0:T(8,128)S(1)} %get-tuple-element.83.refs_0_), channel_id=1, source_target_pairs={{0,8},{4,12},{8,0},{12,4},{16,24},{20,28},{24,16},{28,20},{1,9},{5... | collective-permute-start | bytes 331784 | tf_op jit(solution)/shard_map/ppermute | solution.py:420
  69.5 14.8 %collective-permute-start.15 = (f32[72,384]{1,0:T(8,128)S(1)}, f32[72,384]{1,0:T(8,128)S(1)}, u32[]{:S(2)}, u32[]{:S(2)}) collective-permute-start(f32[72,384]{1,0:T(8,128)S(1)} %get-tuple-element.83.refs_0_), channel_id=1, source_target_pairs={{0,24},{4,28},{8,16},{12,20},{16,8},{20,12},{24,0},{28,4},{1,25},{... | collective-permute-start | bytes 331784 | tf_op jit(solution)/shard_map/ppermute | solution.py:420
  77.1 10.4 %copy-start.33 = (f32[1,256,1024]{2,1,0:T(8,128)}, f32[1,256,1024]{2,1,0:T(8,128)S(1)}, u32[]{:S(2)}) copy-start(f32[1,256,1024]{2,1,0:T(8,128)S(1)} %local.4.refs_7_) | copy-start | bytes 3145732
  87.5 14.8 %collective-permute-start.17 = (bf16[128,2048]{1,0:T(8,128)(2,1)S(1)}, bf16[128,2048]{1,0:T(8,128)(2,1)S(1)}, u32[]{:S(2)}, u32[]{:S(2)}) collective-permute-start(bf16[128,2048]{1,0:T(8,128)(2,1)S(1)} %get-tuple-element.84), channel_id=1, source_target_pairs={{0,8},{4,12},{8,0},{12,4},{16,24},{20,28},{24,16},{28,20},{1,9},{5... | collective-permute-start | bytes 1572872 | tf_op jit(solution)/shard_map/ppermute | solution.py:420
  94.0 8.4 %copy-start.34 = (f32[1,256,1024]{2,1,0:T(8,128)}, f32[1,256,1024]{2,1,0:T(8,128)S(1)}, u32[]{:S(2)}) copy-start(f32[1,256,1024]{2,1,0:T(8,128)S(1)} %local.5.refs_8_) | copy-start | bytes 3145732
  94.0 8.4 %copy-start.47 = (bf16[256,1024]{1,0:T(8,128)(2,1)}, bf16[256,1024]{1,0:T(8,128)(2,1)S(1)}, u32[]{:S(2)}) copy-start(bf16[256,1024]{1,0:T(8,128)(2,1)S(1)} %collective-permute-done.6) | copy-start | bytes 1572868
  94.3 11.2 %copy-start.49 = (bf16[2,128,4096]{2,1,0:T(8,128)(2,1)S(1)}, bf16[2,128,4096]{2,1,0:T(8,128)(2,1)}, u32[]{:S(2)}) copy-start(bf16[2,128,4096]{2,1,0:T(8,128)(2,1)} %refs_0_.8) | copy-start | bytes 6291460
  94.3 18.7 %collective-permute-start.16 = (bf16[256,1024]{1,0:T(8,128)(2,1)S(1)}, bf16[256,1024]{1,0:T(8,128)(2,1)S(1)}, u32[]{:S(2)}, u32[]{:S(2)}) collective-permute-start(bf16[256,1024]{1,0:T(8,128)(2,1)S(1)} %fusion.21), channel_id=1, source_target_pairs={{0,8},{4,12},{8,16},{12,20},{16,24},{20,28},{1,9},{5,13},{9,17},{1... | collective-permute-start | bytes 1572872 | tf_op jit(solution)/shard_map/ppermute | solution.py:778
  102.5 22.0 %collective-permute-start.19 = (bf16[64,2048]{1,0:T(8,128)(2,1)S(1)}, bf16[64,2048]{1,0:T(8,128)(2,1)S(1)}, u32[]{:S(2)}, u32[]{:S(2)}) collective-permute-start(bf16[64,2048]{1,0:T(8,128)(2,1)S(1)} %get-tuple-element.132), channel_id=1, source_target_pairs={{0,16},{4,20},{8,24},{12,28},{16,0},{20,4},{24,8},{28,12},{1,17},{... | collective-permute-start | bytes 786440 | tf_op jit(solution)/shard_map/ppermute | solution.py:420
  106.5 37.3 %collective-permute-start.20 = (bf16[2,128,2048]{2,1,0:T(8,128)(2,1)}, bf16[2,128,2048]{2,1,0:T(8,128)(2,1)}, u32[]{:S(2)}, u32[]{:S(2)}) collective-permute-start(bf16[2,128,2048]{2,1,0:T(8,128)(2,1)} %constant_dynamic-slice_fusion.2), channel_id=1, source_target_pairs={{0,4},{4,0},{8,12},{12,8},{16,20},{20,16},{24,28},{28,24},{1,5},{5... | collective-permute-start | bytes 3145736 | tf_op jit(solution)/shard_map/ppermute | solution.py:400
  110.6 12.9 %copy-start.31 = (f32[1,256,1024]{2,1,0:T(8,128)}, f32[1,256,1024]{2,1,0:T(8,128)S(1)}, u32[]{:S(2)}) copy-start(f32[1,256,1024]{2,1,0:T(8,128)S(1)} %local.6.refs_7_) | copy-start | bytes 3145732
  114.1 10.4 %copy-start.14 = (f32[1,2048]{1,0:T(1,128)S(1)}, f32[1,2048]{1,0:T(1,128)}, u32[]{:S(2)}) copy-start(f32[1,2048]{1,0:T(1,128)} %fusion.38.refs_6_) | copy-start | bytes 24580
  114.1 29.8 %collective-permute-start.18 = (bf16[256,1024]{1,0:T(8,128)(2,1)}, bf16[256,1024]{1,0:T(8,128)(2,1)}, u32[]{:S(2)}, u32[]{:S(2)}) collective-permute-start(bf16[256,1024]{1,0:T(8,128)(2,1)} %fusion.20), channel_id=1, source_target_pairs={{0,8},{4,12},{8,16},{12,20},{16,24},{20,28},{1,9},{5,13},{9,17},{1... | collective-permute-start | bytes 1572872 | tf_op jit(solution)/shard_map/ppermute | solution.py:778
  124.5 19.4 %copy-start.9 = (bf16[2,256,1024]{2,1,0:T(8,128)(2,1)S(1)}, bf16[2,256,1024]{2,1,0:T(8,128)(2,1)}, u32[]{:S(2)}) copy-start(bf16[2,256,1024]{2,1,0:T(8,128)(2,1)} %copy-done.8) | copy-start | bytes 3145732
  124.5 19.4 %copy-start.57 = (f32[1,1,1024]{2,1,0:T(1,128)S(1)}, f32[1,1,1024]{2,1,0:T(1,128)}, u32[]{:S(2)}) copy-start(f32[1,1,1024]{2,1,0:T(1,128)} %get-tuple-element.141) | copy-start | bytes 12292
  126.4 12.5 %collective-permute-start.22 = (bf16[64,2048]{1,0:T(8,128)(2,1)}, bf16[64,2048]{1,0:T(8,128)(2,1)S(1)}, u32[]{:S(2)}, u32[]{:S(2)}) collective-permute-start(bf16[64,2048]{1,0:T(8,128)(2,1)} %finish.1.refs_0_), channel_id=1, source_target_pairs={{0,16},{4,20},{8,24},{12,28},{16,0},{20,4},{24,8},{28,12},{1,17},{... | collective-permute-start | bytes 786440 | tf_op jit(solution)/shard_map/ppermute | solution.py:420
  129.6 19.7 %collective-permute-start.23 = (bf16[64,2048]{1,0:T(8,128)(2,1)}, bf16[64,2048]{1,0:T(8,128)(2,1)}, u32[]{:S(2)}, u32[]{:S(2)}) collective-permute-start(bf16[64,2048]{1,0:T(8,128)(2,1)} %finish.1.refs_0_), channel_id=1, source_target_pairs={{0,8},{4,12},{8,0},{12,4},{16,24},{20,28},{24,16},{28,20},{1,9},{5... | collective-permute-start | bytes 786440 | tf_op jit(solution)/shard_map/ppermute | solution.py:420
  138.9 10.4 %copy-start.64 = (bf16[64,2048]{1,0:T(8,128)(2,1)}, bf16[64,2048]{1,0:T(8,128)(2,1)S(1)}, u32[]{:S(2)}) copy-start(bf16[64,2048]{1,0:T(8,128)(2,1)S(1)} %collective-permute-done.22.refs_1_) | copy-start | bytes 786436
  138.9 11.0 %collective-permute-start.24 = (bf16[64,2048]{1,0:T(8,128)(2,1)S(1)}, bf16[64,2048]{1,0:T(8,128)(2,1)}, u32[]{:S(2)}, u32[]{:S(2)}) collective-permute-start(bf16[64,2048]{1,0:T(8,128)(2,1)S(1)} %collective-permute-done.22.refs_1_), channel_id=1, source_target_pairs={{0,8},{4,12},{8,0},{12,4},{16,24},{20,28},{24,16},{28,20},{1,9},{5... | collective-permute-start | bytes 786440 | tf_op jit(solution)/shard_map/ppermute | solution.py:420
  147.1 12.0 %collective-permute-start.21 = (bf16[256,1024]{1,0:T(8,128)(2,1)}, bf16[256,1024]{1,0:T(8,128)(2,1)S(1)}, u32[]{:S(2)}, u32[]{:S(2)}) collective-permute-start(bf16[256,1024]{1,0:T(8,128)(2,1)} %get-tuple-element.130), channel_id=1, source_target_pairs={{0,8},{4,12},{8,16},{12,20},{16,24},{20,28},{1,9},{5,13},{9,17},{1... | collective-permute-start | bytes 1572872 | tf_op jit(solution)/shard_map/ppermute | solution.py:778
  149.3 17.2 %collective-permute-start.26 = (bf16[64,2048]{1,0:T(8,128)(2,1)S(1)}, bf16[64,2048]{1,0:T(8,128)(2,1)S(1)}, u32[]{:S(2)}, u32[]{:S(2)}) collective-permute-start(bf16[64,2048]{1,0:T(8,128)(2,1)S(1)} %collective-permute-done.22.refs_1_), channel_id=1, source_target_pairs={{0,4},{4,0},{8,12},{12,8},{16,20},{20,16},{24,28},{28,24},{1,5},{5... | collective-permute-start | bytes 786440 | tf_op jit(solution)/shard_map/ppermute | solution.py:400
  149.4 17.1 %collective-permute-start.27 = (bf16[64,2048]{1,0:T(8,128)(2,1)}, bf16[64,2048]{1,0:T(8,128)(2,1)S(1)}, u32[]{:S(2)}, u32[]{:S(2)}) collective-permute-start(bf16[64,2048]{1,0:T(8,128)(2,1)} %collective-permute-done.23.refs_2_), channel_id=1, source_target_pairs={{0,4},{4,0},{8,12},{12,8},{16,20},{20,16},{24,28},{28,24},{1,5},{5... | collective-permute-start | bytes 786440 | tf_op jit(solution)/shard_map/ppermute | solution.py:400
  149.9 16.6 %collective-permute-start.28 = (bf16[64,2048]{1,0:T(8,128)(2,1)}, bf16[64,2048]{1,0:T(8,128)(2,1)S(1)}, u32[]{:S(2)}, u32[]{:S(2)}) collective-permute-start(bf16[64,2048]{1,0:T(8,128)(2,1)} %collective-permute-done.24.refs_3_), channel_id=1, source_target_pairs={{0,4},{4,0},{8,12},{12,8},{16,20},{20,16},{24,28},{28,24},{1,5},{5... | collective-permute-start | bytes 786440 | tf_op jit(solution)/shard_map/ppermute | solution.py:400
  149.9 9.2 %copy-start.51 = (f32[1,1,1024]{2,1,0:T(1,128)S(1)}, f32[1,1,1024]{2,1,0:T(1,128)}, u32[]{:S(2)}) copy-start(f32[1,1,1024]{2,1,0:T(1,128)} %get-tuple-element.137) | copy-start | bytes 12292
  161.4 5.1 %collective-permute-start.25 = (bf16[64,2048]{1,0:T(8,128)(2,1)}, bf16[64,2048]{1,0:T(8,128)(2,1)S(1)}, u32[]{:S(2)}, u32[]{:S(2)}) collective-permute-start(bf16[64,2048]{1,0:T(8,128)(2,1)} %finish.1.refs_0_), channel_id=1, source_target_pairs={{0,4},{4,0},{8,12},{12,8},{16,20},{20,16},{24,28},{28,24},{1,5},{5... | collective-permute-start | bytes 786440 | tf_op jit(solution)/shard_map/ppermute | solution.py:400
  161.4 18.1 %collective-permute-start.30 = (bf16[256,1024]{1,0:T(8,128)(2,1)}, bf16[256,1024]{1,0:T(8,128)(2,1)}, u32[]{:S(2)}, u32[]{:S(2)}) collective-permute-start(bf16[256,1024]{1,0:T(8,128)(2,1)} %fusion.18), channel_id=1, source_target_pairs={{0,8},{4,12},{8,16},{12,20},{16,24},{20,28},{1,9},{5,13},{9,17},{1... | collective-permute-start | bytes 1572872 | tf_op jit(solution)/shard_map/ppermute | solution.py:778
  175.7 17.9 %all-to-all-start = ((f32[4,4,16,1024]{3,2,1,0:T(8,128)}), f32[4,4,16,1024]{3,2,1,0:T(8,128)S(1)}, u32[]{:S(2)}, u32[]{:S(2)}) async-start(f32[4,4,16,1024]{3,2,1,0:T(8,128)} %project.1), calls=%async_computation | async-start | bytes 2097152 | tf_op jit(solution)/shard_map/all_to_all | solution.py:816
  187.8 6.5 %collective-permute-start.31 = (bf16[128,2048]{1,0:T(8,128)(2,1)}, bf16[128,2048]{1,0:T(8,128)(2,1)S(1)}, u32[]{:S(2)}, u32[]{:S(2)}) collective-permute-start(bf16[128,2048]{1,0:T(8,128)(2,1)} %get-tuple-element.119), channel_id=1, source_target_pairs={{0,4},{4,0},{8,12},{12,8},{16,20},{20,16},{24,28},{28,24},{1,5},{5... | collective-permute-start | bytes 1572872 | tf_op jit(solution)/shard_map/ppermute | solution.py:400
  187.9 7.7 %collective-permute-start.29 = (bf16[128,2048]{1,0:T(8,128)(2,1)S(1)}, bf16[128,2048]{1,0:T(8,128)(2,1)S(1)}, u32[]{:S(2)}, u32[]{:S(2)}) collective-permute-start(bf16[128,2048]{1,0:T(8,128)(2,1)S(1)} %copy-done.63), channel_id=1, source_target_pairs={{0,4},{4,0},{8,12},{12,8},{16,20},{20,16},{24,28},{28,24},{1,5},{5... | collective-permute-start | bytes 1572872 | tf_op jit(solution)/shard_map/ppermute | solution.py:400
  (40 other events, 122.8 us)

commit v3 on v2

--- a/solution.py
+++ b/solution.py
@@ -775,6 +775,10 @@
             decay_t = lax.dynamic_index_in_dim(fronts[s][6], at_s, 0, keepdims=False)[:1]
             new = (decay_t * carry.astype(f32) + own_t).astype(bf16)
             leave = new if leave is None else jnp.where(at_k < (s + 1) * per_prompt, new, leave)
+        if t == 1:
+            local, grow, payload = window(leave)
+            blocks = [payload] + [trade(payload, k) for k in order[1:]]
+            _, leave = tied(payload, leave)
         moved = lax.ppermute(leave, "ctx", along)
         if t == 0:
             for s in range(1, prompts):
@@ -782,8 +786,6 @@
                 fronts.append(list(front(s, dt_in)))
             moved, _ = tied(moved, fronts[-1][5])
         if t == 1:
-            local, grow, payload = window(leave)
-            blocks = [payload] + [trade(payload, k) for k in order[1:]]
             moved = locals_after(payload, 1, moved)
             keep, give = read(blocks, y_local[-1])
             got = trade(give, bits[0])

time: 199 us -> 197 us (0.990)
  starting transfers between devices: 55.8 us -> 53.6 us
    ppermute x6, waiting for transfers between devices: 5.43 us -> 9 us  [shards(): moved = lax.ppermute(leave, 'ctx', along)]
    ppermute x11, waiting for transfers between devices: 21.7 us -> 18.3 us  [trade(): lax.ppermute(arr, 'ctx', [(i, (i // per ^ k) * per + i % per) for i in ra...]
    ppermute x11, starting transfers between devices: 23.1 us -> 19.9 us  [trade(): lax.ppermute(arr, 'ctx', [(i, (i // per ^ k) * per + i % per) for i in ra...]
  transfers between devices with their start and end apart: 33 -> 33, of which waited for: 9 -> 8; matrix products, arithmetic and copies ran while one was open for 13% -> 14% of each run, Pallas kernels for 26% -> 25%
where the time goes in v3:
time: 197 us; the launch traced here: 195 us
  Pallas kernels  59.4 us (30%)
  starting transfers between devices  53.6 us (27%)
  waiting for transfers between devices  33.4 us (17%)
  local copies, waits for them, and re-layouts  27.2 us (14%)
  other arithmetic  18.2 us (9%)
    ppermute x6, starting transfers between devices, shards(): moved = lax.ppermute(leave, 'ctx', along)  21.1 us
    ppermute x11, starting transfers between devices, trade(): lax.ppermute(arr, 'ctx', [(i, (i // per ^ k) * per + i % per) for i in ra...  19.9 us
    ppermute x11, waiting for transfers between devices, trade(): lax.ppermute(arr, 'ctx', [(i, (i // per ^ k) * per + i % per) for i in ra...  18.3 us
    unnamed x146, local copies, waits for them, and re-layouts  18 us
    pallas_call x4, Pallas kernels, local_part(): pl.pallas_call(functools.partial(local_kernel, hd, k), grid=(1,), in_spec...  16.3 us
    pallas_call x2, Pallas kernels, front(): pl.pallas_call(functools.partial(front_kernel, per, hd, s), grid_spec=plt...  15.6 us
    pallas_call x2, Pallas kernels, back(): pl.pallas_call(functools.partial(back_kernel, per, hd, heads), grid_spec=...  12.2 us
    ppermute x6, waiting for transfers between devices, shards(): moved = lax.ppermute(leave, 'ctx', along)  9 us
  transfers between devices with their start and end apart: 33, of which 8 were waited for; matrix products, arithmetic and copies ran while one was open for 14% of the time, Pallas kernels for 25%

profile of v3, /device:TPU:0, one launch (start us, length us, event | category | flops | bytes accessed | tf_op | source)
XLA Modules:
  0.0 195.3 jit_solution(53062065808397835)
XLA Ops:
  0.7 2.4 %constant_dynamic-slice_fusion.26 = bf16[2,128,2048]{2,1,0:T(8,128)(2,1)} fusion(bf16[2,128,4096]{2,1,0:T(8,128)(2,1)} %refs_0_.5, s32[]{:T(128)S(6)} %select_n.197), kind=kLoop, calls=%fused_computation.99 | loop fusion | bytes 2097156 | tf_op jit(solution)/shard_map/dynamic_slice | solution.py:432
  3.6 1.4 reshape.143.refs_2_
  5.0 0.7 constant_dynamic-slice_fusion.25
  10.0 1.9 copy.39
  12.1 1.3 convolution_convert_fusion.1
  16.3 4.7 %collective-permute-start.7 = (bf16[16,2560]{1,0:T(8,128)(2,1)S(1)}, bf16[16,2560]{1,0:T(8,128)(2,1)S(1)}, u32[]{:S(2)}, u32[]{:S(2)}) collective-permute-start(bf16[16,2560]{1,0:T(8,128)(2,1)S(1)} %pad_maximum_fusion.2), channel_id=1, source_target_pairs={{0,4},{4,0},{8,12},{12,8},{16,20},{20,16},{24,28},{28,24},{1,5},{5... | collective-permute-start | bytes 245768 | tf_op jit(solution)/shard_map/ppermute | solution.py:400
  21.1 0.8 collective-permute-done.7
  22.0 0.7 copy-done.20
  22.7 1.6 copy-done.4
  24.3 0.9 copy-done.21
  25.2 0.8 copy-done.23
  26.1 7.8 %front.2 = (f32[1,256,2048]{2,1,0:T(8,128)S(1)}, f32[1,256,512]{2,1,0:T(8,128)S(1)}, f32[1,32,256]{2,1,0:T(8,128)S(1)}, f32[1,32,256]{2,1,0:T(8,128)S(1)}, f32[1...) custom-call(s32[4]{0:T(128)S(1)} %pad_add_fusion.sc, ...), custom_call_target="tpu_custom_call" | custom-call | flops 9900000256 | bytes 27000000 | tf_op jit(solution)/shard_map/front/pallas_call | solution.py:522
  33.9 1.0 copy-done.8
  35.5 1.3 copy-done.29
  36.8 1.2 collective-permute-start.8
  38.0 1.1 collective-permute-start.9
  39.1 2.2 %collective-permute-start.10 = (bf16[16,2560]{1,0:T(8,128)(2,1)S(1)}, bf16[16,2560]{1,0:T(8,128)(2,1)}, u32[]{:S(2)}, u32[]{:S(2)}) collective-permute-start(bf16[16,2560]{1,0:T(8,128)(2,1)S(1)} %maximum_add_fusion.refs_5_), channel_id=1, source_target_pairs={{0,24},{4,28},{8,16},{12,20},{16,8},{20,12},{24,0},{28,4},{1,25},{... | collective-permute-start | bytes 245768 | tf_op jit(solution)/shard_map/ppermute | solution.py:420
  41.9 0.9 fusion.17
  42.8 2.9 %collective-permute-start.11 = (bf16[256,1024]{1,0:T(8,128)(2,1)}, bf16[256,1024]{1,0:T(8,128)(2,1)}, u32[]{:S(2)}, u32[]{:S(2)}) collective-permute-start(bf16[256,1024]{1,0:T(8,128)(2,1)} %fusion.17), channel_id=1, source_target_pairs={{0,8},{4,12},{8,16},{12,20},{16,24},{20,28},{1,9},{5,13},{9,17},{1... | collective-permute-start | bytes 1572872 | tf_op jit(solution)/shard_map/ppermute | solution.py:782
  45.7 0.9 reshape.151.refs_1_
  46.8 1.6 copy-done.5
  49.7 0.9 copy-done.22
  50.7 0.8 copy-done.24
  51.5 0.8 copy-done.26
  52.3 0.7 copy-done.28
  53.0 7.8 %front.3 = (f32[1,256,2048]{2,1,0:T(8,128)S(1)}, f32[1,256,512]{2,1,0:T(8,128)S(1)}, f32[1,32,256]{2,1,0:T(8,128)S(1)}, f32[1,32,256]{2,1,0:T(8,128)S(1)}, f32[1...) custom-call(s32[4]{0:T(128)S(1)} %copy-done.19, ...), custom_call_target="tpu_custom_call" | custom-call | flops 9900000256 | bytes 27000000 | tf_op jit(solution)/shard_map/front/pallas_call | solution.py:522
  61.6 1.6 fusion.16
  63.3 2.7 %window.1 = (f32[64,2048]{1,0:T(8,128)S(1)}, f32[64,128]{1,0:T(8,128)S(1)}, f32[72,384]{1,0:T(8,128)S(1)}) custom-call(s32[4]{0:T(128)S(1)} %copy-done.19, bf16[4,8,4096]{2,1,0:T(8,128)(2,1)S(1)} %copy-done.10, bf16[4,8,1024]{2,1,0:T(8,128)(2,1)S(1)} %reshape.151.refs_1_, bf16[4,8,4608]{2,1,0:T(8,128)(2,1)S(1)} %collective-permute-done.5.refs_2_.refs_5_, ...), custom_call_target="tpu_custom_call" | custom-call | flops 2200000000 | bytes 6000000 | tf_op jit(solution)/shard_map/window/pallas_call | solution.py:624
  66.0 0.8 collective-permute-start.13
  66.8 3.7 %collective-permute-start.15 = (f32[72,384]{1,0:T(8,128)S(1)}, f32[72,384]{1,0:T(8,128)S(1)}, u32[]{:S(2)}, u32[]{:S(2)}) collective-permute-start(f32[72,384]{1,0:T(8,128)S(1)} %get-tuple-element.85.refs_0_), channel_id=1, source_target_pairs={{0,24},{4,28},{8,16},{12,20},{16,8},{20,12},{24,0},{28,4},{1,25},{... | collective-permute-start | bytes 331784 | tf_op jit(solution)/shard_map/ppermute | solution.py:420
  70.4 1.5 collective-permute-start.12
  72.0 4.1 %local.4.refs_7_ = f32[1,256,1024]{2,1,0:T(8,128)S(1)} custom-call(f32[1,256,2048]{2,1,0:T(8,128)S(1)} %copy-done.30, f32[1,256,512]{2,1,0:T(8,128)S(1)} %copy-done.37, f32[1,32,256]{2,1,0:T(8,128)S(1)} %copy-done.42, f32[1,32,256]{2,1,0:T(8,128)S(1)} %copy-done.44, f32[1,256,128]{2,1,0:T(8,128)S(1)} %copy-done.40, f32[1,2048]{1,0:T(1,128)S(1)} %copy-done.13), custom_call_target="tpu_custom_call" | custom-call | flops 5500000256 | bytes 15000000 | tf_op jit(solution)/shard_map/local/pallas_call | solution.py:561
  76.6 3.1 %read.1 = (bf16[128,2048]{1,0:T(8,128)(2,1)S(1)}, bf16[128,2048]{1,0:T(8,128)(2,1)S(1)}) custom-call(s32[4]{0:T(128)S(1)} %copy-done.19, f32[72,384]{1,0:T(8,128)S(1)} %get-tuple-element.85.refs_0_, f32[72,384]{1,0:T(8,128)S(1)} %collective-permute-done.13.refs_1_, f32[72,384]{1,0:T(8,128)S(1)} %collective-permute-done.14.refs_2_, ...), custom_call_target="tpu_custom_call" | custom-call | flops 4400000000 | bytes 12000000 | tf_op jit(solution)/shard_map/read/pallas_call | solution.py:660
  79.7 2.9 %collective-permute-start.17 = (bf16[128,2048]{1,0:T(8,128)(2,1)S(1)}, bf16[128,2048]{1,0:T(8,128)(2,1)S(1)}, u32[]{:S(2)}, u32[]{:S(2)}) collective-permute-start(bf16[128,2048]{1,0:T(8,128)(2,1)S(1)} %get-tuple-element.86), channel_id=1, source_target_pairs={{0,8},{4,12},{8,0},{12,4},{16,24},{20,28},{24,16},{28,20},{1,9},{5... | collective-permute-start | bytes 1572872 | tf_op jit(solution)/shard_map/ppermute | solution.py:420
  82.6 4.1 %local.5.refs_8_ = f32[1,256,1024]{2,1,0:T(8,128)S(1)} custom-call(f32[1,256,2048]{2,1,0:T(8,128)S(1)} %copy-done.30, f32[1,256,512]{2,1,0:T(8,128)S(1)} %copy-done.37, f32[1,32,256]{2,1,0:T(8,128)S(1)} %copy-done.42, f32[1,32,256]{2,1,0:T(8,128)S(1)} %copy-done.44, f32[1,256,128]{2,1,0:T(8,128)S(1)} %copy-done.40, f32[1,2048]{1,0:T(1,128)S(1)} %copy-done.13), custom_call_target="tpu_custom_call" | custom-call | flops 5500000256 | bytes 15000000 | tf_op jit(solution)/shard_map/local/pallas_call | solution.py:561
  87.0 4.0 %collective-permute-start.16 = (bf16[256,1024]{1,0:T(8,128)(2,1)S(1)}, bf16[256,1024]{1,0:T(8,128)(2,1)S(1)}, u32[]{:S(2)}, u32[]{:S(2)}) collective-permute-start(bf16[256,1024]{1,0:T(8,128)(2,1)S(1)} %fusion.21), channel_id=1, source_target_pairs={{0,8},{4,12},{8,16},{12,20},{16,24},{20,28},{1,9},{5,13},{9,17},{1... | collective-permute-start | bytes 1572872 | tf_op jit(solution)/shard_map/ppermute | solution.py:782
  91.1 6.4 %collective-permute-done.17 = bf16[128,2048]{1,0:T(8,128)(2,1)S(1)} collective-permute-done((bf16[128,2048]{1,0:T(8,128)(2,1)S(1)}, bf16[128,2048]{1,0:T(8,128)(2,1)S(1)}, u32[]{:S(2)}, u32[]{:S(2)}) %collective-permute-start.17) | collective-permute-done | bytes 524320 | tf_op jit(solution)/shard_map/ppermute | solution.py:420
  97.6 1.2 collective-permute-start.19
  98.8 1.1 constant_dynamic-slice_fusion.2
  99.9 4.1 %local.6.refs_7_ = f32[1,256,1024]{2,1,0:T(8,128)S(1)} custom-call(f32[1,256,2048]{2,1,0:T(8,128)S(1)} %get-tuple-element.97.act, f32[1,256,512]{2,1,0:T(8,128)S(1)} %get-tuple-element.93.bc.refs_4_, f32[1,32,256]{2,1,0:T(8,128)S(1)} %get-tuple-element.94.run, f32[1,32,256]{2,1,0:T(8,128)S(1)} %get-tuple-element.95.step, ...), custom_call_target="tpu_custom_call" | custom-call | flops 5500000256 | bytes 15000000 | tf_op jit(solution)/shard_map/local/pallas_call | solution.py:561
  104.0 4.7 %collective-permute-done.16 = bf16[256,1024]{1,0:T(8,128)(2,1)S(1)} collective-permute-done((bf16[256,1024]{1,0:T(8,128)(2,1)S(1)}, bf16[256,1024]{1,0:T(8,128)(2,1)S(1)}, u32[]{:S(2)}, u32[]{:S(2)}) %collective-permute-start.16) | collective-permute-done | bytes 524320 | tf_op jit(solution)/shard_map/ppermute | solution.py:782
  108.7 1.1 fusion.20
  109.8 5.3 %collective-permute-start.18 = (bf16[256,1024]{1,0:T(8,128)(2,1)}, bf16[256,1024]{1,0:T(8,128)(2,1)}, u32[]{:S(2)}, u32[]{:S(2)}) collective-permute-start(bf16[256,1024]{1,0:T(8,128)(2,1)} %fusion.20), channel_id=1, source_target_pairs={{0,8},{4,12},{8,16},{12,20},{16,24},{20,28},{1,9},{5,13},{9,17},{1... | collective-permute-start | bytes 1572872 | tf_op jit(solution)/shard_map/ppermute | solution.py:782
  115.1 4.1 %local.7.refs_8_ = f32[1,256,1024]{2,1,0:T(8,128)S(1)} custom-call(f32[1,256,2048]{2,1,0:T(8,128)S(1)} %get-tuple-element.97.act, f32[1,256,512]{2,1,0:T(8,128)S(1)} %get-tuple-element.93.bc.refs_4_, f32[1,32,256]{2,1,0:T(8,128)S(1)} %get-tuple-element.94.run, f32[1,32,256]{2,1,0:T(8,128)S(1)} %get-tuple-element.95.step, ...), custom_call_target="tpu_custom_call" | custom-call | flops 5500000256 | bytes 15000000 | tf_op jit(solution)/shard_map/local/pallas_call | solution.py:561
  119.2 1.0 copy-done.32
  120.2 1.9 finish.1.refs_0_
  122.1 5.1 %collective-permute-start.22 = (bf16[64,2048]{1,0:T(8,128)(2,1)}, bf16[64,2048]{1,0:T(8,128)(2,1)S(1)}, u32[]{:S(2)}, u32[]{:S(2)}) collective-permute-start(bf16[64,2048]{1,0:T(8,128)(2,1)} %finish.1.refs_0_), channel_id=1, source_target_pairs={{0,16},{4,20},{8,24},{12,28},{16,0},{20,4},{24,8},{28,12},{1,17},{... | collective-permute-start | bytes 786440 | tf_op jit(solution)/shard_map/ppermute | solution.py:420
  127.2 11.3 %collective-permute-done.22.refs_1_ = bf16[64,2048]{1,0:T(8,128)(2,1)S(1)} collective-permute-done((bf16[64,2048]{1,0:T(8,128)(2,1)}, bf16[64,2048]{1,0:T(8,128)(2,1)S(1)}, u32[]{:S(2)}, u32[]{:S(2)}) %collective-permute-start.22) | collective-permute-done | bytes 262176 | tf_op jit(solution)/shard_map/ppermute | solution.py:420
  138.5 1.9 collective-permute-start.24
  140.4 3.2 %fusion.30 = (bf16[1,256,1024]{2,1,0:T(8,128)(2,1)}, bf16[1,256,1024]{2,1,0:T(8,128)(2,1)}, bf16[256,1024]{1,0:T(8,128)(2,1)}) fusion(bf16[256,1024]{1,0:T(8,128)(2,1)} %collective-permute-done.18, bf16[256,1024]{1,0:T(8,128)(2,1)} %copy-done.45, bf16[256,1024]{1,0:T(8,128)(2,1)} %copy-done.47, bf16[2,256,1024]{2,1,0:T(8,128)(2,1)S(1)} %copy-done.9, ...), kind=kLoop, calls=%fused_computation.49 | loop fusion | flops 3670016 | bytes 6823948 | tf_op jit(solution)/shard_map/broadcast_in_dim | solution.py:746
  143.6 2.2 %collective-permute-start.21 = (bf16[256,1024]{1,0:T(8,128)(2,1)}, bf16[256,1024]{1,0:T(8,128)(2,1)S(1)}, u32[]{:S(2)}, u32[]{:S(2)}) collective-permute-start(bf16[256,1024]{1,0:T(8,128)(2,1)} %get-tuple-element.132), channel_id=1, source_target_pairs={{0,8},{4,12},{8,16},{12,20},{16,24},{20,28},{1,9},{5,13},{9,17},{1... | collective-permute-start | bytes 1572872 | tf_op jit(solution)/shard_map/ppermute | solution.py:782
  146.6 6.1 %back.2 = (bf16[128,2048]{1,0:T(8,128)(2,1)}, bf16[128,2048]{1,0:T(8,128)(2,1)}) custom-call(s32[4]{0:T(128)} %copy-done.18, bf16[2,128,4096]{2,1,0:T(8,128)(2,1)} %refs_0_.8, bf16[2,128,2048]{2,1,0:T(8,128)(2,1)} %collective-permute-done.20.refs_1_, bf16[1,256,1024]{2,1,0:T(8,128)(2,1)} %get-tuple-element.125.refs_2_, ...), custom_call_target="tpu_custom_call" | custom-call | flops 5500000256 | bytes 15000000 | tf_op jit(solution)/shard_map/back/pallas_call | solution.py:723
  152.7 4.3 %collective-permute-done.21 = bf16[256,1024]{1,0:T(8,128)(2,1)S(1)} collective-permute-done((bf16[256,1024]{1,0:T(8,128)(2,1)}, bf16[256,1024]{1,0:T(8,128)(2,1)S(1)}, u32[]{:S(2)}, u32[]{:S(2)}) %collective-permute-start.21) | collective-permute-done | bytes 524320 | tf_op jit(solution)/shard_map/ppermute | solution.py:782
  157.0 2.3 %fusion.18 = bf16[256,1024]{1,0:T(8,128)(2,1)} fusion(f32[2,256,1024]{2,1,0:T(8,128)} %copy-done.2, s32[]{:T(128)S(6)} %min.64, bf16[256,1024]{1,0:T(8,128)(2,1)S(1)} %collective-permute-done.21, f32[2,256,1024]{2,1,0:T(8,128)S(1)} %get-tuple-element.63.refs_4_, s32[]{:T(128)S(6)} %min.52, f32[1024]{0:T(1024)S(1)} %bitcast.152, f32[1024]{0:T(1024)S(1)} %bitcast.151, ...), kind=kLoop, calls=%fused_computation.34 | loop fusion | flops 2097152 | bytes 3153929 | tf_op jit(solution)/shard_map/jit(_where)/select_n | solution.py:777
  159.3 5.1 %collective-permute-start.30 = (bf16[256,1024]{1,0:T(8,128)(2,1)}, bf16[256,1024]{1,0:T(8,128)(2,1)}, u32[]{:S(2)}, u32[]{:S(2)}) collective-permute-start(bf16[256,1024]{1,0:T(8,128)(2,1)} %fusion.18), channel_id=1, source_target_pairs={{0,8},{4,12},{8,16},{12,20},{16,24},{20,28},{1,9},{5,13},{9,17},{1... | collective-permute-start | bytes 1572872 | tf_op jit(solution)/shard_map/ppermute | solution.py:782
  165.3 0.7 copy-done.68
  166.0 7.6 %project.1 = f32[4,4,16,1024]{3,2,1,0:T(8,128)} custom-call(s32[4]{0:T(128)} %copy-done.18, bf16[64,2048]{1,0:T(8,128)(2,1)} %finish.1.refs_0_, bf16[64,2048]{1,0:T(8,128)(2,1)} %copy-done.64, bf16[64,2048]{1,0:T(8,128)(2,1)} %collective-permute-done.23.refs_2_, bf16[64,2048]{1,0:T(8,128)(2,1)} %collective-permute-done.24.refs_3_, ...), custom_call_target="tpu_custom_call" | custom-call | flops 6600000000 | bytes 18000000 | tf_op jit(solution)/shard_map/project/pallas_call | solution.py:695
  173.6 3.9 %all-to-all-start = ((f32[4,4,16,1024]{3,2,1,0:T(8,128)}), f32[4,4,16,1024]{3,2,1,0:T(8,128)S(1)}, u32[]{:S(2)}, u32[]{:S(2)}) async-start(f32[4,4,16,1024]{3,2,1,0:T(8,128)} %project.1), calls=%async_computation | async-start | bytes 2097152 | tf_op jit(solution)/shard_map/all_to_all | solution.py:818
  177.4 2.2 %fusion.24 = (bf16[1,256,1024]{2,1,0:T(8,128)(2,1)}, bf16[1,256,1024]{2,1,0:T(8,128)(2,1)}) fusion(bf16[256,1024]{1,0:T(8,128)(2,1)} %collective-permute-done.30, bf16[256,1024]{1,0:T(8,128)(2,1)S(1)} %collective-permute-done.21, bf16[256,1024]{1,0:T(8,128)(2,1)} %collective-permute-done.18, bf16[2,256,1024]{2,1,0:T(8,128)(2,1)S(1)} %copy-done.7, ...), kind=kLoop, calls=%fused_computation.41 | loop fusion | flops 1572864 | bytes 4194307 | tf_op jit(solution)/shard_map/broadcast_in_dim | solution.py:746
  179.6 6.1 %back.3 = (bf16[128,2048]{1,0:T(8,128)(2,1)}, bf16[128,2048]{1,0:T(8,128)(2,1)}) custom-call(s32[4]{0:T(128)} %copy-done.18, bf16[2,128,4096]{2,1,0:T(8,128)(2,1)} %refs_0_.8, bf16[2,128,2048]{2,1,0:T(8,128)(2,1)} %collective-permute-done.20.refs_1_, bf16[1,256,1024]{2,1,0:T(8,128)(2,1)} %get-tuple-element.123.refs_2_, ...), custom_call_target="tpu_custom_call" | custom-call | flops 5500000256 | bytes 15000000 | tf_op jit(solution)/shard_map/back/pallas_call | solution.py:723
  186.3 5.3 %all-to-all-done = f32[4,4,16,1024]{3,2,1,0:T(8,128)S(1)} async-done(((f32[4,4,16,1024]{3,2,1,0:T(8,128)}), f32[4,4,16,1024]{3,2,1,0:T(8,128)S(1)}, u32[]{:S(2)}, u32[]{:S(2)}) %all-to-all-start) | async-done | bytes 1048608 | tf_op jit(solution)/shard_map/all_to_all | solution.py:818
  191.5 0.7 reduce_sum.9
  192.3 1.2 broadcast_select_fusion.1
  193.8 1.5 pad_maximum_fusion
  (229 shorter events, 14.5 us)
Async XLA Ops:
  0.6 13.3 %copy-start = (f32[4096]{0:T(1024)S(1)}, f32[4096]{0:T(1024)}, u32[]{:S(2)}) copy-start(f32[4096]{0:T(1024)} %param.33) | copy-start | bytes 49156
  0.7 9.0 %copy-start.69 = (f32[64]{0:T(128)S(1)}, f32[64]{0:T(128)}, u32[]{:S(2)}) copy-start(f32[64]{0:T(128)} %param.26) | copy-start | bytes 772
  0.7 9.0 %copy-start.50 = (bf16[2,3,4096]{2,0,1:T(2,128)(2,1)S(1)}, bf16[2,3,4096]{2,0,1:T(2,128)(2,1)}, u32[]{:S(2)}) copy-start(bf16[2,3,4096]{2,0,1:T(2,128)(2,1)} %param.35) | copy-start | bytes 147460
  0.7 9.1 %copy-start.58 = (bf16[2,3,2,512]{3,2,1,0:T(2,128)(2,1)S(1)}, bf16[2,3,2,512]{3,2,1,0:T(2,128)(2,1)}, u32[]{:S(2)}) copy-start(bf16[2,3,2,512]{3,2,1,0:T(2,128)(2,1)} %param.36) | copy-start | bytes 36868
  0.7 9.2 %copy-start.61 = (f32[64]{0:T(128)S(1)}, f32[64]{0:T(128)}, u32[]{:S(2)}) copy-start(f32[64]{0:T(128)} %param.27) | copy-start | bytes 772
  3.2 8.8 %copy-start.60 = (s32[2]{0:T(128)S(1)}, s32[2]{0:T(128)}, u32[]{:S(2)}) copy-start(s32[2]{0:T(128)} %param.37) | copy-start | bytes 28
  3.2 19.5 %collective-permute-start = (bf16[2,128,2048]{2,1,0:T(8,128)(2,1)}, bf16[2,128,2048]{2,1,0:T(8,128)(2,1)}, u32[]{:S(2)}, u32[]{:S(2)}) collective-permute-start(bf16[2,128,2048]{2,1,0:T(8,128)(2,1)} %constant_dynamic-slice_fusion.26), channel_id=1, source_target_pairs={{0,4},{4,0},{8,12},{12,8},{16,20},{20,16},{24,28},{28,24},{1,5},{5... | collective-permute-start | bytes 3145736 | tf_op jit(solution)/shard_map/ppermute | solution.py:400
  5.8 16.2 %collective-permute-start.1 = (bf16[2,128,512]{2,1,0:T(8,128)(2,1)}, bf16[2,128,512]{2,1,0:T(8,128)(2,1)S(1)}, u32[]{:S(2)}, u32[]{:S(2)}) collective-permute-start(bf16[2,128,512]{2,1,0:T(8,128)(2,1)} %constant_dynamic-slice_fusion.25), channel_id=1, source_target_pairs={{0,4},{4,0},{8,12},{12,8},{16,20},{20,16},{24,28},{28,24},{1,5},{5... | collective-permute-start | bytes 786440 | tf_op jit(solution)/shard_map/ppermute | solution.py:400
  6.5 15.5 %collective-permute-start.2 = (f32[2,32,128]{2,1,0:T(8,128)}, f32[2,32,128]{2,1,0:T(8,128)S(1)}, u32[]{:S(2)}, u32[]{:S(2)}) collective-permute-start(f32[2,32,128]{2,1,0:T(8,128)} %constant_dynamic-slice_fusion.24), channel_id=1, source_target_pairs={{0,4},{4,0},{8,12},{12,8},{16,20},{20,16},{24,28},{28,24},{1,5},{5... | collective-permute-start | bytes 98312 | tf_op jit(solution)/shard_map/ppermute | solution.py:400
  7.6 8.6 %collective-permute-start.3 = (bf16[2,3,2560]{2,1,0:T(4,128)(2,1)}, bf16[2,3,2560]{2,1,0:T(4,128)(2,1)S(1)}, u32[]{:S(2)}, u32[]{:S(2)}) collective-permute-start(bf16[2,3,2560]{2,1,0:T(4,128)(2,1)} %pad_maximum_fusion.3), channel_id=1, source_target_pairs={{4,12},{12,20},{20,28},{5,13},{13,21},{21,29},{6,14},{14,22},{22,3... | collective-permute-start | bytes 92168 | tf_op jit(solution)/shard_map/ppermute | solution.py:445
  8.9 12.1 %collective-permute-start.4 = (bf16[2,3,2560]{2,1,0:T(4,128)(2,1)}, bf16[2,3,2560]{2,1,0:T(4,128)(2,1)S(1)}, u32[]{:S(2)}, u32[]{:S(2)}) collective-permute-start(bf16[2,3,2560]{2,1,0:T(4,128)(2,1)} %pad_maximum_fusion.4), channel_id=1, source_target_pairs={{4,8},{12,16},{20,24},{5,9},{13,17},{21,25},{6,10},{14,18},{22,26}... | collective-permute-start | bytes 92168 | tf_op jit(solution)/shard_map/ppermute | solution.py:445
  13.4 9.3 %copy-start.27 = (f32[4096]{0:T(1024)S(1)}, f32[4096]{0:T(1024)}, u32[]{:S(2)}) copy-start(f32[4096]{0:T(1024)} %param.31) | copy-start | bytes 49156
  15.2 18.7 %copy-start.18 = (s32[4]{0:T(128)}, s32[4]{0:T(128)S(1)}, u32[]{:S(2)}) copy-start(s32[4]{0:T(128)S(1)} %pad_add_fusion.sc) | copy-start | bytes 52
  15.4 18.5 %copy-start.16 = (f32[1,1,2,512]{3,1,2,0:T(1,128)}, f32[1,1,2,512]{3,1,2,0:T(1,128)S(1)}, u32[]{:S(2)}) copy-start(f32[1,1,2,512]{3,1,2,0:T(1,128)S(1)} %copy.38) | copy-start | bytes 12292
  16.3 5.7 %collective-permute-start.7 = (bf16[16,2560]{1,0:T(8,128)(2,1)S(1)}, bf16[16,2560]{1,0:T(8,128)(2,1)S(1)}, u32[]{:S(2)}, u32[]{:S(2)}) collective-permute-start(bf16[16,2560]{1,0:T(8,128)(2,1)S(1)} %pad_maximum_fusion.2), channel_id=1, source_target_pairs={{0,4},{4,0},{8,12},{12,8},{16,20},{20,16},{24,28},{28,24},{1,5},{5... | collective-permute-start | bytes 245768 | tf_op jit(solution)/shard_map/ppermute | solution.py:400
  26.1 20.6 %copy-start.10 = (bf16[4,8,4096]{2,1,0:T(8,128)(2,1)S(1)}, bf16[4,8,4096]{2,1,0:T(8,128)(2,1)}, u32[]{:S(2)}) copy-start(bf16[4,8,4096]{2,1,0:T(8,128)(2,1)} %refs_0_.6) | copy-start | bytes 786436
  26.1 20.6 %copy-start.11 = (bf16[4,8,4096]{2,1,0:T(8,128)(2,1)S(1)}, bf16[4,8,4096]{2,1,0:T(8,128)(2,1)}, u32[]{:S(2)}) copy-start(bf16[4,8,4096]{2,1,0:T(8,128)(2,1)} %refs_4_.4) | copy-start | bytes 786436
  36.8 26.4 %collective-permute-start.8 = (bf16[16,2560]{1,0:T(8,128)(2,1)S(1)}, bf16[16,2560]{1,0:T(8,128)(2,1)}, u32[]{:S(2)}, u32[]{:S(2)}) collective-permute-start(bf16[16,2560]{1,0:T(8,128)(2,1)S(1)} %maximum_add_fusion.refs_5_), channel_id=1, source_target_pairs={{0,8},{4,12},{8,0},{12,4},{16,24},{20,28},{24,16},{28,20},{1,9},{5... | collective-permute-start | bytes 245768 | tf_op jit(solution)/shard_map/ppermute | solution.py:420
  38.0 25.2 %collective-permute-start.9 = (bf16[16,2560]{1,0:T(8,128)(2,1)S(1)}, bf16[16,2560]{1,0:T(8,128)(2,1)}, u32[]{:S(2)}, u32[]{:S(2)}) collective-permute-start(bf16[16,2560]{1,0:T(8,128)(2,1)S(1)} %maximum_add_fusion.refs_5_), channel_id=1, source_target_pairs={{0,16},{4,20},{8,24},{12,28},{16,0},{20,4},{24,8},{28,12},{1,17},{... | collective-permute-start | bytes 245768 | tf_op jit(solution)/shard_map/ppermute | solution.py:420
  39.1 24.1 %collective-permute-start.10 = (bf16[16,2560]{1,0:T(8,128)(2,1)S(1)}, bf16[16,2560]{1,0:T(8,128)(2,1)}, u32[]{:S(2)}, u32[]{:S(2)}) collective-permute-start(bf16[16,2560]{1,0:T(8,128)(2,1)S(1)} %maximum_add_fusion.refs_5_), channel_id=1, source_target_pairs={{0,24},{4,28},{8,16},{12,20},{16,8},{20,12},{24,0},{28,4},{1,25},{... | collective-permute-start | bytes 245768 | tf_op jit(solution)/shard_map/ppermute | solution.py:420
  42.8 18.2 %collective-permute-start.11 = (bf16[256,1024]{1,0:T(8,128)(2,1)}, bf16[256,1024]{1,0:T(8,128)(2,1)}, u32[]{:S(2)}, u32[]{:S(2)}) collective-permute-start(bf16[256,1024]{1,0:T(8,128)(2,1)} %fusion.17), channel_id=1, source_target_pairs={{0,8},{4,12},{8,16},{12,20},{16,24},{20,28},{1,9},{5,13},{9,17},{1... | collective-permute-start | bytes 1572872 | tf_op jit(solution)/shard_map/ppermute | solution.py:782
  46.7 16.5 %collective-permute-start.5 = (bf16[4,8,4608]{2,1,0:T(8,128)(2,1)S(1)}, bf16[4,8,4608]{2,1,0:T(8,128)(2,1)S(1)}, u32[]{:S(2)}, u32[]{:S(2)}) collective-permute-start(bf16[4,8,4608]{2,1,0:T(8,128)(2,1)S(1)} %pad_maximum_fusion.1), channel_id=1, source_target_pairs={{0,4},{4,0},{8,12},{12,8},{16,20},{20,16},{24,28},{28,24},{1,5},{5... | collective-permute-start | bytes 884744 | tf_op jit(solution)/shard_map/ppermute | solution.py:400
  53.0 7.8 %copy-start.70 = (s32[8]{0:T(128)S(1)}, s32[8]{0:T(128)}, u32[]{:S(2)}) copy-start(s32[8]{0:T(128)} %param.42) | copy-start | bytes 100
  53.0 8.0 %copy-start.56 = (f32[4,64,8]{1,2,0:T(8,128)S(1)}, f32[4,64,8]{1,2,0:T(8,128)}, u32[]{:S(2)}) copy-start(f32[4,64,8]{1,2,0:T(8,128)} %param.41) | copy-start | bytes 24580
  53.0 8.6 %copy-start.54 = (f32[1,1,1024]{2,1,0:T(1,128)S(1)}, f32[1,1,1024]{2,1,0:T(1,128)}, u32[]{:S(2)}) copy-start(f32[1,1,1024]{2,1,0:T(1,128)} %get-tuple-element.140) | copy-start | bytes 12292
  60.8 47.8 %copy-start.2 = (f32[2,256,1024]{2,1,0:T(8,128)}, f32[2,256,1024]{2,1,0:T(8,128)S(1)}, u32[]{:S(2)}) copy-start(f32[2,256,1024]{2,1,0:T(8,128)S(1)} %get-tuple-element.74.refs_5_) | copy-start | bytes 6291460
  60.9 54.2 %copy-start.35 = (f32[1,256,512]{2,1,0:T(8,128)}, f32[1,256,512]{2,1,0:T(8,128)S(1)}, u32[]{:S(2)}) copy-start(f32[1,256,512]{2,1,0:T(8,128)S(1)} %get-tuple-element.93.bc.refs_4_) | copy-start | bytes 1572868
  60.9 54.2 %copy-start.38 = (f32[1,256,128]{2,1,0:T(8,128)}, f32[1,256,128]{2,1,0:T(8,128)S(1)}, u32[]{:S(2)}) copy-start(f32[1,256,128]{2,1,0:T(8,128)S(1)} %get-tuple-element.118.refs_10_.pack.refs_5_) | copy-start | bytes 393220
  61.0 2.2 %collective-permute-start.6 = (f32[5,8,128]{2,1,0:T(8,128)S(1)}, f32[5,8,128]{2,1,0:T(8,128)S(1)}, u32[]{:S(2)}, u32[]{:S(2)}) collective-permute-start(f32[5,8,128]{2,1,0:T(8,128)S(1)} %select_maximum_fusion.refs_3_), channel_id=1, source_target_pairs={{0,4},{4,0},{8,12},{12,8},{16,20},{20,16},{24,28},{28,24},{1,5},{5... | collective-permute-start | bytes 61448 | tf_op jit(solution)/shard_map/ppermute | solution.py:400
  63.2 8.7 %copy-start.13 = (f32[1,2048]{1,0:T(1,128)S(1)}, f32[1,2048]{1,0:T(1,128)}, u32[]{:S(2)}) copy-start(f32[1,2048]{1,0:T(1,128)} %broadcast_in_dim_reshape.3.skip) | copy-start | bytes 24580
  63.3 8.7 %copy-start.30 = (f32[1,256,2048]{2,1,0:T(8,128)S(1)}, f32[1,256,2048]{2,1,0:T(8,128)}, u32[]{:S(2)}) copy-start(f32[1,256,2048]{2,1,0:T(8,128)} %copy-done.29) | copy-start | bytes 6291460
  63.3 8.7 %copy-start.37 = (f32[1,256,512]{2,1,0:T(8,128)S(1)}, f32[1,256,512]{2,1,0:T(8,128)}, u32[]{:S(2)}) copy-start(f32[1,256,512]{2,1,0:T(8,128)} %copy-done.36) | copy-start | bytes 1572868
  63.3 8.7 %copy-start.42 = (f32[1,32,256]{2,1,0:T(8,128)S(1)}, f32[1,32,256]{2,1,0:T(8,128)}, u32[]{:S(2)}) copy-start(f32[1,32,256]{2,1,0:T(8,128)} %copy-done.41) | copy-start | bytes 98308
  63.3 8.7 %copy-start.44 = (f32[1,32,256]{2,1,0:T(8,128)S(1)}, f32[1,32,256]{2,1,0:T(8,128)}, u32[]{:S(2)}) copy-start(f32[1,32,256]{2,1,0:T(8,128)} %copy-done.43) | copy-start | bytes 98308
  66.0 10.1 %collective-permute-start.13 = (f32[72,384]{1,0:T(8,128)S(1)}, f32[72,384]{1,0:T(8,128)S(1)}, u32[]{:S(2)}, u32[]{:S(2)}) collective-permute-start(f32[72,384]{1,0:T(8,128)S(1)} %get-tuple-element.85.refs_0_), channel_id=1, source_target_pairs={{0,16},{4,20},{8,24},{12,28},{16,0},{20,4},{24,8},{28,12},{1,17},{... | collective-permute-start | bytes 331784 | tf_op jit(solution)/shard_map/ppermute | solution.py:420
  66.8 9.3 %collective-permute-start.14 = (f32[72,384]{1,0:T(8,128)S(1)}, f32[72,384]{1,0:T(8,128)S(1)}, u32[]{:S(2)}, u32[]{:S(2)}) collective-permute-start(f32[72,384]{1,0:T(8,128)S(1)} %get-tuple-element.85.refs_0_), channel_id=1, source_target_pairs={{0,8},{4,12},{8,0},{12,4},{16,24},{20,28},{24,16},{28,20},{1,9},{5... | collective-permute-start | bytes 331784 | tf_op jit(solution)/shard_map/ppermute | solution.py:420
  66.8 9.8 %collective-permute-start.15 = (f32[72,384]{1,0:T(8,128)S(1)}, f32[72,384]{1,0:T(8,128)S(1)}, u32[]{:S(2)}, u32[]{:S(2)}) collective-permute-start(f32[72,384]{1,0:T(8,128)S(1)} %get-tuple-element.85.refs_0_), channel_id=1, source_target_pairs={{0,24},{4,28},{8,16},{12,20},{16,8},{20,12},{24,0},{28,4},{1,25},{... | collective-permute-start | bytes 331784 | tf_op jit(solution)/shard_map/ppermute | solution.py:420
  70.4 16.3 %collective-permute-start.12 = (bf16[256,1024]{1,0:T(8,128)(2,1)S(1)}, bf16[256,1024]{1,0:T(8,128)(2,1)S(1)}, u32[]{:S(2)}, u32[]{:S(2)}) collective-permute-start(bf16[256,1024]{1,0:T(8,128)(2,1)S(1)} %fusion.16), channel_id=1, source_target_pairs={{0,8},{4,12},{8,16},{12,20},{16,24},{20,28},{1,9},{5,13},{9,17},{1... | collective-permute-start | bytes 1572872 | tf_op jit(solution)/shard_map/ppermute | solution.py:782
  79.7 17.7 %collective-permute-start.17 = (bf16[128,2048]{1,0:T(8,128)(2,1)S(1)}, bf16[128,2048]{1,0:T(8,128)(2,1)S(1)}, u32[]{:S(2)}, u32[]{:S(2)}) collective-permute-start(bf16[128,2048]{1,0:T(8,128)(2,1)S(1)} %get-tuple-element.86), channel_id=1, source_target_pairs={{0,8},{4,12},{8,0},{12,4},{16,24},{20,28},{24,16},{28,20},{1,9},{5... | collective-permute-start | bytes 1572872 | tf_op jit(solution)/shard_map/ppermute | solution.py:420
  86.7 10.9 %copy-start.34 = (f32[1,256,1024]{2,1,0:T(8,128)}, f32[1,256,1024]{2,1,0:T(8,128)S(1)}, u32[]{:S(2)}) copy-start(f32[1,256,1024]{2,1,0:T(8,128)S(1)} %local.5.refs_8_) | copy-start | bytes 3145732
  86.7 10.9 %copy-start.47 = (bf16[256,1024]{1,0:T(8,128)(2,1)}, bf16[256,1024]{1,0:T(8,128)(2,1)S(1)}, u32[]{:S(2)}) copy-start(bf16[256,1024]{1,0:T(8,128)(2,1)S(1)} %collective-permute-done.12) | copy-start | bytes 1572868
  87.0 11.8 %copy-start.49 = (bf16[2,128,4096]{2,1,0:T(8,128)(2,1)S(1)}, bf16[2,128,4096]{2,1,0:T(8,128)(2,1)}, u32[]{:S(2)}) copy-start(bf16[2,128,4096]{2,1,0:T(8,128)(2,1)} %refs_0_.8) | copy-start | bytes 6291460
  87.0 21.7 %collective-permute-start.16 = (bf16[256,1024]{1,0:T(8,128)(2,1)S(1)}, bf16[256,1024]{1,0:T(8,128)(2,1)S(1)}, u32[]{:S(2)}, u32[]{:S(2)}) collective-permute-start(bf16[256,1024]{1,0:T(8,128)(2,1)S(1)} %fusion.21), channel_id=1, source_target_pairs={{0,8},{4,12},{8,16},{12,20},{16,24},{20,28},{1,9},{5,13},{9,17},{1... | collective-permute-start | bytes 1572872 | tf_op jit(solution)/shard_map/ppermute | solution.py:782
  97.6 22.5 %collective-permute-start.19 = (bf16[64,2048]{1,0:T(8,128)(2,1)S(1)}, bf16[64,2048]{1,0:T(8,128)(2,1)S(1)}, u32[]{:S(2)}, u32[]{:S(2)}) collective-permute-start(bf16[64,2048]{1,0:T(8,128)(2,1)S(1)} %get-tuple-element.134), channel_id=1, source_target_pairs={{0,16},{4,20},{8,24},{12,28},{16,0},{20,4},{24,8},{28,12},{1,17},{... | collective-permute-start | bytes 786440 | tf_op jit(solution)/shard_map/ppermute | solution.py:420
  99.9 40.5 %collective-permute-start.20 = (bf16[2,128,2048]{2,1,0:T(8,128)(2,1)}, bf16[2,128,2048]{2,1,0:T(8,128)(2,1)}, u32[]{:S(2)}, u32[]{:S(2)}) collective-permute-start(bf16[2,128,2048]{2,1,0:T(8,128)(2,1)} %constant_dynamic-slice_fusion.2), channel_id=1, source_target_pairs={{0,4},{4,0},{8,12},{12,8},{16,20},{20,16},{24,28},{28,24},{1,5},{5... | collective-permute-start | bytes 3145736 | tf_op jit(solution)/shard_map/ppermute | solution.py:400
  99.9 8.8 %copy-start.52 = (f32[1,1,1024]{2,1,0:T(1,128)S(1)}, f32[1,1,1024]{2,1,0:T(1,128)}, u32[]{:S(2)}) copy-start(f32[1,1,1024]{2,1,0:T(1,128)} %get-tuple-element.142) | copy-start | bytes 12292
  104.0 15.2 %copy-start.31 = (f32[1,256,1024]{2,1,0:T(8,128)}, f32[1,256,1024]{2,1,0:T(8,128)S(1)}, u32[]{:S(2)}) copy-start(f32[1,256,1024]{2,1,0:T(8,128)S(1)} %local.6.refs_7_) | copy-start | bytes 3145732
  109.8 10.4 %copy-start.14 = (f32[1,2048]{1,0:T(1,128)S(1)}, f32[1,2048]{1,0:T(1,128)}, u32[]{:S(2)}) copy-start(f32[1,2048]{1,0:T(1,128)} %fusion.38.refs_6_) | copy-start | bytes 24580
  109.8 30.6 %collective-permute-start.18 = (bf16[256,1024]{1,0:T(8,128)(2,1)}, bf16[256,1024]{1,0:T(8,128)(2,1)}, u32[]{:S(2)}, u32[]{:S(2)}) collective-permute-start(bf16[256,1024]{1,0:T(8,128)(2,1)} %fusion.20), channel_id=1, source_target_pairs={{0,8},{4,12},{8,16},{12,20},{16,24},{20,28},{1,9},{5,13},{9,17},{1... | collective-permute-start | bytes 1572872 | tf_op jit(solution)/shard_map/ppermute | solution.py:782
  120.2 20.2 %copy-start.9 = (bf16[2,256,1024]{2,1,0:T(8,128)(2,1)S(1)}, bf16[2,256,1024]{2,1,0:T(8,128)(2,1)}, u32[]{:S(2)}) copy-start(bf16[2,256,1024]{2,1,0:T(8,128)(2,1)} %copy-done.8) | copy-start | bytes 3145732
  120.2 20.2 %copy-start.57 = (f32[1,1,1024]{2,1,0:T(1,128)S(1)}, f32[1,1,1024]{2,1,0:T(1,128)}, u32[]{:S(2)}) copy-start(f32[1,1,1024]{2,1,0:T(1,128)} %get-tuple-element.143) | copy-start | bytes 12292
  122.1 16.4 %collective-permute-start.22 = (bf16[64,2048]{1,0:T(8,128)(2,1)}, bf16[64,2048]{1,0:T(8,128)(2,1)S(1)}, u32[]{:S(2)}, u32[]{:S(2)}) collective-permute-start(bf16[64,2048]{1,0:T(8,128)(2,1)} %finish.1.refs_0_), channel_id=1, source_target_pairs={{0,16},{4,20},{8,24},{12,28},{16,0},{20,4},{24,8},{28,12},{1,17},{... | collective-permute-start | bytes 786440 | tf_op jit(solution)/shard_map/ppermute | solution.py:420
  127.2 18.8 %collective-permute-start.23 = (bf16[64,2048]{1,0:T(8,128)(2,1)}, bf16[64,2048]{1,0:T(8,128)(2,1)}, u32[]{:S(2)}, u32[]{:S(2)}) collective-permute-start(bf16[64,2048]{1,0:T(8,128)(2,1)} %finish.1.refs_0_), channel_id=1, source_target_pairs={{0,8},{4,12},{8,0},{12,4},{16,24},{20,28},{24,16},{28,20},{1,9},{5... | collective-permute-start | bytes 786440 | tf_op jit(solution)/shard_map/ppermute | solution.py:420
  138.5 8.1 %collective-permute-start.24 = (bf16[64,2048]{1,0:T(8,128)(2,1)S(1)}, bf16[64,2048]{1,0:T(8,128)(2,1)}, u32[]{:S(2)}, u32[]{:S(2)}) collective-permute-start(bf16[64,2048]{1,0:T(8,128)(2,1)S(1)} %collective-permute-done.22.refs_1_), channel_id=1, source_target_pairs={{0,8},{4,12},{8,0},{12,4},{16,24},{20,28},{24,16},{28,20},{1,9},{5... | collective-permute-start | bytes 786440 | tf_op jit(solution)/shard_map/ppermute | solution.py:420
  143.6 13.4 %collective-permute-start.21 = (bf16[256,1024]{1,0:T(8,128)(2,1)}, bf16[256,1024]{1,0:T(8,128)(2,1)S(1)}, u32[]{:S(2)}, u32[]{:S(2)}) collective-permute-start(bf16[256,1024]{1,0:T(8,128)(2,1)} %get-tuple-element.132), channel_id=1, source_target_pairs={{0,8},{4,12},{8,16},{12,20},{16,24},{20,28},{1,9},{5,13},{9,17},{1... | collective-permute-start | bytes 1572872 | tf_op jit(solution)/shard_map/ppermute | solution.py:782
  145.9 18.5 %collective-permute-start.26 = (bf16[64,2048]{1,0:T(8,128)(2,1)S(1)}, bf16[64,2048]{1,0:T(8,128)(2,1)S(1)}, u32[]{:S(2)}, u32[]{:S(2)}) collective-permute-start(bf16[64,2048]{1,0:T(8,128)(2,1)S(1)} %collective-permute-done.22.refs_1_), channel_id=1, source_target_pairs={{0,4},{4,0},{8,12},{12,8},{16,20},{20,16},{24,28},{28,24},{1,5},{5... | collective-permute-start | bytes 786440 | tf_op jit(solution)/shard_map/ppermute | solution.py:400
  146.0 18.4 %collective-permute-start.27 = (bf16[64,2048]{1,0:T(8,128)(2,1)}, bf16[64,2048]{1,0:T(8,128)(2,1)S(1)}, u32[]{:S(2)}, u32[]{:S(2)}) collective-permute-start(bf16[64,2048]{1,0:T(8,128)(2,1)} %collective-permute-done.23.refs_2_), channel_id=1, source_target_pairs={{0,4},{4,0},{8,12},{12,8},{16,20},{20,16},{24,28},{28,24},{1,5},{5... | collective-permute-start | bytes 786440 | tf_op jit(solution)/shard_map/ppermute | solution.py:400
  146.6 17.8 %collective-permute-start.28 = (bf16[64,2048]{1,0:T(8,128)(2,1)}, bf16[64,2048]{1,0:T(8,128)(2,1)S(1)}, u32[]{:S(2)}, u32[]{:S(2)}) collective-permute-start(bf16[64,2048]{1,0:T(8,128)(2,1)} %collective-permute-done.24.refs_3_), channel_id=1, source_target_pairs={{0,4},{4,0},{8,12},{12,8},{16,20},{20,16},{24,28},{28,24},{1,5},{5... | collective-permute-start | bytes 786440 | tf_op jit(solution)/shard_map/ppermute | solution.py:400
  146.6 10.4 %copy-start.51 = (f32[1,1,1024]{2,1,0:T(1,128)S(1)}, f32[1,1,1024]{2,1,0:T(1,128)}, u32[]{:S(2)}) copy-start(f32[1,1,1024]{2,1,0:T(1,128)} %get-tuple-element.139) | copy-start | bytes 12292
  159.3 5.1 %collective-permute-start.25 = (bf16[64,2048]{1,0:T(8,128)(2,1)}, bf16[64,2048]{1,0:T(8,128)(2,1)S(1)}, u32[]{:S(2)}, u32[]{:S(2)}) collective-permute-start(bf16[64,2048]{1,0:T(8,128)(2,1)} %finish.1.refs_0_), channel_id=1, source_target_pairs={{0,4},{4,0},{8,12},{12,8},{16,20},{20,16},{24,28},{28,24},{1,5},{5... | collective-permute-start | bytes 786440 | tf_op jit(solution)/shard_map/ppermute | solution.py:400
  159.3 18.1 %collective-permute-start.30 = (bf16[256,1024]{1,0:T(8,128)(2,1)}, bf16[256,1024]{1,0:T(8,128)(2,1)}, u32[]{:S(2)}, u32[]{:S(2)}) collective-permute-start(bf16[256,1024]{1,0:T(8,128)(2,1)} %fusion.18), channel_id=1, source_target_pairs={{0,8},{4,12},{8,16},{12,20},{16,24},{20,28},{1,9},{5,13},{9,17},{1... | collective-permute-start | bytes 1572872 | tf_op jit(solution)/shard_map/ppermute | solution.py:782
  173.6 17.9 %all-to-all-start = ((f32[4,4,16,1024]{3,2,1,0:T(8,128)}), f32[4,4,16,1024]{3,2,1,0:T(8,128)S(1)}, u32[]{:S(2)}, u32[]{:S(2)}) async-start(f32[4,4,16,1024]{3,2,1,0:T(8,128)} %project.1), calls=%async_computation | async-start | bytes 2097152 | tf_op jit(solution)/shard_map/all_to_all | solution.py:818
  185.7 6.5 %collective-permute-start.31 = (bf16[128,2048]{1,0:T(8,128)(2,1)}, bf16[128,2048]{1,0:T(8,128)(2,1)S(1)}, u32[]{:S(2)}, u32[]{:S(2)}) collective-permute-start(bf16[128,2048]{1,0:T(8,128)(2,1)} %get-tuple-element.121), channel_id=1, source_target_pairs={{0,4},{4,0},{8,12},{12,8},{16,20},{20,16},{24,28},{28,24},{1,5},{5... | collective-permute-start | bytes 1572872 | tf_op jit(solution)/shard_map/ppermute | solution.py:400
  185.8 7.7 %collective-permute-start.29 = (bf16[128,2048]{1,0:T(8,128)(2,1)S(1)}, bf16[128,2048]{1,0:T(8,128)(2,1)S(1)}, u32[]{:S(2)}, u32[]{:S(2)}) collective-permute-start(bf16[128,2048]{1,0:T(8,128)(2,1)S(1)} %copy-done.63), channel_id=1, source_target_pairs={{0,4},{4,0},{8,12},{12,8},{16,20},{20,16},{24,28},{28,24},{1,5},{5... | collective-permute-start | bytes 1572872 | tf_op jit(solution)/shard_map/ppermute | solution.py:400
  (40 other events, 114.7 us)
